TPU v7x, 32 devices: a whole 2x2x4 slice. The times are simulated.
32 devices in a mesh: expert: 8 (over z, y), tensor: 4 (over x, core).
Axes of the slice: x: 2, y: 2, z: 4, core: 2. Of those that a mesh axis runs over, the one named last changes fastest.
Arguments:
- tokens: bfloat16 [16384, 768], P('expert'), may hold values from -6 to 6
- lengths: int32 [8, 8], P('expert'), may hold values from 1 to 512, 2048 in all within a row
- routes: int32 [16384, 2], P(('expert', 'tensor')), may hold values from 0 to 7, all different within a row; in each aligned block of 512 rows (0 to 511, 512 to 1023, ...) at most 256 rows name the same one
- norm1_gain: float32 [768], replicated, may hold values from 0.25 to 1.75
- attn_qkv: bfloat16 [768, 3, 768], P(None, None, 'tensor'), may hold values from -0.21875 to 0.21875
- attn_out: bfloat16 [768, 768], P('tensor'), may hold values from -0.875 to 0.875
- rel_bias: float32 [12, 128], P('tensor'), may hold values from -3 to 3
- norm2_gain: float32 [768], replicated, may hold values from 0.25 to 1.75
- router: bfloat16 [768, 8], replicated, may hold values from -0.15625 to 0.15625
- expert_in: bfloat16 [8, 768, 3072], P('expert', None, 'tensor'), may hold values from -0.21875 to 0.21875
- expert_out: bfloat16 [8, 3072, 768], P('expert', 'tensor'), may hold values from -0.109375 to 0.109375
- out_grad: bfloat16 [16384, 768], P(('expert', 'tensor')), may hold values from -6 to 6
Outputs:
- output: float32 [16384, 768], P(('expert', 'tensor'))
- grad_tokens: float32 [16384, 768], P(('expert', 'tensor'))
- grad_norm1_gain: float32 [768], P('tensor')
- grad_attn_qkv: float32 [768, 3, 768], P(None, None, 'tensor')
- grad_attn_out: float32 [768, 768], P('tensor')
- grad_rel_bias: float32 [12, 128], P('tensor')
- grad_norm2_gain: float32 [768], P('tensor')
- grad_router: float32 [768, 8], P('tensor')
- grad_expert_in: float32 [8, 768, 3072], P('expert', None, 'tensor')
- grad_expert_out: float32 [8, 3072, 768], P('expert', 'tensor')
Inputs may be any that keep to these rules, and one draw needn't show every extreme that they name: Row g gives in order the lengths of the sequences that fill group g; each row sums to 2048 and its longest is exactly 512. `routes`: each token names two different experts. Within each aligned block of 512 tokens no expert is named more than 256 times, and in some block one expert is named exactly 256 times.
All inputs are finite; a program needn't handle non-finite values.
Results may differ from a plain program's by a relative error of at most 0.025.
Values may be sent and summed in bfloat16 or wider, within the bound.
No kernel may reach another device: no remote copies, remote signals or barrier semaphores. Data moves between devices by JAX's collectives and lax.ppermute only.
A program may use at most 320 MiB of HBM per device.

v0:
```python
import jax
import jax.numpy as jnp
from jax import lax
from jax.sharding import PartitionSpec as P

QBLK = 512


EPSILON = 1e-06
BLOCKED = -1e30
PRECISE = lax.Precision.HIGHEST


def rms_norm(values, gain):
    return values * lax.rsqrt(jnp.mean(values * values, axis=-1, keepdims=True) + EPSILON) * gain


def gelu_tanh(values):
    return (
        0.5
        * values
        * (1.0 + jnp.tanh(0.7978845608028654 * (values + 0.044715 * values * values * values)))
    )


def contract_rows(left, right):
    return lax.dot_general(
        left, right, (((0,), (0,)), ((), ())), preferred_element_type=jnp.float32
    )


def contract_cols(left, right):
    return lax.dot_general(
        left, right, (((1,), (1,)), ((), ())), preferred_element_type=jnp.float32
    )


def fold_keys(pieces, block):
    later = pieces[:, block:]
    earlier = pieces[:, :block]
    shifted = jnp.concatenate([earlier[1:], jnp.zeros_like(earlier[:1])], axis=0)
    return (later + shifted).reshape(-1, pieces.shape[2] * pieces.shape[3])


def spread_diag(vector, block):
    head_count, diag_span = vector.shape
    repeated = jnp.tile(vector, (1, block))
    trimmed = repeated[:, block : block + block * (diag_span - 1)].reshape(
        head_count, block, diag_span - 1
    )
    return trimmed[:, :, : 2 * block]


def fold_diag(matrix, block, diag_span):
    head_count = matrix.shape[0]
    padded_mat = jnp.pad(matrix, ((0, 0), (0, 0), (0, diag_span - 1 - 2 * block)))
    flattened = jnp.pad(padded_mat.reshape(head_count, -1), ((0, 0), (block, 0)))
    return jnp.sum(flattened.reshape(head_count, block, diag_span), axis=1)


def local(
    tokens,
    lengths,
    routes,
    norm1_gain,
    attn_qkv,
    attn_out,
    rel_bias,
    norm2_gain,
    router,
    expert_in,
    expert_out,
    out_grad,
):
    n_expert = lax.axis_size("expert")
    n_tensor = lax.axis_size("tensor")
    group_rows, width = tokens.shape
    groups_here, seq_slots = lengths.shape
    group_len = group_rows // groups_here
    own_rows = routes.shape[0]
    inner_width = attn_out.shape[0]
    head_count, bucket_count = rel_bias.shape
    head_dim = inner_width // head_count
    expert_count = router.shape[1]
    local_experts = expert_in.shape[0]
    hidden_here = expert_in.shape[2]
    capacity = max(2, 4 * own_rows // expert_count)
    block = QBLK
    block_count = group_rows // block
    scale = head_dim ** (-0.5)
    own_first = lax.axis_index("tensor") * own_rows
    widened = tokens.astype(jnp.float32)
    normed_one, norm1_pull = jax.vjp(rms_norm, widened, norm1_gain)
    hidden_one = normed_one.astype(jnp.bfloat16)
    projected = jnp.einsum(
        "td,dcf->tcf", hidden_one, attn_qkv, preferred_element_type=jnp.float32
    ).astype(jnp.bfloat16)
    queries = projected[:, 0].reshape(group_rows, head_count, head_dim)
    zero_rows = jnp.zeros((block, head_count, head_dim), jnp.bfloat16)
    keys_pad = jnp.concatenate(
        [zero_rows, projected[:, 1].reshape(group_rows, head_count, head_dim)], axis=0
    )
    values_pad = jnp.concatenate(
        [zero_rows, projected[:, 2].reshape(group_rows, head_count, head_dim)], axis=0
    )
    ends = jnp.cumsum(lengths, axis=1)
    positions = jnp.arange(group_rows, dtype=jnp.int32)
    group_of = positions // group_len
    local_pos = positions - group_of * group_len
    group_hot = (group_of[:, None] == jnp.arange(groups_here, dtype=jnp.int32)[None, :]).astype(
        jnp.int32
    )
    row_ends = jnp.sum(group_hot[:, :, None] * ends[None, :, :], axis=1)
    segment = group_of * seq_slots + jnp.sum(
        (local_pos[:, None] >= row_ends).astype(jnp.int32), axis=1
    )
    segment_pad = jnp.concatenate([jnp.full((block,), -1, jnp.int32), segment], axis=0)
    distance = (
        jnp.arange(block, dtype=jnp.int32)[:, None]
        - jnp.arange(2 * block, dtype=jnp.int32)[None, :]
        + block
    )
    causal = distance >= 0
    diag_span = 3 * block
    offsets = jnp.arange(diag_span, dtype=jnp.int32)
    spot_hot = (
        jnp.clip(2 * block - offsets, 0, bucket_count - 1)[:, None]
        == jnp.arange(bucket_count, dtype=jnp.int32)[None, :]
    ).astype(jnp.float32)
    diag_bias = jnp.dot(rel_bias, spot_hot.T, precision=PRECISE, preferred_element_type=jnp.float32)
    bias_block = spread_diag(diag_bias, block)

    def block_scores(index):
        first_row = index * block
        query_blk = lax.dynamic_slice_in_dim(queries, first_row, block, 0)
        key_blk = lax.dynamic_slice_in_dim(keys_pad, first_row, 2 * block, 0)
        value_blk = lax.dynamic_slice_in_dim(values_pad, first_row, 2 * block, 0)
        seg_query = lax.dynamic_slice_in_dim(segment, first_row, block, 0)
        seg_key = lax.dynamic_slice_in_dim(segment_pad, first_row, 2 * block, 0)
        allowed = causal & (seg_query[:, None] == seg_key[None, :])
        scores = (
            jnp.einsum("ahd,chd->hac", query_blk, key_blk, preferred_element_type=jnp.float32)
            * scale
            + bias_block
        )
        return (query_blk, key_blk, value_blk, allowed, scores)

    def attend(index):
        query_blk, key_blk, value_blk, allowed, scores = block_scores(index)
        masked = jnp.where(allowed[None], scores, BLOCKED)
        peak = jnp.max(masked, axis=-1, keepdims=True)
        raised = jnp.exp(masked - peak)
        total = jnp.sum(raised, axis=-1, keepdims=True)
        weights = (raised / total).astype(jnp.bfloat16)
        mixed = jnp.einsum(
            "hac,chd->ahd", weights, value_blk, preferred_element_type=jnp.float32
        ).astype(jnp.bfloat16)
        return (mixed, (peak + jnp.log(total))[:, :, 0])

    mixed_blocks, log_totals = lax.map(attend, jnp.arange(block_count, dtype=jnp.int32))
    attention = mixed_blocks.reshape(group_rows, inner_width)
    branch = lax.psum_scatter(
        jnp.dot(attention, attn_out, preferred_element_type=jnp.float32).astype(jnp.bfloat16),
        "tensor",
        scatter_dimension=0,
        tiled=True,
    ).astype(jnp.float32)
    resid = lax.dynamic_slice_in_dim(widened, own_first, own_rows, 0) + branch
    normed_two, norm2_pull = jax.vjp(rms_norm, resid, norm2_gain)
    hidden_two = normed_two.astype(jnp.bfloat16)
    logits = jnp.dot(hidden_two, router, preferred_element_type=jnp.float32)
    route_hot = (routes[:, :, None] == jnp.arange(expert_count, dtype=jnp.int32)).astype(jnp.int32)
    route_float = route_hot.astype(jnp.float32)
    chosen_logit = jnp.sum(route_float * logits[:, None, :], axis=-1)
    gate_vals = jax.nn.softmax(chosen_logit, axis=-1)
    counts = jnp.sum(route_hot, axis=1)
    before = jnp.cumsum(counts, axis=0) - counts
    slot_rank = jnp.sum(route_hot * before[:, None, :], axis=-1)
    slot_index = routes * capacity + slot_rank
    slot_ids = jnp.arange(expert_count * capacity, dtype=jnp.int32)
    slot_hot = (slot_index[:, :, None] == slot_ids[None, None, :]).astype(jnp.bfloat16)
    dispatch = slot_hot[:, 0] + slot_hot[:, 1]
    outgoing = (
        contract_rows(dispatch, hidden_two)
        .astype(jnp.bfloat16)
        .reshape(expert_count, capacity, width)
    )
    source_slots = n_expert * local_experts * capacity
    stacked = lax.all_gather(outgoing[None], "tensor", axis=0, tiled=True)
    arrived = lax.all_to_all(stacked, "expert", split_axis=1, concat_axis=1, tiled=True)
    expert_rows = arrived.reshape(n_tensor, n_expert, local_experts, capacity, width)
    pre = jnp.einsum("tnecw,ewf->tnecf", expert_rows, expert_in, preferred_element_type=jnp.float32)
    act_value, gelu_pull = jax.vjp(gelu_tanh, pre)
    act = act_value.astype(jnp.bfloat16)
    act_flat = act.reshape(-1, hidden_here)
    piece = act_flat.reshape(-1, local_experts, capacity, hidden_here)
    summed = lax.psum_scatter(
        jnp.einsum("kecf,efd->kecd", piece, expert_out, preferred_element_type=jnp.float32)
        .reshape(source_slots * lax.axis_size("tensor"), width)
        .astype(jnp.bfloat16),
        "tensor",
        scatter_dimension=0,
        tiled=True,
    )
    result = summed.reshape(n_expert * local_experts, capacity, width)
    came_back = lax.all_to_all(result, "expert", split_axis=0, concat_axis=0, tiled=True)
    picked = jnp.einsum(
        "tks,sd->tkd", slot_hot, came_back.reshape(-1, width), preferred_element_type=jnp.float32
    )
    output = resid + jnp.sum(gate_vals[:, :, None] * picked, axis=1)
    grad_in = out_grad.astype(jnp.float32)
    grad_gates = jnp.sum(grad_in[:, None, :] * picked, axis=-1)
    grad_split = gate_vals[:, 0] * gate_vals[:, 1] * (grad_gates[:, 0] - grad_gates[:, 1])
    grad_chosen = jnp.stack([grad_split, -grad_split], axis=1)
    grad_logits = jnp.sum(route_float * grad_chosen[:, :, None], axis=1).astype(jnp.bfloat16)
    router_part = contract_rows(hidden_two, grad_logits)
    gate_slot = jnp.einsum(
        "tks,tk->s",
        slot_hot.astype(jnp.float32),
        gate_vals,
        precision=PRECISE,
        preferred_element_type=jnp.float32,
    )
    slot_grads = (
        (contract_rows(dispatch, out_grad) * gate_slot[:, None])
        .astype(jnp.bfloat16)
        .reshape(expert_count, capacity, width)
    )
    grad_landed = lax.all_to_all(slot_grads, "expert", split_axis=0, concat_axis=0, tiled=True)
    grad_rows = lax.all_gather(grad_landed[None], "tensor", axis=0, tiled=True).reshape(
        n_tensor, n_expert, local_experts, capacity, width
    )
    grad_act = jnp.einsum(
        "tnecd,efd->tnecf", grad_rows, expert_out, preferred_element_type=jnp.float32
    )
    grad_w_out = jnp.einsum("tnecf,tnecd->efd", act, grad_rows, preferred_element_type=jnp.float32)
    grad_pre = gelu_pull(grad_act)[0].astype(jnp.bfloat16)
    grad_w_in = jnp.einsum(
        "tnecw,tnecf->ewf", expert_rows, grad_pre, preferred_element_type=jnp.float32
    )
    grad_pre_flat = grad_pre.reshape(-1, hidden_here)
    piece = grad_pre_flat.reshape(-1, local_experts, capacity, hidden_here)
    grad_summed = lax.psum_scatter(
        jnp.einsum("kecf,ewf->kecw", piece, expert_in, preferred_element_type=jnp.float32)
        .reshape(source_slots * lax.axis_size("tensor"), width)
        .astype(jnp.bfloat16),
        "tensor",
        scatter_dimension=0,
        tiled=True,
    )
    grad_outgoing = grad_summed.reshape(n_expert * local_experts, capacity, width)
    grad_sent = lax.all_to_all(grad_outgoing, "expert", split_axis=0, concat_axis=0, tiled=True)
    grad_hidden_two = jnp.dot(
        dispatch, grad_sent.reshape(-1, width), preferred_element_type=jnp.float32
    ) + contract_cols(grad_logits, router)
    grad_resid_norm, gain_two_part = norm2_pull(grad_hidden_two)
    grad_resid = grad_in + grad_resid_norm
    grad_branch = lax.all_gather(grad_resid.astype(jnp.bfloat16), "tensor", axis=0, tiled=True)
    grad_attention = contract_cols(grad_branch, attn_out).astype(jnp.bfloat16)
    grad_attn_out = contract_rows(attention, grad_branch)
    grad_mixed = grad_attention.reshape(group_rows, head_count, head_dim)

    def attend_back(bias_acc, packed):
        index, log_block = packed
        query_blk, key_blk, value_blk, allowed, scores = block_scores(index)
        grad_blk = lax.dynamic_slice_in_dim(grad_mixed, index * block, block, 0)
        probs = jnp.where(allowed[None], jnp.exp(scores - log_block[:, :, None]), 0.0)
        grad_probs = jnp.einsum(
            "ahd,chd->hac", grad_blk, value_blk, preferred_element_type=jnp.float32
        )
        row_inner = jnp.sum(probs * grad_probs, axis=-1, keepdims=True)
        grad_scores = (probs * (grad_probs - row_inner)).astype(jnp.bfloat16)
        grad_query = (
            jnp.einsum("hac,chd->ahd", grad_scores, key_blk, preferred_element_type=jnp.float32)
            * scale
        )
        grad_key = (
            jnp.einsum("hac,ahd->chd", grad_scores, query_blk, preferred_element_type=jnp.float32)
            * scale
        )
        grad_value = jnp.einsum(
            "hac,ahd->chd", probs.astype(jnp.bfloat16), grad_blk, preferred_element_type=jnp.float32
        )
        return (bias_acc + grad_scores.astype(jnp.float32), (grad_query, grad_key, grad_value))

    bias_start = jnp.zeros((head_count, block, 2 * block), jnp.float32)
    bias_acc, (grad_query, grad_key, grad_value) = lax.scan(
        attend_back, bias_start, (jnp.arange(block_count, dtype=jnp.int32), log_totals)
    )
    grad_projected = jnp.stack(
        [
            grad_query.reshape(group_rows, inner_width),
            fold_keys(grad_key, block),
            fold_keys(grad_value, block),
        ],
        axis=1,
    ).astype(jnp.bfloat16)
    grad_attn_qkv = jnp.einsum(
        "td,tcf->dcf", hidden_one, grad_projected, preferred_element_type=jnp.float32
    )
    grad_hidden_one = jnp.einsum(
        "tcf,dcf->td", grad_projected, attn_qkv, preferred_element_type=jnp.float32
    )
    bias_part = jnp.dot(
        fold_diag(bias_acc, block, diag_span),
        spot_hot,
        precision=PRECISE,
        preferred_element_type=jnp.float32,
    )
    tokens_part, gain_one_part = norm1_pull(grad_hidden_one)
    tokens_shared, gain_one_share, gain_two_share, router_share = (
        lax.psum_scatter(
            tokens_part.astype(jnp.bfloat16), "tensor", scatter_dimension=0, tiled=True
        ).astype(jnp.float32),
        lax.psum_scatter(
            gain_one_part.astype(jnp.bfloat16), "tensor", scatter_dimension=0, tiled=True
        ).astype(jnp.float32),
        lax.psum_scatter(
            gain_two_part.astype(jnp.bfloat16), "tensor", scatter_dimension=0, tiled=True
        ).astype(jnp.float32),
        lax.psum_scatter(
            router_part.astype(jnp.bfloat16), "tensor", scatter_dimension=0, tiled=True
        ).astype(jnp.float32),
    )
    totals = lax.psum(
        (grad_attn_qkv, grad_attn_out, bias_part, gain_one_share, gain_two_share, router_share),
        "expert",
    )
    grad_tokens = grad_resid + tokens_shared
    return (
        output,
        grad_tokens,
        totals[3],
        totals[0],
        totals[1],
        totals[2],
        totals[4],
        totals[5],
        grad_w_in,
        grad_w_out,
    )


def solution(mesh):
    return jax.shard_map(
        local,
        mesh=mesh,
        in_specs=(
            P("expert", None),
            P("expert", None),
            P(("expert", "tensor"), None),
            P(),
            P(None, None, "tensor"),
            P("tensor", None),
            P("tensor", None),
            P(),
            P(),
            P("expert", None, "tensor"),
            P("expert", "tensor", None),
            P(("expert", "tensor"), None),
        ),
        out_specs=(
            P(("expert", "tensor"), None),
            P(("expert", "tensor"), None),
            P("tensor"),
            P(None, None, "tensor"),
            P("tensor", None),
            P("tensor", None),
            P("tensor"),
            P("tensor", None),
            P("expert", None, "tensor"),
            P("expert", "tensor", None),
        ),
        check_vma=False,
    )
```

profile of v0, /device:TPU:0, one launch (start us, length us, event | category | flops | bytes accessed | tf_op | source)
XLA Modules:
  0.0 1192.9 jit_solution(6999704778568768069)
XLA Ops:
  17.2 20.4 %copy.78 = f32[1,3,512,1536]{3,1,2,0:T(4,128)S(1)} copy(f32[1,3,512,1536]{3,2,1,0:T(8,128)S(1)} %broadcast_bitcast_fusion) | data formatting | bytes 18874368
  43.4 13.2 %reshape.399 = f32[2357760]{0:T(1024)} reshape(f32[3,785920]{1,0:T(4,128)} %slice.75) | data formatting | bytes 18862080
  56.6 15.8 %reshape.361 = f32[3,512,1535]{2,1,0:T(8,128)} reshape(f32[2357760]{0:T(1024)} %reshape.399) | data formatting | bytes 18862080 | tf_op jit(solution)/shard_map/reshape | solution.py:48
  72.4 6.6 slice.76
  79.0 47.0 %while.30 = (s32[]{:T(128)}, bf16[4,512,3,64]{1,3,2,0:T(8,128)(2,1)}, f32[4,3,512]{2,1,0:T(4,128)}, s32[4]{0:T(128)S(1)}, bf16[2560,3,64]{0,2,1:T(8,128)(2,1)}, ...) while((s32[]{:T(128)}, ...), condition=%wide.region_6.7_spmd.clone, body=%wide.region_3.6_spmd.clone.sunk | while | flops 419527168 | bytes 27464948 | solution.py:160
  142.0 31.2 %reduce-scatter.8.cloned.1.call-done = bf16[512,768]{1,0:T(8,128)(2,1)} async-done(((bf16[2048,768]{1,0:T(8,128)(2,1)}), bf16[512,768]{1,0:T(8,128)(2,1)}) %reduce-scatter.8.cloned.1.call-update) | async-done | bytes 786448 | tf_op jit(solution)/shard_map/reduce_scatter | solution.py:162
  195.5 67.0 %all-gather.5.cloned.1.call-done = bf16[4,8,256,768]{3,2,1,0:T(8,128)(2,1)} async-done(((bf16[1,8,256,768]{3,2,1,0:T(8,128)(2,1)}), bf16[4,8,256,768]{3,2,1,0:T(8,128)(2,1)}) %all-gather.5.cloned.1.call-update) | async-done | bytes 12582928 | tf_op jit(solution)/shard_map/all_gather | solution.py:189
  262.5 10.8 copy.59
  279.6 272.7 %all-to-all-done = bf16[4,8,256,768]{3,2,0,1:T(8,128)(2,1)} async-done(((bf16[4,8,256,768]{3,2,0,1:T(8,128)(2,1)}), bf16[4,8,256,768]{3,2,0,1:T(8,128)(2,1)}, u32[]{:S(2)}, u32[]{:S(2)}) %all-to-all-start) | async-done | bytes 12582944 | tf_op jit(solution)/shard_map/all_to_all | solution.py:190
  552.4 24.1 %multiply_convert_fusion.1 = (bf16[4,8,1,256,768]{4,3,1,0,2:T(8,128)(2,1)}, f32[4,8,256,768]{3,2,1,0:T(8,128)}) fusion(bf16[1,768,768]{2,1,0:T(8,128)(2,1)S(1)} %copy-done, bf16[4,8,256,768]{3,2,0,1:T(8,128)(2,1)} %all-to-all-done), kind=kOutput, calls=%fused_computation.67 | convolution fusion | flops 9720299520 | bytes 51511296 | tf_op jit(solution)/shard_map/tnecw,ewf->tnecf/dot_general | solution.py:192
  576.4 17.1 %convolution_convert_fusion.1 = bf16[32,256,768]{2,1,0:T(8,128)(2,1)} fusion(bf16[32,256,768]{2,1,0:T(8,128)(2,1)} %bitcast.268, bf16[1,768,768]{2,1,0:T(8,128)(2,1)S(1)} %copy-done.68), kind=kOutput, calls=%fused_computation.82 | convolution fusion | flops 9669967872 | bytes 26345472 | tf_op jit(solution)/shard_map/kecf,efd->kecd/dot_general | solution.py:198
  593.6 33.3 %fusion.44 = bf16[4,8,1,256,768]{4,3,1,0,2:T(8,128)(2,1)} fusion(f32[4,8,256,768]{3,2,1,0:T(8,128)} %get-tuple-element.301, bf16[4,8,256,768]{3,2,1,0:T(8,128)(2,1)} %bitcast.263, bf16[1,768,768]{2,1,0:T(8,128)(2,1)S(1)} %copy-done.68), kind=kOutput, calls=%fused_computation.55 | convolution fusion | flops 9814671360 | bytes 51511296 | tf_op jit(solution)/shard_map/tnecd,efd->tnecf/dot_general | solution.py:233
  626.9 17.3 %convolution_convert_fusion = bf16[32,256,768]{2,1,0:T(8,128)(2,1)} fusion(bf16[32,256,768]{2,1,0:T(8,128)(2,1)} %bitcast.267, bf16[1,768,768]{2,1,0:T(8,128)(2,1)S(1)} %copy-done), kind=kOutput, calls=%fused_computation.81 | convolution fusion | flops 9669967872 | bytes 26345472 | tf_op jit(solution)/shard_map/kecf,ewf->kecw/dot_general | solution.py:244
  644.2 46.7 %reduce-scatter.10.cloned.1.call-done = bf16[2048,768]{1,0:T(8,128)(2,1)} async-done(((bf16[8192,768]{1,0:T(8,128)(2,1)}), bf16[2048,768]{1,0:T(8,128)(2,1)}) %reduce-scatter.10.cloned.1.call-update) | async-done | bytes 3145744 | tf_op jit(solution)/shard_map/reduce_scatter | solution.py:197
  696.4 96.2 %reduce-scatter.12.cloned.1.call-done = bf16[2048,768]{1,0:T(8,128)(2,1)} async-done(((bf16[8192,768]{1,0:T(8,128)(2,1)}), bf16[2048,768]{1,0:T(8,128)(2,1)}) %reduce-scatter.12.cloned.1.call-update) | async-done | bytes 3145744 | tf_op jit(solution)/shard_map/reduce_scatter | solution.py:243
  798.7 7.2 multiply_reduce_fusion.3
  805.9 63.1 %all-to-all-done.3 = bf16[8,256,768]{2,1,0:T(8,128)(2,1)} async-done(((bf16[8,256,768]{2,1,0:T(8,128)(2,1)}), bf16[8,256,768]{2,1,0:T(8,128)(2,1)}, u32[]{:S(2)}, u32[]{:S(2)}) %all-to-all-start.3) | async-done | bytes 3145760 | tf_op jit(solution)/shard_map/all_to_all | solution.py:252
  879.4 25.6 %all-gather.7.cloned.1.call-done = bf16[2048,768]{1,0:T(8,128)(2,1)} async-done(((bf16[512,768]{1,0:T(8,128)(2,1)}), bf16[2048,768]{1,0:T(8,128)(2,1)}) %all-gather.7.cloned.1.call-update) | async-done | bytes 3145744 | tf_op jit(solution)/shard_map/all_gather | solution.py:258
  908.0 102.3 %while.31 = (s32[]{:T(128)}, f32[3,512,1024]{2,1,0:T(8,128)}, bf16[4,512,3,64]{1,3,2,0:T(8,128)(2,1)}, f32[4,1024,3,64]{1,3,2,0:T(8,128)}, f32[4,1024,3,64]{1,3,...) while((s32[]{:T(128)}, f32[3,512,1024]{2,1,0:T(8,128)}, ...), condition=%wide.region_24.25_spmd.clone, body=%wide.region_22.24_spmd.clone.sunk | while | flops 1029995008 | bytes 159174160 | solution.py:287
  919.0 7.6 select_add_fusion.2
  942.8 9.8 select_add_fusion.2
  968.8 9.8 select_add_fusion.2
  994.8 9.8 select_add_fusion.2
  1021.6 6.6 fusion.62
  1032.8 17.1 %fusion.69 = f32[1,768,768]{2,1,0:T(8,128)} fusion(bf16[4,8,256,768]{3,2,1,0:T(8,128)(2,1)} %bitcast.264, bf16[4,8,1,256,768]{4,3,1,0,2:T(8,128)(2,1)} %get-tuple-element.300), kind=kOutput, calls=%fused_computation.105 | convolution fusion | flops 9663676416 | bytes 27525120 | tf_op jit(solution)/shard_map/tnecf,tnecd->efd/dot_general | solution.py:236
  1055.5 16.6 %fusion.66 = f32[1,768,768]{2,1,0:T(8,128)} fusion(bf16[4,8,256,768]{3,2,0,1:T(8,128)(2,1)} %all-to-all-done, bf16[4,8,1,256,768]{4,3,1,0,2:T(8,128)(2,1)} %fusion.44), kind=kOutput, calls=%fused_computation.104 | convolution fusion | flops 9663676416 | bytes 27525120 | tf_op jit(solution)/shard_map/tnecw,tnecf->ewf/dot_general | solution.py:238
  1073.0 7.7 pad.13
  1080.7 15.2 %reshape.401 = f32[2357760]{0:T(1024)} reshape(f32[3,512,1535]{2,1,0:T(8,128)} %pad.13) | data formatting | bytes 18862080
  1095.9 13.2 %reshape.375 = f32[3,785920]{1,0:T(4,128)} reshape(f32[2357760]{0:T(1024)} %reshape.401) | data formatting | bytes 18862080 | tf_op jit(solution)/shard_map/reshape | solution.py:57
  1109.1 11.1 pad.14
  1126.8 7.2 bitcast_reduce_fusion
  1134.5 37.9 %all-reduce.9 = (f32[192]{0:T(256)}, f32[3,128]{1,0:T(4,128)}, f32[192]{0:T(256)}, f32[192,8]{0,1:T(8,128)}) all-reduce(f32[192]{0:T(256)S(1)} %dynamic-slice_convert_fusion.1, f32[3,128]{1,0:T(4,128)S(1)} %fusion.81, f32[192]{0:T(256)S(1)} %dynamic-slice_convert_fusion, ...), channel_id=1, replica_groups=mesh['expert'=8,'tensor'=4] {'expert'}, use_global_device_ids=true, to_apply=%region_29.30 | all-reduce | flops 2304 | bytes 15360 | tf_op jit(solution)/shard_map/psum | solution.py:325
  (372 shorter events, 233.4 us)
Async XLA Ops:
  7.2 545.2 %copy-start = (bf16[1,768,768]{2,1,0:T(8,128)(2,1)S(1)}, bf16[1,768,768]{2,1,0:T(8,128)(2,1)}, u32[]{:S(2)}) copy-start(bf16[1,768,768]{2,1,0:T(8,128)(2,1)} %param.25) | copy-start | bytes 3538948
  7.2 165.9 %reduce-scatter.8.cloned.1.call-start = ((), (), s32[]{:S(2)}) async-start(), calls=%async_computation.9 | async-start | bytes 3932160 | tf_op jit(solution)/shard_map/reduce_scatter | solution.py:162
  132.3 130.2 %all-gather.5.cloned.1.call-start = ((), (), s32[]{:S(2)}) async-start(), calls=%async_computation.10 | async-start | bytes 15728640 | tf_op jit(solution)/shard_map/all_gather | solution.py:189
  139.1 42.3 %copy-start.61 = (s32[512,2]{0,1:T(2,128)}, s32[512,2]{0,1:T(2,128)S(1)}, u32[]{:S(2)}) copy-start(s32[512,2]{0,1:T(2,128)S(1)} %multiply_add_fusion.3) | copy-start | bytes 12292
  139.1 37.2 %copy-start.43 = (f32[768]{0:T(1024)S(1)}, f32[768]{0:T(1024)}, u32[]{:S(2)}) copy-start(f32[768]{0:T(1024)} %param.23) | copy-start | bytes 9220
  181.3 8.8 copy-start.37
  181.3 8.8 copy-start.51
  190.1 83.2 %all-to-all-start.2 = ((bf16[8,256,768]{2,1,0:T(8,128)(2,1)}), bf16[8,256,768]{2,1,0:T(8,128)(2,1)}, u32[]{:S(2)}, u32[]{:S(2)}) async-start(bf16[8,256,768]{2,1,0:T(8,128)(2,1)} %bitcast.255), calls=%async_computation.4 | async-start | bytes 6291456 | tf_op jit(solution)/shard_map/all_to_all | solution.py:229
  273.3 279.0 %all-to-all-start = ((bf16[4,8,256,768]{3,2,0,1:T(8,128)(2,1)}), bf16[4,8,256,768]{3,2,0,1:T(8,128)(2,1)}, u32[]{:S(2)}, u32[]{:S(2)}) async-start(bf16[4,8,256,768]{3,2,0,1:T(8,128)(2,1)} %copy.59), calls=%async_computation.1 | async-start | bytes 25165824 | tf_op jit(solution)/shard_map/all_to_all | solution.py:190
  278.8 314.8 %all-gather.9.cloned.1.call-start = ((), (), s32[]{:S(2)}) async-start(), calls=%async_computation.15 | async-start | bytes 15728640 | tf_op jit(solution)/shard_map/all_gather | solution.py:230
  279.6 296.9 %copy-start.68 = (bf16[1,768,768]{2,1,0:T(8,128)(2,1)S(1)}, bf16[1,768,768]{2,1,0:T(8,128)(2,1)}, u32[]{:S(2)}) copy-start(bf16[1,768,768]{2,1,0:T(8,128)(2,1)} %param.26) | copy-start | bytes 3538948
  279.6 411.3 %reduce-scatter.10.cloned.1.call-start = ((), (), s32[]{:S(2)}) async-start(), calls=%async_computation.11 | async-start | bytes 15728640 | tf_op jit(solution)/shard_map/reduce_scatter | solution.py:197
  593.5 199.0 %reduce-scatter.12.cloned.1.call-start = ((), (), s32[]{:S(2)}) async-start(), calls=%async_computation.12 | async-start | bytes 15728640 | tf_op jit(solution)/shard_map/reduce_scatter | solution.py:243
  690.9 101.7 %all-to-all-start.1 = ((bf16[8,256,768]{2,1,0:T(8,128)(2,1)}), bf16[8,256,768]{2,1,0:T(8,128)(2,1)}, u32[]{:S(2)}, u32[]{:S(2)}) async-start(bf16[8,256,768]{2,1,0:T(8,128)(2,1)} %bitcast.253), calls=%async_computation.3 | async-start | bytes 6291456 | tf_op jit(solution)/shard_map/all_to_all | solution.py:206
  792.6 76.5 %all-to-all-start.3 = ((bf16[8,256,768]{2,1,0:T(8,128)(2,1)}), bf16[8,256,768]{2,1,0:T(8,128)(2,1)}, u32[]{:S(2)}, u32[]{:S(2)}) async-start(bf16[8,256,768]{2,1,0:T(8,128)(2,1)} %bitcast.252), calls=%async_computation.6 | async-start | bytes 6291456 | tf_op jit(solution)/shard_map/all_to_all | solution.py:252
  798.2 106.7 %all-gather.7.cloned.1.call-start = ((), (), s32[]{:S(2)}) async-start(), calls=%async_computation.13 | async-start | bytes 3932160 | tf_op jit(solution)/shard_map/all_gather | solution.py:258
  876.7 28.2 %copy-start.33 = (bf16[192,768]{1,0:T(8,128)(2,1)S(1)}, bf16[192,768]{1,0:T(8,128)(2,1)}, u32[]{:S(2)}) copy-start(bf16[192,768]{1,0:T(8,128)(2,1)} %param.21) | copy-start | bytes 884740
  878.1 194.0 %reduce-scatter.16.cloned.1.call-start = ((), (), s32[]{:S(2)}) async-start(), calls=%async_computation.16 | async-start | bytes 245760
  879.3 28.7 %copy-start.6 = (bf16[2560,3,64]{0,2,1:T(8,128)(2,1)S(1)}, bf16[2560,3,64]{0,2,1:T(8,128)(2,1)}, u32[]{:S(2)}) copy-start(bf16[2560,3,64]{0,2,1:T(8,128)(2,1)} %copy-done.5) | copy-start | bytes 2949124
  879.3 28.7 %copy-start.14 = (bf16[2048,3,64]{0,2,1:T(8,128)(2,1)S(1)}, bf16[2048,3,64]{0,2,1:T(8,128)(2,1)}, u32[]{:S(2)}) copy-start(bf16[2048,3,64]{0,2,1:T(8,128)(2,1)} %copy-done.13) | copy-start | bytes 2359300
  879.3 293.1 %reduce-scatter.14.cloned.1.call-start = ((), (), s32[]{:S(2)}) async-start(), calls=%async_computation.14 | async-start | bytes 3932160 | tf_op jit(solution)/shard_map/reduce_scatter | solution.py:312
  1030.9 151.5 %all-reduce.14.cloned.1.call-start = ((), (), s32[]{:S(2)}) async-start(), calls=%async_computation.17 | async-start | bytes 4718592 | tf_op jit(solution)/shard_map/psum | solution.py:325
  1032.8 17.2 %copy-start.17 = (bf16[24,8,4,512]{3,1,2,0:T(8,128)(2,1)S(1)}, bf16[24,8,4,512]{3,1,2,0:T(8,128)(2,1)}, u32[]{:S(2)}) copy-start(bf16[24,8,4,512]{3,1,2,0:T(8,128)(2,1)} %copy-done.16) | copy-start | bytes 2359300
  1032.8 17.2 %copy-start.26 = (bf16[2048,768]{1,0:T(8,128)(2,1)S(1)}, bf16[2048,768]{1,0:T(8,128)(2,1)}, u32[]{:S(2)}) copy-start(bf16[2048,768]{1,0:T(8,128)(2,1)} %all-gather.7.cloned.1.call-done) | copy-start | bytes 9437188
  1032.8 18.8 %copy-start.34 = (bf16[2048,3,192]{0,2,1:T(8,128)(2,1)S(1)}, bf16[2048,3,192]{0,2,1:T(8,128)(2,1)}, u32[]{:S(2)}) copy-start(bf16[2048,3,192]{0,2,1:T(8,128)(2,1)} %constant_dynamic-update-slice_fusion) | copy-start | bytes 7077892
  1109.1 11.1 copy-start.63
  1126.7 45.6 %copy-start.9 = (f32[512,768]{1,0:T(8,128)S(1)}, f32[512,768]{1,0:T(8,128)}, u32[]{:S(2)}) copy-start(f32[512,768]{1,0:T(8,128)} %copy-done.7) | copy-start | bytes 4718596
  1126.7 45.6 %copy-start.22 = (bf16[512,768]{1,0:T(8,128)(2,1)S(1)}, bf16[512,768]{1,0:T(8,128)(2,1)}, u32[]{:S(2)}) copy-start(bf16[512,768]{1,0:T(8,128)(2,1)} %param.27) | copy-start | bytes 2359300
  1126.7 45.6 %copy-start.45 = (f32[768]{0:T(1024)S(1)}, f32[768]{0:T(1024)}, u32[]{:S(2)}) copy-start(f32[768]{0:T(1024)} %param.23) | copy-start | bytes 9220
  1126.7 45.6 %copy-start.48 = (f32[512]{0:T(512)S(1)}, f32[512]{0:T(512)}, u32[]{:S(2)}) copy-start(f32[512]{0:T(512)} %copy-done.46) | copy-start | bytes 6148
  1126.7 45.6 %copy-start.60 = (f32[512]{0:T(512)S(1)}, f32[512]{0:T(512)}, u32[]{:S(2)}) copy-start(f32[512]{0:T(512)} %copy-done.59) | copy-start | bytes 6148
  1172.4 13.7 %copy-start.1 = (bf16[1,768,768]{2,1,0:T(8,128)(2,1)S(1)}, bf16[1,768,768]{2,1,0:T(8,128)(2,1)}, u32[]{:S(2)}) copy-start(bf16[1,768,768]{2,1,0:T(8,128)(2,1)} %param.25) | copy-start | bytes 3538948
  (74 other events, 287.6 us)
Sparse Core Ops, SparseCore 0:
  132.4 40.6 reduce-scatter.7
  180.4 82.0 all-gather.4
  281.3 82.5 all-gather.8
  593.7 97.1 reduce-scatter.9
  693.5 99.0 reduce-scatter.11
  878.2 26.6 all-gather.6
  907.5 19.7 reduce-scatter.15
  1031.0 37.8 reduce-scatter.13
  1073.1 109.2 all-reduce.13
where the time goes:
time: 1200 us; the launch traced here: 1190 us
  waiting for transfers between devices  609 us (51%)
  matrix products  249 us (21%)
  local copies, waits for them, and re-layouts  164 us (14%)
  other arithmetic  81.8 us (7%)
  blocking collectives  44.4 us (4%)
  starting transfers between devices  22.6 us (2%)
  between operations  15.7 us (1%)
    all_to_all x1, waiting for transfers between devices, local(): lax.all_to_all(stacked, 'expert', split_axis=1, concat_axis=1, tiled=True)  273 us
    reduce_scatter x1, waiting for transfers between devices, local(): lax.psum_scatter(jnp.einsum('kecf,ewf->kecw', piece, expert_in, preferred...  96.2 us
    all_gather x1, waiting for transfers between devices, local(): stacked = lax.all_gather(outgoing[None], 'tensor', axis=0, tiled=True)  67 us
    all_to_all x1, waiting for transfers between devices, local(): lax.all_to_all(grad_outgoing, 'expert', split_axis=0, concat_axis=0, tile...  63.1 us
    unnamed x142, local copies, waits for them, and re-layouts  63.1 us
    reduce_scatter x1, waiting for transfers between devices, local(): lax.psum_scatter(jnp.einsum('kecf,efd->kecd', piece, expert_out, preferre...  46.7 us
    psum x1, blocking collectives, local(): lax.psum((grad_attn_qkv, grad_attn_out, bias_part, gain_one_share, gain_t...  37.9 us
    add x4, other arithmetic, attend_back(): bias_acc + grad_scores.astype(jnp.float32)  37.1 us
  transfers between devices with their start and end apart: 13, of which 8 were waited for; matrix products, arithmetic and copies ran while one was open for 29% of the time, Pallas kernels for 0%

commit v1 on v0

--- a/solution.py
+++ b/solution.py
@@ -73,7 +73,6 @@
     out_grad,
 ):
     n_expert = lax.axis_size("expert")
-    n_tensor = lax.axis_size("tensor")
     group_rows, width = tokens.shape
     groups_here, seq_slots = lengths.shape
     group_len = group_rows // groups_here
@@ -82,13 +81,34 @@
     head_count, bucket_count = rel_bias.shape
     head_dim = inner_width // head_count
     expert_count = router.shape[1]
-    local_experts = expert_in.shape[0]
-    hidden_here = expert_in.shape[2]
     capacity = max(2, 4 * own_rows // expert_count)
     block = QBLK
     block_count = group_rows // block
     scale = head_dim ** (-0.5)
     own_first = lax.axis_index("tensor") * own_rows
+    def exchange(rows):
+        return lax.all_to_all(
+            rows.reshape(n_expert, -1, rows.shape[-1]), "expert", split_axis=0, concat_axis=0, tiled=True
+        ).reshape(rows.shape)
+
+    route_hot = (routes[:, :, None] == jnp.arange(expert_count, dtype=jnp.int32)).astype(jnp.int32)
+    counts = jnp.sum(route_hot, axis=1)
+    before = jnp.cumsum(counts, axis=0) - counts
+    slot_rank = jnp.sum(route_hot * before[:, None, :], axis=-1)
+    slot_index = routes * capacity + slot_rank
+    slot_ids = jnp.arange(expert_count * capacity, dtype=jnp.int32)
+    slot_hot = (slot_index[:, :, None] == slot_ids[None, None, :]).astype(jnp.bfloat16)
+    dispatch = slot_hot[:, 0] + slot_hot[:, 1]
+    other_ids = jnp.sum(
+        jnp.where(slot_index[:, :, None] == slot_ids[None, None, :], routes[:, ::-1, None] + 1, 0),
+        axis=(0, 1),
+    )
+    other_here = lax.all_to_all(
+        other_ids.reshape(n_expert, -1), "expert", split_axis=0, concat_axis=0, tiled=True
+    ).reshape(-1)
+    grad_rows = exchange(contract_rows(dispatch, out_grad).astype(jnp.bfloat16))
+    weights_in = lax.all_gather(expert_in[0], "tensor")
+    weights_out = lax.all_gather(expert_out[0], "tensor")
     widened = tokens.astype(jnp.float32)
     normed_one, norm1_pull = jax.vjp(rms_norm, widened, norm1_gain)
     hidden_one = normed_one.astype(jnp.bfloat16)
@@ -168,91 +188,49 @@
     resid = lax.dynamic_slice_in_dim(widened, own_first, own_rows, 0) + branch
     normed_two, norm2_pull = jax.vjp(rms_norm, resid, norm2_gain)
     hidden_two = normed_two.astype(jnp.bfloat16)
-    logits = jnp.dot(hidden_two, router, preferred_element_type=jnp.float32)
-    route_hot = (routes[:, :, None] == jnp.arange(expert_count, dtype=jnp.int32)).astype(jnp.int32)
-    route_float = route_hot.astype(jnp.float32)
-    chosen_logit = jnp.sum(route_float * logits[:, None, :], axis=-1)
-    gate_vals = jax.nn.softmax(chosen_logit, axis=-1)
-    counts = jnp.sum(route_hot, axis=1)
-    before = jnp.cumsum(counts, axis=0) - counts
-    slot_rank = jnp.sum(route_hot * before[:, None, :], axis=-1)
-    slot_index = routes * capacity + slot_rank
-    slot_ids = jnp.arange(expert_count * capacity, dtype=jnp.int32)
-    slot_hot = (slot_index[:, :, None] == slot_ids[None, None, :]).astype(jnp.bfloat16)
-    dispatch = slot_hot[:, 0] + slot_hot[:, 1]
-    outgoing = (
-        contract_rows(dispatch, hidden_two)
-        .astype(jnp.bfloat16)
-        .reshape(expert_count, capacity, width)
-    )
-    source_slots = n_expert * local_experts * capacity
-    stacked = lax.all_gather(outgoing[None], "tensor", axis=0, tiled=True)
-    arrived = lax.all_to_all(stacked, "expert", split_axis=1, concat_axis=1, tiled=True)
-    expert_rows = arrived.reshape(n_tensor, n_expert, local_experts, capacity, width)
-    pre = jnp.einsum("tnecw,ewf->tnecf", expert_rows, expert_in, preferred_element_type=jnp.float32)
+    outgoing = contract_rows(dispatch, hidden_two).astype(jnp.bfloat16)
+    expert_rows = exchange(outgoing)
+    pre = jnp.einsum("sd,jdf->jsf", expert_rows, weights_in, preferred_element_type=jnp.float32)
     act_value, gelu_pull = jax.vjp(gelu_tanh, pre)
     act = act_value.astype(jnp.bfloat16)
-    act_flat = act.reshape(-1, hidden_here)
-    piece = act_flat.reshape(-1, local_experts, capacity, hidden_here)
-    summed = lax.psum_scatter(
-        jnp.einsum("kecf,efd->kecd", piece, expert_out, preferred_element_type=jnp.float32)
-        .reshape(source_slots * lax.axis_size("tensor"), width)
-        .astype(jnp.bfloat16),
-        "tensor",
-        scatter_dimension=0,
-        tiled=True,
-    )
-    result = summed.reshape(n_expert * local_experts, capacity, width)
-    came_back = lax.all_to_all(result, "expert", split_axis=0, concat_axis=0, tiled=True)
-    picked = jnp.einsum(
-        "tks,sd->tkd", slot_hot, came_back.reshape(-1, width), preferred_element_type=jnp.float32
-    )
-    output = resid + jnp.sum(gate_vals[:, :, None] * picked, axis=1)
+    slot_logits = jnp.dot(expert_rows, router, preferred_element_type=jnp.float32)
+    own_hot = (jnp.arange(expert_count, dtype=jnp.int32) == lax.axis_index("expert")).astype(
+        jnp.float32
+    )
+    other_hot = (other_here[:, None] == jnp.arange(1, expert_count + 1, dtype=jnp.int32)).astype(
+        jnp.float32
+    )
+    hot_gap = own_hot[None, :] - other_hot
+    logit_gap = jnp.sum(hot_gap * slot_logits, axis=-1, keepdims=True)
+    gate = 1.0 / (1.0 + jnp.exp(-logit_gap))
+    other_gate = 1.0 / (1.0 + jnp.exp(logit_gap))
+    act_grads = jnp.einsum("sd,jfd->jsf", grad_rows, weights_out, preferred_element_type=jnp.float32)
+    gate_grads = jnp.sum(act_value * act_grads, axis=(0, 2))[:, None]
+    grad_logits = (gate * other_gate * gate_grads * hot_gap).astype(jnp.bfloat16)
+    grad_pre = gelu_pull(gate[None] * act_grads)[0].astype(jnp.bfloat16)
+    grad_sent = exchange(
+        (
+            jnp.einsum("jsf,jdf->sd", grad_pre, weights_in, preferred_element_type=jnp.float32)
+            + contract_cols(grad_logits, router)
+        ).astype(jnp.bfloat16)
+    )
+    result = (
+        gate * jnp.einsum("jsf,jfd->sd", act, weights_out, preferred_element_type=jnp.float32)
+    ).astype(jnp.bfloat16)
+    came_back = exchange(result)
+    output = resid + jnp.dot(dispatch, came_back, preferred_element_type=jnp.float32)
+    router_part = contract_rows(expert_rows, grad_logits)
+    gated_rows = (gate * grad_rows.astype(jnp.float32)).astype(jnp.bfloat16)
+    grad_w_out = jnp.einsum("jsf,sd->jfd", act, gated_rows, preferred_element_type=jnp.float32)
+    grad_w_in = jnp.einsum("sd,jsf->jdf", expert_rows, grad_pre, preferred_element_type=jnp.float32)
+    grad_w_out = lax.psum_scatter(
+        grad_w_out.astype(jnp.bfloat16), "tensor", scatter_dimension=0
+    ).astype(jnp.float32)[None]
+    grad_w_in = lax.psum_scatter(
+        grad_w_in.astype(jnp.bfloat16), "tensor", scatter_dimension=0
+    ).astype(jnp.float32)[None]
     grad_in = out_grad.astype(jnp.float32)
-    grad_gates = jnp.sum(grad_in[:, None, :] * picked, axis=-1)
-    grad_split = gate_vals[:, 0] * gate_vals[:, 1] * (grad_gates[:, 0] - grad_gates[:, 1])
-    grad_chosen = jnp.stack([grad_split, -grad_split], axis=1)
-    grad_logits = jnp.sum(route_float * grad_chosen[:, :, None], axis=1).astype(jnp.bfloat16)
-    router_part = contract_rows(hidden_two, grad_logits)
-    gate_slot = jnp.einsum(
-        "tks,tk->s",
-        slot_hot.astype(jnp.float32),
-        gate_vals,
-        precision=PRECISE,
-        preferred_element_type=jnp.float32,
-    )
-    slot_grads = (
-        (contract_rows(dispatch, out_grad) * gate_slot[:, None])
-        .astype(jnp.bfloat16)
-        .reshape(expert_count, capacity, width)
-    )
-    grad_landed = lax.all_to_all(slot_grads, "expert", split_axis=0, concat_axis=0, tiled=True)
-    grad_rows = lax.all_gather(grad_landed[None], "tensor", axis=0, tiled=True).reshape(
-        n_tensor, n_expert, local_experts, capacity, width
-    )
-    grad_act = jnp.einsum(
-        "tnecd,efd->tnecf", grad_rows, expert_out, preferred_element_type=jnp.float32
-    )
-    grad_w_out = jnp.einsum("tnecf,tnecd->efd", act, grad_rows, preferred_element_type=jnp.float32)
-    grad_pre = gelu_pull(grad_act)[0].astype(jnp.bfloat16)
-    grad_w_in = jnp.einsum(
-        "tnecw,tnecf->ewf", expert_rows, grad_pre, preferred_element_type=jnp.float32
-    )
-    grad_pre_flat = grad_pre.reshape(-1, hidden_here)
-    piece = grad_pre_flat.reshape(-1, local_experts, capacity, hidden_here)
-    grad_summed = lax.psum_scatter(
-        jnp.einsum("kecf,ewf->kecw", piece, expert_in, preferred_element_type=jnp.float32)
-        .reshape(source_slots * lax.axis_size("tensor"), width)
-        .astype(jnp.bfloat16),
-        "tensor",
-        scatter_dimension=0,
-        tiled=True,
-    )
-    grad_outgoing = grad_summed.reshape(n_expert * local_experts, capacity, width)
-    grad_sent = lax.all_to_all(grad_outgoing, "expert", split_axis=0, concat_axis=0, tiled=True)
-    grad_hidden_two = jnp.dot(
-        dispatch, grad_sent.reshape(-1, width), preferred_element_type=jnp.float32
-    ) + contract_cols(grad_logits, router)
+    grad_hidden_two = jnp.dot(dispatch, grad_sent, preferred_element_type=jnp.float32)
     grad_resid_norm, gain_two_part = norm2_pull(grad_hidden_two)
     grad_resid = grad_in + grad_resid_norm
     grad_branch = lax.all_gather(grad_resid.astype(jnp.bfloat16), "tensor", axis=0, tiled=True)

time: 1200 us -> 835 us (0.70)
  waiting for transfers between devices: 609 us -> 221 us
  blocking collectives: 44.4 us -> 116 us
  other arithmetic: 81.8 us -> 55.6 us
    reduce_scatter x2, waiting for transfers between devices: 143 us -> 0.01 us  [the longest x1 0.01 us: local(): lax.psum_scatter(grad_w_in.astype(jnp.bfloat16), 'tensor', scatter_dimens...]
    all_to_all x4, waiting for transfers between devices: 336 us -> 197 us  [the longest x3 197 us: exchange(): lax.all_to_all(rows.reshape(n_expert, -1, rows.shape[-1]), 'expert', spli...]
    all_to_all x0 -> x1, blocking collectives: none -> 74.4 us  [exchange(): lax.all_to_all(rows.reshape(n_expert, -1, rows.shape[-1]), 'expert', spli...]
    all_gather x2, waiting for transfers between devices: 67 us -> 0.02 us  [the longest x1 0.02 us: local(): weights_in = lax.all_gather(expert_in[0], 'tensor')]
    add x4, other arithmetic: 37.1 us -> 6.9 us  [attend_back(): bias_acc + grad_scores.astype(jnp.float32)]
    all_gather x1, waiting for transfers between devices: 25.6 us -> 0.02 us  [local(): lax.all_gather(grad_resid.astype(jnp.bfloat16), 'tensor', axis=0, tiled=T...]
    dot_general x10 -> x9, matrix products: 141 us -> 128 us  [the longest x1 37.6 us: local(): jnp.einsum('sd,jfd->jsf', grad_rows, weights_out, preferred_element_type=...]
    unnamed x142 -> x101, local copies, waits for them, and re-layouts: 63.1 us -> 64.7 us
  transfers between devices with their start and end apart: 13 -> 13, of which waited for: 8 -> 4; matrix products, arithmetic and copies ran while one was open for 29% -> 32% of each run, Pallas kernels for 0% -> 0%
where the time goes in v1:
time: 835 us; the launch traced here: 829 us
  matrix products  240 us (29%)
  waiting for transfers between devices  221 us (26%)
  local copies, waits for them, and re-layouts  153 us (18%)
  blocking collectives  116 us (14%)
  other arithmetic  55.6 us (7%)
  starting transfers between devices  22.8 us (3%)
  between operations  15.5 us (2%)
    all_to_all x3, waiting for transfers between devices, exchange(): lax.all_to_all(rows.reshape(n_expert, -1, rows.shape[-1]), 'expert', spli...  197 us
    all_to_all x1, blocking collectives, exchange(): lax.all_to_all(rows.reshape(n_expert, -1, rows.shape[-1]), 'expert', spli...  74.4 us
    unnamed x101, local copies, waits for them, and re-layouts  64.7 us
    dot_general x1, matrix products, local(): jnp.einsum('sd,jfd->jsf', grad_rows, weights_out, preferred_element_type=...  37.6 us
    psum x1, blocking collectives, local(): lax.psum((grad_attn_qkv, grad_attn_out, bias_part, gain_one_share, gain_t...  35.6 us
    dot_general x8, matrix products, block_scores(): jnp.einsum('ahd,chd->hac', query_blk, key_blk, preferred_element_type=jnp...  32.7 us
    reduce_scatter x1, waiting for transfers between devices, local(): lax.psum_scatter(jnp.dot(attention, attn_out, preferred_element_type=jnp....  21.8 us
    dot_general x1, matrix products, local(): jnp.einsum('sd,jdf->jsf', expert_rows, weights_in, preferred_element_type...  17.6 us
  transfers between devices with their start and end apart: 13, of which 4 were waited for; matrix products, arithmetic and copies ran while one was open for 32% of the time, Pallas kernels for 0%

profile of v1, /device:TPU:0, one launch (start us, length us, event | category | flops | bytes accessed | tf_op | source)
XLA Modules:
  0.0 829.4 jit_solution(16072026714052983737)
XLA Ops:
  16.7 20.4 %copy.67 = f32[1,3,512,1536]{3,1,2,0:T(4,128)S(1)} copy(f32[1,3,512,1536]{3,2,1,0:T(8,128)S(1)} %broadcast_bitcast_fusion) | data formatting | bytes 18874368
  37.1 5.8 slice.59
  42.9 13.2 %reshape.365 = f32[2357760]{0:T(1024)} reshape(f32[3,785920]{1,0:T(4,128)} %slice.59) | data formatting | bytes 18862080
  56.1 15.8 %reshape.335 = f32[3,512,1535]{2,1,0:T(8,128)} reshape(f32[2357760]{0:T(1024)} %reshape.365) | data formatting | bytes 18862080 | tf_op jit(solution)/shard_map/reshape | solution.py:48
  71.9 6.6 slice.60
  78.5 44.5 %while.30 = (s32[]{:T(128)}, bf16[4,512,3,64]{1,3,2,0:T(8,128)(2,1)S(1)}, f32[4,3,512]{2,1,0:T(4,128)}, s32[4]{0:T(128)S(1)}, bf16[2560,3,64]{0,2,1:T(8,128)(2,1...) while((s32[]{:T(128)}, ...), condition=%wide.region_6.7_spmd.clone, body=%wide.region_3.6_spmd.clone.sunk | while | flops 419527168 | bytes 27468036 | solution.py:180
  131.7 7.3 all-to-all-start
  139.0 5.2 convert_element_type.147
  146.5 21.8 %reduce-scatter.8.cloned.1.call-done = bf16[512,768]{1,0:T(8,128)(2,1)} async-done(((bf16[2048,768]{1,0:T(8,128)(2,1)}), bf16[512,768]{1,0:T(8,128)(2,1)}) %reduce-scatter.8.cloned.1.call-update) | async-done | bytes 786448 | tf_op jit(solution)/shard_map/reduce_scatter | solution.py:182
  174.2 5.7 all-to-all-start.1
  180.6 5.1 convolution_convert_fusion
  185.8 64.9 %all-to-all-done.1 = bf16[8,256,768]{2,1,0:T(8,128)(2,1)} async-done(((bf16[8,256,768]{2,1,0:T(8,128)(2,1)}), bf16[8,256,768]{2,1,0:T(8,128)(2,1)}, u32[]{:S(2)}, u32[]{:S(2)}) %all-to-all-start.1) | async-done | bytes 3145760 | tf_op jit(solution)/shard_map/all_to_all | solution.py:90
  250.7 4.6 all-to-all-start.3
  258.3 17.6 %fusion.95 = f32[2048,4,768]{0,2,1:T(8,128)} fusion(bf16[2048,768,1]{1,0,2:T(8,128)(2,1)} %bitcast.17, bf16[4,768,768]{2,1,0:T(8,128)(2,1)} %all-gather.4.cloned.1.call-done), kind=kOutput, calls=%fused_computation.171 | convolution fusion | flops 9663676416 | bytes 33030144 | tf_op jit(solution)/shard_map/sd,jdf->jsf/dot_general | solution.py:193
  275.9 49.6 %all-to-all-done.3 = bf16[8,256,768]{2,1,0:T(8,128)(2,1)} async-done(((bf16[8,256,768]{2,1,0:T(8,128)(2,1)}), bf16[8,256,768]{2,1,0:T(8,128)(2,1)}, u32[]{:S(2)}, u32[]{:S(2)}) %all-to-all-start.3) | async-done | bytes 3145760 | tf_op jit(solution)/shard_map/all_to_all | solution.py:90
  325.5 37.6 %fusion.47 = (f32[2048]{0:T(1024)S(1)}, bf16[4,2048,768]{1,2,0:T(8,128)(2,1)}, bf16[4,2048,768]{1,2,0:T(8,128)(2,1)}) fusion(f32[2048,4,768]{0,2,1:T(8,128)} %fusion.95, f32[2048]{0:T(1024)S(1)} %add_divide_fusion, bf16[2048,768,1]{1,0,2:T(8,128)(2,1)} %bitcast.24, bf16[4,768,768]{2,1,0:T(8,128)(2,1)} %all-gather.6.cloned.1.call-done), kind=kOutput, calls=%fused_computation.60 | convolution fusion | flops 9846126592 | bytes 58212352 | tf_op jit(solution)/shard_map/sd,jfd->jsf/dot_general | solution.py:207
  363.1 13.5 %fusion.96 = f32[2048,768,1]{1,0,2:T(8,128)S(1)} fusion(bf16[4,2048,768]{1,2,0:T(8,128)(2,1)} %get-tuple-element.332, bf16[4,768,768]{2,1,0:T(8,128)(2,1)S(1)} %copy-done.46), kind=kOutput, calls=%fused_computation.172 | convolution fusion | flops 9663676416 | bytes 23592960 | tf_op jit(solution)/shard_map/jsf,jdf->sd/dot_general | solution.py:213
  377.8 74.4 %all_to_all.29 = bf16[8,256,768]{2,1,0:T(8,128)(2,1)S(1)} all-to-all(bf16[8,256,768]{2,1,0:T(8,128)(2,1)S(1)} %bitcast.203), channel_id=1, replica_groups=mesh['expert'=8,'tensor'=4] {'expert'}, dimensions={0} | all-to-all | bytes 6291456 | tf_op jit(solution)/shard_map/all_to_all | solution.py:90
  460.6 16.4 %convert_bitcast_fusion = bf16[4,768,768]{1,2,0:T(8,128)(2,1)} fusion(bf16[4,2048,768]{1,2,0:T(8,128)(2,1)} %get-tuple-element.332, bf16[2048,768,1]{1,0,2:T(8,128)(2,1)} %bitcast.17), kind=kOutput, calls=%fused_computation.85 | convolution fusion | flops 9666035712 | bytes 20447232 | tf_op jit(solution)/shard_map/sd,jsf->jdf/dot_general | solution.py:225
  477.2 15.7 %fusion.60 = bf16[4,768,768]{2,1,0:T(8,128)(2,1)} fusion(bf16[4,2048,768]{1,2,0:T(8,128)(2,1)} %get-tuple-element.333, bf16[2048,768]{1,0:T(8,128)(2,1)} %bitcast.23, f32[2048]{0:T(1024)S(1)} %add_divide_fusion), kind=kOutput, calls=%fused_computation.93 | convolution fusion | flops 9670754304 | bytes 20455424 | tf_op jit(solution)/shard_map/jsf,sd->jfd/dot_general | solution.py:224
  496.9 73.3 %while.31 = (s32[]{:T(128)}, f32[3,512,1024]{2,1,0:T(8,128)}, bf16[4,512,3,64]{1,3,2,0:T(8,128)(2,1)}, f32[4,1024,3,64]{1,3,2,0:T(8,128)}, f32[4,1024,3,64]{1,3,...) while((s32[]{:T(128)}, f32[3,512,1024]{2,1,0:T(8,128)}, ...), condition=%wide.region_19.20_spmd.clone, body=%wide.region_17.19_spmd.clone.sunk | while | flops 1029995008 | bytes 152881680 | solution.py:265
  592.4 15.8 %fusion.55 = bf16[2048,768]{1,0:T(8,128)(2,1)} fusion(bf16[4,2048,768]{1,2,0:T(8,128)(2,1)} %get-tuple-element.333, bf16[4,768,768]{2,1,0:T(8,128)(2,1)} %all-gather.6.cloned.1.call-done, f32[2048]{0:T(1024)S(1)} %add_divide_fusion), kind=kOutput, calls=%fused_computation.79 | convolution fusion | flops 9666822144 | bytes 20455424 | tf_op jit(solution)/shard_map/jsf,jfd->sd/dot_general | solution.py:218
  616.6 5.8 fusion.66
  624.5 82.9 %all-to-all-done.2 = bf16[8,256,768]{2,1,0:T(8,128)(2,1)} async-done(((bf16[8,256,768]{2,1,0:T(8,128)(2,1)}), bf16[8,256,768]{2,1,0:T(8,128)(2,1)}, u32[]{:S(2)}, u32[]{:S(2)}) %all-to-all-start.2) | async-done | bytes 3145760 | tf_op jit(solution)/shard_map/all_to_all | solution.py:90
  707.5 5.7 convolution_add_fusion
  718.9 7.7 pad.13
  726.6 15.3 %reshape.367 = f32[2357760]{0:T(1024)} reshape(f32[3,512,1535]{2,1,0:T(8,128)} %pad.13) | data formatting | bytes 18862080
  741.9 13.1 %reshape.348 = f32[3,785920]{1,0:T(4,128)} reshape(f32[2357760]{0:T(1024)} %reshape.367) | data formatting | bytes 18862080 | tf_op jit(solution)/shard_map/reshape | solution.py:57
  755.0 11.0 %pad.14 = f32[3,786432]{1,0:T(4,128)} pad(f32[3,785920]{1,0:T(4,128)} %reshape.348, f32[]{:T(128)} %constant.74.clone.1), padding=0_0x512_0 | pad | bytes 18868228 | tf_op jit(solution)/shard_map/jit(_pad)/pad | solution.py:57
  766.0 6.3 all-reduce.11
  772.4 7.1 bitcast_reduce_fusion
  780.0 35.6 %all-reduce.9 = (f32[192]{0:T(256)}, f32[3,128]{1,0:T(4,128)}, f32[192]{0:T(256)}, f32[192,8]{0,1:T(8,128)}) all-reduce(f32[192]{0:T(256)S(1)} %dynamic-slice_convert_fusion.1, f32[3,128]{1,0:T(4,128)S(1)} %fusion.70, f32[192]{0:T(256)S(1)} %dynamic-slice_convert_fusion, ...), channel_id=1, replica_groups=mesh['expert'=8,'tensor'=4] {'expert'}, use_global_device_ids=true, to_apply=%region_24.25 | all-reduce | flops 2304 | bytes 15360 | tf_op jit(solution)/shard_map/psum | solution.py:303
  (341 shorter events, 200.3 us)
Async XLA Ops:
  7.2 161.1 %reduce-scatter.8.cloned.1.call-start = ((), (), s32[]{:S(2)}) async-start(), calls=%async_computation.10 | async-start | bytes 3932160 | tf_op jit(solution)/shard_map/reduce_scatter | solution.py:182
  7.3 7.6 copy-start.41
  71.9 6.6 copy-start.20
  127.5 130.8 %all-gather.4.cloned.1.call-start = ((), (), s32[]{:S(2)}) async-start(), calls=%async_computation.11 | async-start | bytes 5898240 | tf_op jit(solution)/shard_map/all_gather | solution.py:110
  131.7 42.5 %all-to-all-start = ((s32[8,1,256]{2,1,0:T(1,128)}), s32[8,1,256]{2,1,0:T(1,128)S(1)}, u32[]{:S(2)}, u32[]{:S(2)}) async-start(s32[8,1,256]{2,1,0:T(1,128)} %bitcast.13), calls=%async_computation.1 | async-start | bytes 16384 | tf_op jit(solution)/shard_map/all_to_all | solution.py:106
  146.5 23.9 %copy-start.39 = (f32[768]{0:T(1024)S(1)}, f32[768]{0:T(1024)}, u32[]{:S(2)}) copy-start(f32[768]{0:T(1024)} %param.23) | copy-start | bytes 9220
  170.4 284.4 %copy-start.9 = (f32[512,768]{1,0:T(8,128)}, f32[512,768]{1,0:T(8,128)S(1)}, u32[]{:S(2)}) copy-start(f32[512,768]{1,0:T(8,128)S(1)} %get-tuple-element.326) | copy-start | bytes 4718596
  170.4 284.3 %copy-start.37 = (f32[512]{0:T(512)}, f32[512]{0:T(512)S(1)}, u32[]{:S(2)}) copy-start(f32[512]{0:T(512)S(1)} %fusion.91) | copy-start | bytes 6148
  174.2 6.4 copy-start.16
  174.2 76.5 %all-to-all-start.1 = ((bf16[8,256,768]{2,1,0:T(8,128)(2,1)}), bf16[8,256,768]{2,1,0:T(8,128)(2,1)}, u32[]{:S(2)}, u32[]{:S(2)}) async-start(bf16[8,256,768]{2,1,0:T(8,128)(2,1)} %bitcast.210), calls=%async_computation.2 | async-start | bytes 6291456 | tf_op jit(solution)/shard_map/all_to_all | solution.py:90
  179.9 145.6 %all-gather.6.cloned.1.call-start = ((), (), s32[]{:S(2)}) async-start(), calls=%async_computation.12 | async-start | bytes 5898240 | tf_op jit(solution)/shard_map/all_gather | solution.py:111
  250.7 74.8 %all-to-all-start.3 = ((bf16[8,256,768]{2,1,0:T(8,128)(2,1)}), bf16[8,256,768]{2,1,0:T(8,128)(2,1)}, u32[]{:S(2)}, u32[]{:S(2)}) async-start(bf16[8,256,768]{2,1,0:T(8,128)(2,1)} %bitcast.209), calls=%async_computation.4 | async-start | bytes 6291456 | tf_op jit(solution)/shard_map/all_to_all | solution.py:90
  255.3 237.6 %all-gather.8.cloned.1.call-start = ((), (), s32[]{:S(2)}) async-start(), calls=%async_computation.13 | async-start | bytes 3932160 | tf_op jit(solution)/shard_map/all_gather | solution.py:236
  325.5 37.6 %copy-start.46 = (bf16[4,768,768]{2,1,0:T(8,128)(2,1)S(1)}, bf16[4,768,768]{2,1,0:T(8,128)(2,1)}, u32[]{:S(2)}) copy-start(bf16[4,768,768]{2,1,0:T(8,128)(2,1)} %all-gather.4.cloned.1.call-done) | copy-start | bytes 14155780
  377.8 74.4 %copy-start.19 = (bf16[512,2048]{1,0:T(8,128)(2,1)S(1)}, bf16[512,2048]{1,0:T(8,128)(2,1)}, u32[]{:S(2)}) copy-start(bf16[512,2048]{1,0:T(8,128)(2,1)} %fusion.63) | copy-start | bytes 6291460
  457.2 166.4 %reduce-scatter.16.cloned.1.call-start = ((), (), s32[]{:S(2)}) async-start(), calls=%async_computation.17 | async-start | bytes 245760
  460.6 252.6 %reduce-scatter.12.cloned.1.call-start = ((), (), s32[]{:S(2)}) async-start(), calls=%async_computation.15 | async-start | bytes 5898240 | tf_op jit(solution)/shard_map/reduce_scatter | solution.py:229
  477.1 238.9 %reduce-scatter.14.cloned.1.call-start = ((), (), s32[]{:S(2)}) async-start(), calls=%async_computation.16 | async-start | bytes 5898240 | tf_op jit(solution)/shard_map/reduce_scatter | solution.py:226
  492.9 322.8 %reduce-scatter.10.cloned.1.call-start = ((), (), s32[]{:S(2)}) async-start(), calls=%async_computation.14 | async-start | bytes 3932160 | tf_op jit(solution)/shard_map/reduce_scatter | solution.py:290
  516.6 5.6 copy-start.1
  528.7 5.4 copy-start.22
  564.8 5.4 copy-start.22
  608.3 99.2 %all-to-all-start.2 = ((bf16[8,256,768]{2,1,0:T(8,128)(2,1)}), bf16[8,256,768]{2,1,0:T(8,128)(2,1)}, u32[]{:S(2)}, u32[]{:S(2)}) async-start(bf16[8,256,768]{2,1,0:T(8,128)(2,1)} %bitcast.208), calls=%async_computation.3 | async-start | bytes 6291456 | tf_op jit(solution)/shard_map/all_to_all | solution.py:90
  612.9 206.1 %all-reduce.14.cloned.1.call-start = ((), (), s32[]{:S(2)}) async-start(), calls=%async_computation.18 | async-start | bytes 4718592 | tf_op jit(solution)/shard_map/psum | solution.py:303
  616.6 5.8 copy-start.49
  616.6 90.9 %copy-start.10 = (f32[512,768]{1,0:T(8,128)S(1)}, f32[512,768]{1,0:T(8,128)}, u32[]{:S(2)}) copy-start(f32[512,768]{1,0:T(8,128)} %copy-done.9) | copy-start | bytes 4718596
  755.0 11.0 %copy-start.45 = (bf16[768]{0:T(1024)(128)(2,1)S(1)}, bf16[768]{0:T(1024)(128)(2,1)}, u32[]{:S(2)}) copy-start(bf16[768]{0:T(1024)(128)(2,1)} %get-tuple-element.265) | copy-start | bytes 4612
  772.4 7.1 copy-start.42
  772.4 43.2 %copy-start.17 = (bf16[512,768]{1,0:T(8,128)(2,1)S(1)}, bf16[512,768]{1,0:T(8,128)(2,1)}, u32[]{:S(2)}) copy-start(bf16[512,768]{1,0:T(8,128)(2,1)} %param.27) | copy-start | bytes 2359300
  772.4 43.2 %copy-start.36 = (f32[512]{0:T(512)S(1)}, f32[512]{0:T(512)}, u32[]{:S(2)}) copy-start(f32[512]{0:T(512)} %copy-done.35) | copy-start | bytes 6148
  772.4 43.2 %copy-start.38 = (f32[512]{0:T(512)S(1)}, f32[512]{0:T(512)}, u32[]{:S(2)}) copy-start(f32[512]{0:T(512)} %copy-done.37) | copy-start | bytes 6148
  772.4 43.2 %copy-start.40 = (f32[768]{0:T(1024)S(1)}, f32[768]{0:T(1024)}, u32[]{:S(2)}) copy-start(f32[768]{0:T(1024)} %param.23) | copy-start | bytes 9220
  (57 other events, 185.1 us)
Sparse Core Ops, SparseCore 0:
  127.6 40.6 reduce-scatter.7
  170.0 37.4 all-gather.3
  209.1 37.4 all-gather.5
  457.4 26.6 all-gather.7
  486.5 19.7 reduce-scatter.15
  508.8 47.8 reduce-scatter.11
  559.3 47.8 reduce-scatter.13
  609.8 37.9 reduce-scatter.9
  652.0 126.2 all-reduce.13

commit v2 on v1

v2 whole, which is shorter than its diff:
```python
import functools

import jax
import jax.numpy as jnp
from jax import lax
from jax.experimental import pallas as pl
from jax.experimental.pallas import tpu as pltpu
from jax.sharding import PartitionSpec as P

BLOCK = 512
HALF = 256
EPSILON = 1e-06
BLOCKED = -1e30
VMEM_LIMIT = 48 * 2**20


def mul(left, right, left_dim, right_dim):
    return lax.dot_general(
        left,
        right,
        (((left_dim,), (right_dim,)), ((), ())),
        preferred_element_type=jnp.float32,
    )


def spread_bias(bias_ref, spread_ref, head_count):
    for head in range(head_count):
        line = jnp.broadcast_to(bias_ref[head : head + 1, :], (2 * HALF, 2 * HALF))
        rolled = pltpu.roll(line, 0, 1, stride=1, stride_axis=0)
        spread_ref[head] = rolled[:, :HALF]


def fold_bias(total):
    line = jnp.concatenate([total, jnp.zeros_like(total)], axis=1)
    rows = lax.broadcasted_iota(jnp.int32, line.shape, 0)
    step = 1
    while step < 2 * HALF:
        line = jnp.where((rows & step) != 0, pltpu.roll(line, 2 * HALF - step, 1), line)
        step *= 2
    return jnp.sum(line, axis=0, keepdims=True)


def window_masks(lengths_ref, block_index, half, slots):
    query_pos = (
        lax.broadcasted_iota(jnp.int32, (1, HALF), 1) + block_index * BLOCK + half * HALF
    )
    start = jnp.zeros_like(query_pos)
    end = jnp.int32(0)
    for slot in range(slots):
        end = end + lengths_ref[0, slot]
        start = jnp.where(query_pos >= end, end, start)
    first_key = (block_index - 1) * BLOCK + half * HALF
    far_pos = lax.broadcasted_iota(jnp.int32, (HALF, 1), 0) + first_key
    near_pos = lax.broadcasted_iota(jnp.int32, (2 * HALF, 1), 0) + first_key + HALF
    return far_pos >= start, (near_pos >= start) & (near_pos <= query_pos)


def forward_kernel(
    lengths_ref, tokens_ref, gain_ref, qkv_ref, out_ref, bias_ref,
    branch_ref, proj_ref, mixed_ref, log_ref,
    keys_ref, values_ref, spread_ref,
    *, head_count, head_dim, slots,
):
    block_index = pl.program_id(0)
    inner = head_count * head_dim

    @pl.when(block_index == 0)
    def _():
        keys_ref[:, :BLOCK] = jnp.zeros_like(keys_ref[:, :BLOCK])
        values_ref[:, :BLOCK] = jnp.zeros_like(values_ref[:, :BLOCK])
        spread_bias(bias_ref, spread_ref, head_count)

    @pl.when(block_index > 0)
    def _():
        keys_ref[:, :BLOCK] = keys_ref[:, BLOCK:]
        values_ref[:, :BLOCK] = values_ref[:, BLOCK:]

    widened = tokens_ref[...].astype(jnp.float32)
    inverse = lax.rsqrt(jnp.mean(widened * widened, axis=-1, keepdims=True) + EPSILON)
    hidden = (widened * inverse * gain_ref[...]).astype(jnp.bfloat16)
    projected = mul(qkv_ref[...], hidden, 1, 1)
    proj_ref[...] = projected.astype(jnp.bfloat16)
    for head in range(head_count):
        low = inner + head * head_dim
        keys_ref[head, BLOCK:, :] = projected[low : low + head_dim].T.astype(jnp.bfloat16)
    values_ref[:, BLOCK:] = proj_ref[2 * inner :, :]
    scale = head_dim**-0.5
    for half in range(BLOCK // HALF):
        far_mask, near_mask = window_masks(lengths_ref, block_index, half, slots)
        cols = slice(half * HALF, (half + 1) * HALF)
        window = slice(half * HALF, (half + 3) * HALF)
        for head in range(head_count):
            rows = slice(head * head_dim, (head + 1) * head_dim)
            query = proj_ref[rows, cols] * jnp.bfloat16(scale)
            scores = mul(keys_ref[head, window, :], query, 1, 0)
            far = jnp.where(far_mask, scores[:HALF], BLOCKED)
            near = jnp.where(near_mask, scores[HALF:] + spread_ref[head], BLOCKED)
            peak = jnp.maximum(
                jnp.max(far, axis=0, keepdims=True), jnp.max(near, axis=0, keepdims=True)
            )
            far = jnp.exp(far - peak)
            near = jnp.exp(near - peak)
            total = jnp.sum(far, axis=0, keepdims=True) + jnp.sum(near, axis=0, keepdims=True)
            share = 1.0 / total
            weights = jnp.concatenate(
                [(far * share).astype(jnp.bfloat16), (near * share).astype(jnp.bfloat16)], axis=0
            )
            mixed_ref[rows, cols] = mul(values_ref[rows, window], weights, 1, 0).astype(
                jnp.bfloat16
            )
            log_ref[head : head + 1, cols] = peak + jnp.log(total)
    branch_ref[...] = mul(mixed_ref[...], out_ref[...], 0, 0).astype(jnp.bfloat16)


def backward_kernel(
    lengths_ref, tokens_ref, gain_ref, qkv_ref, out_ref, bias_ref,
    proj_ref, before_ref, mixed_ref, log_ref, grad_ref,
    part_ref, qkv_grad_ref, out_grad_ref, gain_grad_ref, bias_grad_ref, far_grad_ref,
    spread_ref, near_ref, far_ref, carry_ref, pieces_ref,
    *, head_count, head_dim, slots, block_count,
):
    step = pl.program_id(0)
    block_index = block_count - 1 - step
    inner = head_count * head_dim

    @pl.when(step == 0)
    def _():
        spread_bias(bias_ref, spread_ref, head_count)
        near_ref[...] = jnp.zeros_like(near_ref)
        far_ref[...] = jnp.zeros_like(far_ref)
        carry_ref[...] = jnp.zeros_like(carry_ref)
        qkv_grad_ref[...] = jnp.zeros_like(qkv_grad_ref)
        out_grad_ref[...] = jnp.zeros_like(out_grad_ref)
        gain_grad_ref[...] = jnp.zeros_like(gain_grad_ref)
        bias_grad_ref[...] = jnp.zeros_like(bias_grad_ref)

    @pl.when(step > 0)
    def _():
        carry_ref[:, BLOCK:] = carry_ref[:, :BLOCK]
        carry_ref[:, :BLOCK] = jnp.zeros_like(carry_ref[:, :BLOCK])

    grad_branch = grad_ref[...]
    out_grad_ref[...] += mul(mixed_ref[...], grad_branch, 1, 0)
    grad_mixed = mul(out_ref[...], grad_branch, 1, 1).astype(jnp.bfloat16)
    scale = head_dim**-0.5
    for head in range(head_count):
        rows = slice(head * head_dim, (head + 1) * head_dim)
        key_rows = slice(inner + head * head_dim, inner + (head + 1) * head_dim)
        value_rows = slice(2 * inner + head * head_dim, 2 * inner + (head + 1) * head_dim)
        keys_flat = jnp.concatenate([before_ref[key_rows, :], proj_ref[key_rows, :]], axis=1)
        values_flat = jnp.concatenate([before_ref[value_rows, :], proj_ref[value_rows, :]], axis=1)
        keys = keys_flat.astype(jnp.float32).T.astype(jnp.bfloat16)
        values = values_flat.astype(jnp.float32).T.astype(jnp.bfloat16)
        for half in range(BLOCK // HALF):
            far_mask, near_mask = window_masks(lengths_ref, block_index, half, slots)
            cols = slice(half * HALF, (half + 1) * HALF)
            window = slice(half * HALF, (half + 3) * HALF)
            query = proj_ref[rows, cols] * jnp.bfloat16(scale)
            scores = mul(keys[window], query, 1, 0)
            log_total = log_ref[head : head + 1, cols]
            far = jnp.where(far_mask, jnp.exp(scores[:HALF] - log_total), 0.0)
            near = jnp.where(
                near_mask, jnp.exp(scores[HALF:] + spread_ref[head] - log_total), 0.0
            )
            probs = jnp.concatenate([far, near], axis=0)
            grad_out = grad_mixed[rows, cols]
            grad_probs = mul(values[window], grad_out, 1, 0)
            row_inner = jnp.sum(probs * grad_probs, axis=0, keepdims=True)
            grad_scores = (probs * (grad_probs - row_inner)).astype(jnp.bfloat16)
            rounded = grad_scores.astype(jnp.float32)
            near_ref[head] += rounded[HALF:]
            far_ref[head : head + 1] += jnp.sum(rounded[:HALF], axis=0, keepdims=True)
            pieces_ref[rows, cols] = (
                mul(keys_flat[:, window], grad_scores, 1, 0) * scale
            ).astype(jnp.bfloat16)
            carry_ref[rows, window] += mul(query, grad_scores, 1, 1)
            carry_ref[key_rows, window] += mul(grad_out, probs.astype(jnp.bfloat16), 1, 1)
    pieces_ref[inner:, :] = carry_ref[:, BLOCK:].astype(jnp.bfloat16)
    widened = tokens_ref[...].astype(jnp.float32)
    inverse = lax.rsqrt(jnp.mean(widened * widened, axis=-1, keepdims=True) + EPSILON)
    normed = widened * inverse
    hidden = (normed * gain_ref[...]).astype(jnp.bfloat16)
    pieces = pieces_ref[...]
    qkv_grad_ref[...] += mul(pieces, hidden, 1, 0)
    grad_hidden = mul(pieces, qkv_ref[...], 0, 0)
    gain_grad_ref[...] += jnp.sum(
        (grad_hidden * normed).reshape(BLOCK // 8, 8, normed.shape[1]), axis=0
    )
    gained = grad_hidden * gain_ref[...]
    part_ref[...] = (
        inverse * (gained - normed * jnp.mean(gained * normed, axis=-1, keepdims=True))
    ).astype(jnp.bfloat16)

    @pl.when(step == block_count - 1)
    def _():
        for head in range(head_count):
            bias_grad_ref[head : head + 1, :] = fold_bias(near_ref[head])
        far_grad_ref[...] = far_ref[...]


def whole(shape):
    return pl.BlockSpec(shape, lambda step: (0,) * len(shape))


def bias_line(rel_bias):
    head_count, bucket_count = rel_bias.shape
    line = rel_bias - rel_bias[:, bucket_count - 1 :]
    line = jnp.concatenate(
        [
            jnp.zeros((head_count, HALF), jnp.float32),
            line,
            jnp.zeros((head_count, HALF - bucket_count), jnp.float32),
        ],
        axis=1,
    )
    return jnp.concatenate([line, jnp.zeros((8 - head_count, 2 * HALF), jnp.float32)], axis=0)


def attend(tokens, lengths, gain, qkv_flat, attn_out, rel_bias):
    rows, width = tokens.shape
    inner = attn_out.shape[0]
    head_count = rel_bias.shape[0]
    head_dim = inner // head_count
    block_count = rows // BLOCK
    return pl.pallas_call(
        functools.partial(
            forward_kernel, head_count=head_count, head_dim=head_dim, slots=lengths.shape[1]
        ),
        grid=(block_count,),
        in_specs=[
            pl.BlockSpec(memory_space=pltpu.SMEM),
            pl.BlockSpec((BLOCK, width), lambda step: (step, 0)),
            whole((1, width)),
            whole(qkv_flat.shape),
            whole(attn_out.shape),
            whole((8, 2 * HALF)),
        ],
        out_specs=[
            pl.BlockSpec((BLOCK, width), lambda step: (step, 0)),
            pl.BlockSpec((3 * inner, BLOCK), lambda step: (0, step)),
            pl.BlockSpec((inner, BLOCK), lambda step: (0, step)),
            pl.BlockSpec((8, BLOCK), lambda step: (0, step)),
        ],
        out_shape=[
            jax.ShapeDtypeStruct((rows, width), jnp.bfloat16),
            jax.ShapeDtypeStruct((3 * inner, rows), jnp.bfloat16),
            jax.ShapeDtypeStruct((inner, rows), jnp.bfloat16),
            jax.ShapeDtypeStruct((8, rows), jnp.float32),
        ],
        scratch_shapes=[
            pltpu.VMEM((head_count, 2 * BLOCK, head_dim), jnp.bfloat16),
            pltpu.VMEM((inner, 2 * BLOCK), jnp.bfloat16),
            pltpu.VMEM((head_count, 2 * HALF, HALF), jnp.float32),
        ],
        compiler_params=pltpu.CompilerParams(vmem_limit_bytes=VMEM_LIMIT),
        cost_estimate=pl.CostEstimate(
            flops=2 * rows * width * inner * 4 + 4 * rows * 768 * inner,
            bytes_accessed=10 * rows * width,
            transcendentals=rows * 768 * head_count,
        ),
        name="attend_forward",
    )(lengths, tokens, gain[None, :], qkv_flat, attn_out, bias_line(rel_bias))


def attend_back(
    tokens, lengths, gain, qkv_flat, attn_out, rel_bias, projected, mixed, log_total, grad_branch
):
    rows, width = tokens.shape
    inner = attn_out.shape[0]
    head_count, bucket_count = rel_bias.shape
    head_dim = inner // head_count
    block_count = rows // BLOCK
    last = block_count - 1
    part, qkv_grad, out_grad, gain_grad, bias_grad, far_grad = pl.pallas_call(
        functools.partial(
            backward_kernel,
            head_count=head_count,
            head_dim=head_dim,
            slots=lengths.shape[1],
            block_count=block_count,
        ),
        grid=(block_count,),
        in_specs=[
            pl.BlockSpec(memory_space=pltpu.SMEM),
            pl.BlockSpec((BLOCK, width), lambda step: (last - step, 0)),
            whole((1, width)),
            whole(qkv_flat.shape),
            whole(attn_out.shape),
            whole((8, 2 * HALF)),
            pl.BlockSpec((3 * inner, BLOCK), lambda step: (0, last - step)),
            pl.BlockSpec((3 * inner, BLOCK), lambda step: (0, jnp.maximum(last - step - 1, 0))),
            pl.BlockSpec((inner, BLOCK), lambda step: (0, last - step)),
            pl.BlockSpec((8, BLOCK), lambda step: (0, last - step)),
            pl.BlockSpec((BLOCK, width), lambda step: (last - step, 0)),
        ],
        out_specs=[
            pl.BlockSpec((BLOCK, width), lambda step: (last - step, 0)),
            whole((3 * inner, width)),
            whole((inner, width)),
            whole((8, width)),
            whole((8, 2 * HALF)),
            whole((8, HALF)),
        ],
        out_shape=[
            jax.ShapeDtypeStruct((rows, width), jnp.bfloat16),
            jax.ShapeDtypeStruct((3 * inner, width), jnp.float32),
            jax.ShapeDtypeStruct((inner, width), jnp.float32),
            jax.ShapeDtypeStruct((8, width), jnp.float32),
            jax.ShapeDtypeStruct((8, 2 * HALF), jnp.float32),
            jax.ShapeDtypeStruct((8, HALF), jnp.float32),
        ],
        scratch_shapes=[
            pltpu.VMEM((head_count, 2 * HALF, HALF), jnp.float32),
            pltpu.VMEM((head_count, 2 * HALF, HALF), jnp.float32),
            pltpu.VMEM((8, HALF), jnp.float32),
            pltpu.VMEM((2 * inner, 2 * BLOCK), jnp.float32),
            pltpu.VMEM((3 * inner, BLOCK), jnp.bfloat16),
        ],
        compiler_params=pltpu.CompilerParams(vmem_limit_bytes=VMEM_LIMIT),
        cost_estimate=pl.CostEstimate(
            flops=2 * rows * width * inner * 8 + 10 * rows * 768 * inner,
            bytes_accessed=14 * rows * width,
            transcendentals=rows * 768 * head_count,
        ),
        name="attend_backward",
    )(
        lengths, tokens, gain[None, :], qkv_flat, attn_out, bias_line(rel_bias),
        projected, projected, mixed, log_total, grad_branch,
    )
    near_grad = bias_grad[:head_count, HALF : HALF + bucket_count - 1]
    rest = jnp.sum(bias_grad[:head_count], axis=1) - jnp.sum(near_grad, axis=1)
    rest = rest + jnp.sum(far_grad[:head_count], axis=1)
    bias_part = jnp.concatenate([near_grad, rest[:, None]], axis=1)
    return part, qkv_grad, out_grad, jnp.sum(gain_grad, axis=0), bias_part


def rms_norm(values, gain):
    return values * lax.rsqrt(jnp.mean(values * values, axis=-1, keepdims=True) + EPSILON) * gain


def gelu_tanh(values):
    return (
        0.5
        * values
        * (1.0 + jnp.tanh(0.7978845608028654 * (values + 0.044715 * values * values * values)))
    )


def exchange(rows):
    parts = lax.axis_size("expert")
    return lax.all_to_all(
        rows.reshape((parts, -1) + rows.shape[1:]), "expert", split_axis=0, concat_axis=0, tiled=True
    ).reshape(rows.shape)


def local(
    tokens,
    lengths,
    routes,
    norm1_gain,
    attn_qkv,
    attn_out,
    rel_bias,
    norm2_gain,
    router,
    expert_in,
    expert_out,
    out_grad,
):
    n_tensor = lax.axis_size("tensor")
    tensor_index = lax.axis_index("tensor")
    width = tokens.shape[1]
    own_rows = routes.shape[0]
    inner = attn_out.shape[0]
    head_count, bucket_count = rel_bias.shape
    expert_count = router.shape[1]
    capacity = max(2, 4 * own_rows // expert_count)

    route_hot = (routes[:, :, None] == jnp.arange(expert_count, dtype=jnp.int32)).astype(jnp.int32)
    counts = jnp.sum(route_hot, axis=1)
    before = jnp.cumsum(counts, axis=0) - counts
    slot_rank = jnp.sum(route_hot * before[:, None, :], axis=-1)
    slot_index = routes * capacity + slot_rank
    slot_ids = jnp.arange(expert_count * capacity, dtype=jnp.int32)
    slot_match = slot_index[:, :, None] == slot_ids[None, None, :]
    dispatch = (slot_match[:, 0] | slot_match[:, 1]).astype(jnp.bfloat16)
    other_ids = jnp.sum(jnp.where(slot_match, routes[:, ::-1, None] + 1, 0), axis=(0, 1))
    other_here = exchange(other_ids)
    grad_rows = exchange(mul(dispatch, out_grad, 0, 0).astype(jnp.bfloat16))

    qkv_flat = attn_qkv.transpose(1, 2, 0).reshape(3 * inner, width)
    branch, projected, mixed, log_total = attend(
        tokens, lengths, norm1_gain, qkv_flat, attn_out, rel_bias
    )
    branch = lax.psum_scatter(branch, "tensor", scatter_dimension=0, tiled=True)
    branch, grad_rows, other_here = lax.optimization_barrier((branch, grad_rows, other_here))
    own_tokens = lax.dynamic_slice_in_dim(tokens, tensor_index * own_rows, own_rows, 0)
    resid = own_tokens.astype(jnp.float32) + branch.astype(jnp.float32)
    normed_two, norm2_pull = jax.vjp(rms_norm, resid, norm2_gain)
    hidden_two = normed_two.astype(jnp.bfloat16)
    expert_rows = exchange(mul(dispatch, hidden_two, 0, 0).astype(jnp.bfloat16))
    weights_in = lax.all_gather(expert_in[0], "tensor")
    weights_out = lax.all_gather(expert_out[0], "tensor")

    pre = jnp.einsum("sd,jdf->jsf", expert_rows, weights_in, preferred_element_type=jnp.float32)
    act_value, gelu_pull = jax.vjp(gelu_tanh, pre)
    act = act_value.astype(jnp.bfloat16)
    slot_logits = jnp.dot(expert_rows, router, preferred_element_type=jnp.float32)
    own_hot = (jnp.arange(expert_count, dtype=jnp.int32) == lax.axis_index("expert")).astype(
        jnp.float32
    )
    other_hot = (other_here[:, None] == jnp.arange(1, expert_count + 1, dtype=jnp.int32)).astype(
        jnp.float32
    )
    hot_gap = own_hot[None, :] - other_hot
    logit_gap = jnp.sum(hot_gap * slot_logits, axis=-1, keepdims=True)
    gate = 1.0 / (1.0 + jnp.exp(-logit_gap))
    other_gate = 1.0 / (1.0 + jnp.exp(logit_gap))
    act_grads = jnp.einsum("sd,jfd->jsf", grad_rows, weights_out, preferred_element_type=jnp.float32)
    gate_grads = jnp.sum(act_value * act_grads, axis=(0, 2))[:, None]
    grad_logits = (gate * other_gate * gate_grads * hot_gap).astype(jnp.bfloat16)
    grad_pre = gelu_pull(gate[None] * act_grads)[0].astype(jnp.bfloat16)
    grad_sent = exchange(
        (
            jnp.einsum("jsf,jdf->sd", grad_pre, weights_in, preferred_element_type=jnp.float32)
            + mul(grad_logits, router, 1, 1)
        ).astype(jnp.bfloat16)
    )
    result = (
        gate * jnp.einsum("jsf,jfd->sd", act, weights_out, preferred_element_type=jnp.float32)
    ).astype(jnp.bfloat16)
    router_part = mul(expert_rows, grad_logits, 0, 0)
    gated_rows = (gate * grad_rows.astype(jnp.float32)).astype(jnp.bfloat16)
    grad_w_out = jnp.einsum(
        "jsf,sd->jfd", act, gated_rows, preferred_element_type=jnp.float32
    ).astype(jnp.bfloat16)
    grad_w_in = jnp.einsum(
        "sd,jsf->jdf", expert_rows, grad_pre, preferred_element_type=jnp.float32
    ).astype(jnp.bfloat16)
    grad_sent, result, grad_w_in, grad_w_out = lax.optimization_barrier(
        (grad_sent, result, grad_w_in, grad_w_out)
    )
    came_back = exchange(result)
    grad_in = out_grad.astype(jnp.float32)
    grad_hidden_two = jnp.dot(dispatch, grad_sent, preferred_element_type=jnp.float32)
    grad_resid_norm, gain_two_part = norm2_pull(grad_hidden_two)
    grad_resid = grad_in + grad_resid_norm
    grad_branch = lax.all_gather(grad_resid.astype(jnp.bfloat16), "tensor", axis=0, tiled=True)
    grad_w_out = lax.psum_scatter(grad_w_out, "tensor", scatter_dimension=0)
    grad_w_in = lax.psum_scatter(grad_w_in, "tensor", scatter_dimension=0)

    tokens_part, qkv_part, out_part, gain_one_part, bias_part = attend_back(
        tokens, lengths, norm1_gain, qkv_flat, attn_out, rel_bias,
        projected, mixed, log_total, grad_branch,
    )
    tokens_part, came_back = lax.optimization_barrier((tokens_part, came_back))
    output = resid + jnp.dot(dispatch, came_back, preferred_element_type=jnp.float32)
    tokens_shared = lax.psum_scatter(tokens_part, "tensor", scatter_dimension=0, tiled=True)
    grad_tokens = grad_resid + tokens_shared.astype(jnp.float32)
    weights_part = jnp.concatenate([qkv_part, out_part], axis=0).astype(jnp.bfloat16)
    weights_total = lax.psum(weights_part, "expert").astype(jnp.float32)
    bias_slots = lax.dynamic_update_slice_in_dim(
        jnp.zeros((n_tensor * head_count, bucket_count), jnp.float32),
        bias_part,
        tensor_index * head_count,
        0,
    )
    small = jnp.concatenate(
        [gain_one_part, gain_two_part, router_part.T.reshape(-1), bias_slots.reshape(-1)]
    )
    small = lax.psum(small, ("expert", "tensor"))
    count = 2 + expert_count
    columns = lax.dynamic_slice_in_dim(
        small[: count * width].reshape(count, width),
        tensor_index * (width // n_tensor),
        width // n_tensor,
        1,
    )
    bias_total = lax.dynamic_slice_in_dim(
        small[count * width :].reshape(n_tensor * head_count, bucket_count),
        tensor_index * head_count,
        head_count,
        0,
    )
    return (
        output,
        grad_tokens,
        columns[0],
        weights_total[: 3 * inner].reshape(3, inner, width).transpose(2, 0, 1),
        weights_total[3 * inner :],
        bias_total,
        columns[1],
        columns[2:].T,
        grad_w_in.astype(jnp.float32)[None],
        grad_w_out.astype(jnp.float32)[None],
    )


def solution(mesh):
    return jax.shard_map(
        local,
        mesh=mesh,
        in_specs=(
            P("expert", None),
            P("expert", None),
            P(("expert", "tensor"), None),
            P(),
            P(None, None, "tensor"),
            P("tensor", None),
            P("tensor", None),
            P(),
            P(),
            P("expert", None, "tensor"),
            P("expert", "tensor", None),
            P(("expert", "tensor"), None),
        ),
        out_specs=(
            P(("expert", "tensor"), None),
            P(("expert", "tensor"), None),
            P("tensor"),
            P(None, None, "tensor"),
            P("tensor", None),
            P("tensor", None),
            P("tensor"),
            P("tensor", None),
            P("expert", None, "tensor"),
            P("expert", "tensor", None),
        ),
        check_vma=False,
    )
```

time: 835 us -> 703 us (0.84)
  local copies, waits for them, and re-layouts: 153 us -> 16.3 us
  matrix products: 240 us -> 142 us
  Pallas kernels: 0 us -> 58.5 us
  waiting for transfers between devices: 221 us -> 277 us
  other arithmetic: 55.6 us -> 18.7 us
  blocking collectives: 116 us -> 144 us
    dot_general x38 -> x4, matrix products: 104 us -> 13.8 us  [mul(): lax.dot_general(left, right, (((left_dim,), (right_dim,)), ((), ())), pre...]
    reduce_scatter x4, waiting for transfers between devices: 21.8 us -> 84.4 us  [the longest x1 46.8 us: local(): grad_w_out = lax.psum_scatter(grad_w_out, 'tensor', scatter_dimension=0)]
    pallas_call x0 -> x2, Pallas kernels: none -> 58.5 us  [the longest x1 35.6 us: attend_back(): pl.pallas_call(functools.partial(backward_kernel, head_count=head_count,...]
    unnamed x101 -> x61, local copies, waits for them, and re-layouts: 64.7 us -> 8.88 us
    all_to_all x4, waiting for transfers between devices: 197 us -> 163 us  [exchange(): lax.all_to_all(rows.reshape((parts, -1) + rows.shape[1:]), 'expert', spli...]
    all_to_all x1, blocking collectives: 74.4 us -> 105 us  [exchange(): lax.all_to_all(rows.reshape((parts, -1) + rows.shape[1:]), 'expert', spli...]
    reshape x2 -> x1, local copies, waits for them, and re-layouts: 28.9 us -> 0.01 us  [local(): router_part.T.reshape(-1)]
    all_gather x1, waiting for transfers between devices: 0.02 us -> 27.7 us  [local(): lax.all_gather(grad_resid.astype(jnp.bfloat16), 'tensor', axis=0, tiled=T...]
  transfers between devices with their start and end apart: 13 -> 12, of which waited for: 4 -> 6; matrix products, arithmetic and copies ran while one was open for 32% -> 15% of each run, Pallas kernels for 0% -> 0%
where the time goes in v2:
time: 703 us; the launch traced here: 695 us
  waiting for transfers between devices  277 us (39%)
  blocking collectives  144 us (20%)
  matrix products  142 us (20%)
  Pallas kernels  58.5 us (8%)
  starting transfers between devices  22.9 us (3%)
  other arithmetic  18.7 us (3%)
  local copies, waits for them, and re-layouts  16.3 us (2%)
  between operations  15.1 us (2%)
    all_to_all x4, waiting for transfers between devices, exchange(): lax.all_to_all(rows.reshape((parts, -1) + rows.shape[1:]), 'expert', spli...  163 us
    all_to_all x1, blocking collectives, exchange(): lax.all_to_all(rows.reshape((parts, -1) + rows.shape[1:]), 'expert', spli...  105 us
    reduce_scatter x1, waiting for transfers between devices, local(): grad_w_out = lax.psum_scatter(grad_w_out, 'tensor', scatter_dimension=0)  46.8 us
    psum x1, blocking collectives, local(): small = lax.psum(small, ('expert', 'tensor'))  38.7 us
    dot_general x1, matrix products, local(): jnp.einsum('sd,jfd->jsf', grad_rows, weights_out, preferred_element_type=...  37.8 us
    reduce_scatter x1, waiting for transfers between devices, local(): lax.psum_scatter(tokens_part, 'tensor', scatter_dimension=0, tiled=True)  37.7 us
    pallas_call x1, Pallas kernels, attend_back(): pl.pallas_call(functools.partial(backward_kernel, head_count=head_count,...  35.6 us
    all_gather x1, waiting for transfers between devices, local(): lax.all_gather(grad_resid.astype(jnp.bfloat16), 'tensor', axis=0, tiled=T...  27.7 us
  transfers between devices with their start and end apart: 12, of which 6 were waited for; matrix products, arithmetic and copies ran while one was open for 15% of the time, Pallas kernels for 0%

profile of v2, /device:TPU:0, one launch (start us, length us, event | category | flops | bytes accessed | tf_op | source)
XLA Modules:
  0.0 694.7 jit_solution(18301395687091779633)
XLA Ops:
  12.4 22.9 %attend_forward.1 = (bf16[2048,768]{1,0:T(8,128)(2,1)}, bf16[576,2048]{1,0:T(8,128)(2,1)S(1)}, bf16[192,2048]{1,0:T(8,128)(2,1)S(1)}, f32[8,2048]{1,0:T(8,128)S(1)}) custom-call(s32[1,8]{1,0:T(1,128)S(1)} %copy-done.9, bf16[2048,768]{1,0:T(8,128)(2,1)} %tokens_ref.3, f32[1,768]{1,0:T(1,128)S(1)} %broadcast_in_dim.18.gain_ref, ...), custom_call_target="tpu_custom_call" | custom-call | flops 3623878656 | bytes 15728640 | tf_op jit(solution)/shard_map/attend_forward/pallas_call | solution.py:225
  40.8 7.3 %all-to-all-start.1 = ((s32[8,1,256]{2,1,0:T(1,128)}), s32[8,1,256]{2,1,0:T(1,128)S(1)}, u32[]{:S(2)}, u32[]{:S(2)}) async-start(s32[8,1,256]{2,1,0:T(1,128)} %bitcast.9), calls=%async_computation.2 | async-start | bytes 16384 | tf_op jit(solution)/shard_map/all_to_all | solution.py:351
  51.7 3.5 convolution_convert_fusion.1
  55.2 6.4 all-to-all-start
  61.6 70.2 %all-to-all-done = bf16[8,256,768]{2,1,0:T(8,128)(2,1)} async-done(((bf16[8,256,768]{2,1,0:T(8,128)(2,1)}), bf16[8,256,768]{2,1,0:T(8,128)(2,1)}, u32[]{:S(2)}, u32[]{:S(2)}) %all-to-all-start) | async-done | bytes 3145760 | tf_op jit(solution)/shard_map/all_to_all | solution.py:351
  133.5 5.0 convolution_convert_fusion
  138.5 4.5 all-to-all-start.2
  143.8 69.4 %all-to-all-done.2 = bf16[8,256,768]{2,1,0:T(8,128)(2,1)} async-done(((bf16[8,256,768]{2,1,0:T(8,128)(2,1)}), bf16[8,256,768]{2,1,0:T(8,128)(2,1)}, u32[]{:S(2)}, u32[]{:S(2)}) %all-to-all-start.2) | async-done | bytes 3145760 | tf_op jit(solution)/shard_map/all_to_all | solution.py:351
  213.2 2.8 fusion.23
  216.1 17.5 %fusion.41 = f32[2048,4,768]{0,2,1:T(8,128)} fusion(bf16[2048,768,1]{1,0,2:T(8,128)(2,1)} %bitcast.14, bf16[4,768,768]{2,1,0:T(8,128)(2,1)} %all-gather.4.cloned.1.call-done), kind=kOutput, calls=%fused_computation.94 | convolution fusion | flops 9663676416 | bytes 33030144 | tf_op jit(solution)/shard_map/sd,jdf->jsf/dot_general | solution.py:405
  233.6 37.8 %fusion.6 = (f32[2048]{0:T(1024)S(1)}, bf16[4,2048,768]{1,2,0:T(8,128)(2,1)}, bf16[4,2048,768]{1,2,0:T(8,128)(2,1)}) fusion(f32[2048,4,768]{0,2,1:T(8,128)} %fusion.41, f32[2048]{0:T(1024)S(1)} %add_divide_fusion, bf16[4,768,768]{2,1,0:T(8,128)(2,1)} %all-gather.6.cloned.1.call-done, bf16[2048,768]{1,0:T(8,128)(2,1)} %bitcast.8), kind=kOutput, calls=%fused_computation.12 | convolution fusion | flops 9846126592 | bytes 58212352 | tf_op jit(solution)/shard_map/sd,jfd->jsf/dot_general | solution.py:419
  271.4 13.6 %fusion.42 = f32[2048,768,1]{1,0,2:T(8,128)S(1)} fusion(bf16[4,2048,768]{1,2,0:T(8,128)(2,1)} %get-tuple-element.91, bf16[4,768,768]{2,1,0:T(8,128)(2,1)S(1)} %copy-done.29), kind=kOutput, calls=%fused_computation.95 | convolution fusion | flops 9663676416 | bytes 23592960 | tf_op jit(solution)/shard_map/jsf,jdf->sd/dot_general | solution.py:425
  285.0 2.8 fusion.11
  287.8 4.4 all-to-all-start.3
  292.3 15.4 %convert_bitcast_fusion = bf16[4,768,768]{1,2,0:T(8,128)(2,1)} fusion(bf16[4,2048,768]{1,2,0:T(8,128)(2,1)} %get-tuple-element.91, bf16[2048,768,1]{1,0,2:T(8,128)(2,1)} %bitcast.14), kind=kOutput, calls=%fused_computation.26 | convolution fusion | flops 9666035712 | bytes 20447232 | tf_op jit(solution)/shard_map/sd,jsf->jdf/dot_general | solution.py:437
  307.8 15.6 %fusion.19 = bf16[4,768,768]{2,1,0:T(8,128)(2,1)} fusion(bf16[4,2048,768]{1,2,0:T(8,128)(2,1)} %get-tuple-element.92, bf16[2048,768]{1,0:T(8,128)(2,1)} %bitcast.8, f32[2048]{0:T(1024)S(1)} %add_divide_fusion), kind=kOutput, calls=%fused_computation.36 | convolution fusion | flops 9670754304 | bytes 20455424 | tf_op jit(solution)/shard_map/jsf,sd->jfd/dot_general | solution.py:434
  323.4 16.0 %fusion.10 = bf16[2048,768]{1,0:T(8,128)(2,1)} fusion(bf16[4,2048,768]{1,2,0:T(8,128)(2,1)} %get-tuple-element.92, bf16[4,768,768]{2,1,0:T(8,128)(2,1)} %all-gather.6.cloned.1.call-done, f32[2048]{0:T(1024)S(1)} %add_divide_fusion), kind=kOutput, calls=%fused_computation.22 | convolution fusion | flops 9666822144 | bytes 20455424 | tf_op jit(solution)/shard_map/jsf,jfd->sd/dot_general | solution.py:430
  339.4 23.0 %all-to-all-done.3 = bf16[8,256,768]{2,1,0:T(8,128)(2,1)} async-done(((bf16[8,256,768]{2,1,0:T(8,128)(2,1)}), bf16[8,256,768]{2,1,0:T(8,128)(2,1)}, u32[]{:S(2)}, u32[]{:S(2)}) %all-to-all-start.3) | async-done | bytes 3145760 | tf_op jit(solution)/shard_map/all_to_all | solution.py:351
  362.5 4.2 multiply_reduce_fusion
  367.9 2.6 fusion.38
  370.5 27.7 %all-gather.8.cloned.1.call-done.grad_ref = bf16[2048,768]{1,0:T(8,128)(2,1)} async-done(((bf16[512,768]{1,0:T(8,128)(2,1)}), bf16[2048,768]{1,0:T(8,128)(2,1)}) %all-gather.8.cloned.1.call-update) | async-done | bytes 3145744 | tf_op jit(solution)/shard_map/all_gather | solution.py:448
  398.2 35.6 %attend_backward.1 = (bf16[2048,768]{1,0:T(8,128)(2,1)}, f32[576,768]{1,0:T(8,128)S(1)}, f32[192,768]{1,0:T(8,128)S(1)}, f32[8,768]{1,0:T(8,128)S(1)}, f32[8,512]{1,0:T(8,128)S(1)}, /*index=5*/f32[8,256]{1,0:T(8,128)S(1)}) custom-call(s32[1,8]{1,0:T(1,128)S(1)} %copy-done.10, bf16[2048,768]{1,0:T(8,128)(2,1)} %tokens_ref.3, f32[1,768]{1,0:T(1,128)S(1)} %copy-done.4, ...), custom_call_target="tpu_custom_call" | custom-call | flops 7851737088 | bytes 22020096 | tf_op jit(solution)/shard_map/attend_backward/pallas_call | solution.py:274
  436.4 105.1 %all_to_all.29 = bf16[8,256,768]{2,1,0:T(8,128)(2,1)} all-to-all(bf16[8,256,768]{2,1,0:T(8,128)(2,1)} %bitcast.114), channel_id=1, replica_groups=mesh['expert'=8,'tensor'=4] {'expert'}, dimensions={0} | all-to-all | bytes 6291456 | tf_op jit(solution)/shard_map/all_to_all | solution.py:351
  541.6 2.5 fusion.27
  544.8 38.7 %psum.14 = f32[9216]{0:T(1024)S(1)} all-reduce(f32[9216]{0:T(1024)S(1)} %pad_maximum_fusion.1), channel_id=1, replica_groups=mesh['expert'=8,'tensor'=4] {'expert','tensor'}, use_global_device_ids=true, to_apply=%region_16.17 | all-reduce | flops 9216 | bytes 73728 | tf_op jit(solution)/shard_map/psum | solution.py:471
  585.5 5.1 convolution_add_fusion
  590.6 2.6 slice.87
  594.1 2.9 copy.50
  596.9 46.8 %reduce-scatter.11.cloned.1.call-done = bf16[1,768,768]{2,1,0:T(8,128)(2,1)} async-done(((bf16[4,768,768]{2,1,0:T(8,128)(2,1)}), bf16[1,768,768]{2,1,0:T(8,128)(2,1)}) %reduce-scatter.11.cloned.1.call-update) | async-done | bytes 1179664 | tf_op jit(solution)/shard_map/reduce_scatter | solution.py:449
  643.7 2.8 convert_element_type.103
  646.5 37.7 %reduce-scatter.7.cloned.1.call-done = bf16[512,768]{1,0:T(8,128)(2,1)} async-done(((bf16[2048,768]{1,0:T(8,128)(2,1)}), bf16[512,768]{1,0:T(8,128)(2,1)}) %reduce-scatter.7.cloned.1.call-update) | async-done | bytes 786448 | tf_op jit(solution)/shard_map/reduce_scatter | solution.py:458
  684.2 3.2 convert_add_fusion
  (131 shorter events, 23.9 us)
Async XLA Ops:
  7.2 206.0 %copy-start = (bf16[768,8]{0,1:T(8,128)(2,1)S(1)}, bf16[768,8]{0,1:T(8,128)(2,1)}, u32[]{:S(2)}) copy-start(bf16[768,8]{0,1:T(8,128)(2,1)} %param.20) | copy-start | bytes 36868
  7.2 124.6 %reduce-scatter.5.cloned.1.call-start = ((), (), s32[]{:S(2)}) async-start(), calls=%async_computation.9 | async-start | bytes 3932160 | tf_op jit(solution)/shard_map/reduce_scatter | solution.py:395
  7.9 27.4 %copy-start.3 = (f32[1,768]{1,0:T(1,128)}, f32[1,768]{1,0:T(1,128)S(1)}, u32[]{:S(2)}) copy-start(f32[1,768]{1,0:T(1,128)S(1)} %broadcast_in_dim.18.gain_ref) | copy-start | bytes 9220
  9.6 25.7 %copy-start.1 = (f32[8,512]{1,0:T(8,128)}, f32[8,512]{1,0:T(8,128)S(1)}, u32[]{:S(2)}) copy-start(f32[8,512]{1,0:T(8,128)S(1)} %concatenate.19.bias_ref) | copy-start | bytes 49156
  40.8 14.4 %all-to-all-start.1 = ((s32[8,1,256]{2,1,0:T(1,128)}), s32[8,1,256]{2,1,0:T(1,128)S(1)}, u32[]{:S(2)}, u32[]{:S(2)}) async-start(s32[8,1,256]{2,1,0:T(1,128)} %bitcast.9), calls=%async_computation.2 | async-start | bytes 16384 | tf_op jit(solution)/shard_map/all_to_all | solution.py:351
  48.1 168.0 %all-gather.4.cloned.1.call-start = ((), (), s32[]{:S(2)}) async-start(), calls=%async_computation.10 | async-start | bytes 5898240 | tf_op jit(solution)/shard_map/all_gather | solution.py:402
  51.7 81.8 %copy-start.19 = (pred[512,2048]{1,0:T(32,128)(4,1)}, pred[512,2048]{1,0:T(32,128)(4,1)S(1)}, u32[]{:S(2)}) copy-start(pred[512,2048]{1,0:T(32,128)(4,1)S(1)} %fusion.12) | copy-start | bytes 3145732
  55.2 78.3 %copy-start.27 = (f32[768]{0:T(1024)S(1)}, f32[768]{0:T(1024)}, u32[]{:S(2)}) copy-start(f32[768]{0:T(1024)} %param.19) | copy-start | bytes 9220
  55.2 76.6 %all-to-all-start = ((bf16[8,256,768]{2,1,0:T(8,128)(2,1)}), bf16[8,256,768]{2,1,0:T(8,128)(2,1)}, u32[]{:S(2)}, u32[]{:S(2)}) async-start(bf16[8,256,768]{2,1,0:T(8,128)(2,1)} %bitcast.115), calls=%async_computation.1 | async-start | bytes 6291456 | tf_op jit(solution)/shard_map/all_to_all | solution.py:351
  133.5 5.1 copy-start.25
  138.5 74.7 %all-to-all-start.2 = ((bf16[8,256,768]{2,1,0:T(8,128)(2,1)}), bf16[8,256,768]{2,1,0:T(8,128)(2,1)}, u32[]{:S(2)}, u32[]{:S(2)}) async-start(bf16[8,256,768]{2,1,0:T(8,128)(2,1)} %bitcast.116), calls=%async_computation.3 | async-start | bytes 6291456 | tf_op jit(solution)/shard_map/all_to_all | solution.py:351
  143.0 90.6 %all-gather.6.cloned.1.call-start = ((), (), s32[]{:S(2)}) async-start(), calls=%async_computation.11 | async-start | bytes 5898240 | tf_op jit(solution)/shard_map/all_gather | solution.py:403
  233.6 37.8 %copy-start.29 = (bf16[4,768,768]{2,1,0:T(8,128)(2,1)S(1)}, bf16[4,768,768]{2,1,0:T(8,128)(2,1)}, u32[]{:S(2)}) copy-start(bf16[4,768,768]{2,1,0:T(8,128)(2,1)} %all-gather.4.cloned.1.call-done) | copy-start | bytes 14155780
  287.8 74.6 %all-to-all-start.3 = ((bf16[8,256,768]{2,1,0:T(8,128)(2,1)}), bf16[8,256,768]{2,1,0:T(8,128)(2,1)}, u32[]{:S(2)}, u32[]{:S(2)}) async-start(bf16[8,256,768]{2,1,0:T(8,128)(2,1)} %bitcast.112), calls=%async_computation.4 | async-start | bytes 6291456 | tf_op jit(solution)/shard_map/all_to_all | solution.py:351
  292.3 105.9 %all-gather.8.cloned.1.call-start = ((), (), s32[]{:S(2)}) async-start(), calls=%async_computation.12 | async-start | bytes 3932160 | tf_op jit(solution)/shard_map/all_gather | solution.py:448
  323.4 39.1 %copy-start.12 = (bf16[512,768]{1,0:T(8,128)(2,1)S(1)}, bf16[512,768]{1,0:T(8,128)(2,1)}, u32[]{:S(2)}) copy-start(bf16[512,768]{1,0:T(8,128)(2,1)} %reduce-scatter.5.cloned.1.call-done) | copy-start | bytes 2359300
  323.4 39.1 %copy-start.20 = (pred[512,2048]{1,0:T(32,128)(4,1)S(1)}, pred[512,2048]{1,0:T(32,128)(4,1)}, u32[]{:S(2)}) copy-start(pred[512,2048]{1,0:T(32,128)(4,1)} %copy-done.19) | copy-start | bytes 3145732
  323.4 39.1 %copy-start.24 = (f32[512]{0:T(512)S(1)}, f32[512]{0:T(512)}, u32[]{:S(2)}) copy-start(f32[512]{0:T(512)} %copy-done.23) | copy-start | bytes 6148
  323.4 39.1 %copy-start.28 = (f32[768]{0:T(1024)S(1)}, f32[768]{0:T(1024)}, u32[]{:S(2)}) copy-start(f32[768]{0:T(1024)} %param.19) | copy-start | bytes 9220
  362.5 5.4 copy-start.17
  366.7 31.5 %copy-start.2 = (f32[8,512]{1,0:T(8,128)S(1)}, f32[8,512]{1,0:T(8,128)}, u32[]{:S(2)}) copy-start(f32[8,512]{1,0:T(8,128)} %copy-done.1) | copy-start | bytes 49156
  366.7 31.5 %copy-start.4 = (f32[1,768]{1,0:T(1,128)S(1)}, f32[1,768]{1,0:T(1,128)}, u32[]{:S(2)}) copy-start(f32[1,768]{1,0:T(1,128)} %copy-done.3) | copy-start | bytes 9220
  366.7 31.5 %copy-start.6 = (bf16[768,3,192]{0,2,1:T(8,128)(2,1)S(1)}, bf16[768,3,192]{0,2,1:T(8,128)(2,1)}, u32[]{:S(2)}) copy-start(bf16[768,3,192]{0,2,1:T(8,128)(2,1)} %param.16) | copy-start | bytes 2654212
  366.8 31.5 %copy-start.8 = (bf16[192,768]{1,0:T(8,128)(2,1)S(1)}, bf16[192,768]{1,0:T(8,128)(2,1)}, u32[]{:S(2)}) copy-start(bf16[192,768]{1,0:T(8,128)(2,1)} %out_ref.3) | copy-start | bytes 884740
  366.8 31.5 %copy-start.10 = (s32[1,8]{1,0:T(1,128)S(1)}, s32[1,8]{1,0:T(1,128)}, u32[]{:S(2)}) copy-start(s32[1,8]{1,0:T(1,128)} %lengths_ref.3) | copy-start | bytes 100
  370.5 220.1 %all-reduce.3.cloned.1.call-start = ((), (), s32[]{:S(2)}) async-start(), calls=%async_computation.14 | async-start | bytes 2359296 | tf_op jit(solution)/shard_map/psum | solution.py:461
  435.0 159.0 %reduce-scatter.9.cloned.1.call-start = ((), (), s32[]{:S(2)}) async-start(), calls=%async_computation.15 | async-start | bytes 5898240 | tf_op jit(solution)/shard_map/reduce_scatter | solution.py:450
  435.6 208.0 %reduce-scatter.11.cloned.1.call-start = ((), (), s32[]{:S(2)}) async-start(), calls=%async_computation.16 | async-start | bytes 5898240 | tf_op jit(solution)/shard_map/reduce_scatter | solution.py:449
  436.4 247.8 %reduce-scatter.7.cloned.1.call-start = ((), (), s32[]{:S(2)}) async-start(), calls=%async_computation.13 | async-start | bytes 3932160 | tf_op jit(solution)/shard_map/reduce_scatter | solution.py:458
  541.6 43.9 %copy-start.21 = (pred[512,2048]{1,0:T(32,128)(4,1)S(1)}, pred[512,2048]{1,0:T(32,128)(4,1)}, u32[]{:S(2)}) copy-start(pred[512,2048]{1,0:T(32,128)(4,1)} %copy-done.19) | copy-start | bytes 3145732
  594.0 90.1 %copy-start.14 = (f32[512,768]{1,0:T(8,128)S(1)}, f32[512,768]{1,0:T(8,128)}, u32[]{:S(2)}) copy-start(f32[512,768]{1,0:T(8,128)} %copy-done.13) | copy-start | bytes 4718596
  594.0 90.1 %copy-start.18 = (bf16[512,768]{1,0:T(8,128)(2,1)S(1)}, bf16[512,768]{1,0:T(8,128)(2,1)}, u32[]{:S(2)}) copy-start(bf16[512,768]{1,0:T(8,128)(2,1)} %param.23) | copy-start | bytes 2359300
  (10 other events, 21.5 us)
Sparse Core Ops, SparseCore 0:
  36.9 40.6 reduce-scatter.4
  79.2 37.4 all-gather.3
  145.5 38.7 all-gather.5
  370.6 27.5 all-gather.7
  435.2 107.8 all-reduce.2
  545.5 47.5 reduce-scatter.8
  595.8 47.8 reduce-scatter.10
  646.2 37.9 reduce-scatter.6

commit v3 on v2

--- a/solution.py
+++ b/solution.py
@@ -353,6 +353,65 @@
     ).reshape(rows.shape)
 
 
+def swap(value, axis_name, bit):
+    count = lax.axis_size(axis_name)
+    return lax.ppermute(value, axis_name, [(i, i ^ (1 << bit)) for i in range(count)])
+
+
+def own_bit(axis_name, bit):
+    return (lax.axis_index(axis_name) >> bit) & 1
+
+
+def scatter_sum(pieces, axis_name, order):
+    bits = sorted(order, reverse=True)
+    total = pieces.reshape((2,) * len(bits) + pieces.shape[1:])
+    for bit in order:
+        dim = bits.index(bit)
+        bits.remove(bit)
+        mine = own_bit(axis_name, bit)
+        keep = lax.dynamic_index_in_dim(total, mine, dim, keepdims=False)
+        send = lax.dynamic_index_in_dim(total, 1 - mine, dim, keepdims=False)
+        got = swap(send.astype(jnp.bfloat16), axis_name, bit)
+        total = keep.astype(jnp.float32) + got.astype(jnp.float32)
+    return total
+
+
+def gather(piece, axis_name, order):
+    bits = []
+    whole_value = piece
+    for bit in order:
+        bits = sorted(bits + [bit], reverse=True)
+        dim = bits.index(bit)
+        got = swap(whole_value, axis_name, bit)
+        first = own_bit(axis_name, bit) == 0
+        whole_value = jnp.stack(
+            [jnp.where(first, whole_value, got), jnp.where(first, got, whole_value)], axis=dim
+        )
+    return whole_value.reshape((-1,) + piece.shape[1:])
+
+
+def butterfly(value, axis_name):
+    for bit in range(bit_count(axis_name)):
+        value = value + swap(value, axis_name, bit)
+    return value
+
+
+def bit_count(axis_name):
+    return (lax.axis_size(axis_name) - 1).bit_length()
+
+
+def sum_rows(rows, axis_name):
+    bits = list(range(bit_count(axis_name)))
+    parts = lax.axis_size(axis_name)
+    results = []
+    for half, turn in zip(jnp.split(rows, 2, axis=0), (0, 1)):
+        order = bits[turn:] + bits[:turn]
+        pieces = half.reshape((parts, -1) + rows.shape[1:])
+        own = scatter_sum(pieces, axis_name, order).astype(jnp.bfloat16)
+        results.append(gather(own, axis_name, order[::-1]))
+    return jnp.concatenate(results, axis=0)
+
+
 def local(
     tokens,
     lengths,
@@ -385,20 +444,24 @@
     slot_match = slot_index[:, :, None] == slot_ids[None, None, :]
     dispatch = (slot_match[:, 0] | slot_match[:, 1]).astype(jnp.bfloat16)
     other_ids = jnp.sum(jnp.where(slot_match, routes[:, ::-1, None] + 1, 0), axis=(0, 1))
-    other_here = exchange(other_ids)
-    grad_rows = exchange(mul(dispatch, out_grad, 0, 0).astype(jnp.bfloat16))
+    grad_slots = mul(dispatch, out_grad, 0, 0).astype(jnp.bfloat16)
+    grad_rows = exchange(grad_slots)
+    tokens, _ = lax.optimization_barrier((tokens, grad_slots))
+    tensor_bits = list(range(bit_count("tensor")))
 
     qkv_flat = attn_qkv.transpose(1, 2, 0).reshape(3 * inner, width)
     branch, projected, mixed, log_total = attend(
         tokens, lengths, norm1_gain, qkv_flat, attn_out, rel_bias
     )
-    branch = lax.psum_scatter(branch, "tensor", scatter_dimension=0, tiled=True)
-    branch, grad_rows, other_here = lax.optimization_barrier((branch, grad_rows, other_here))
+    branch = scatter_sum(branch.reshape(n_tensor, own_rows, width), "tensor", tensor_bits)
     own_tokens = lax.dynamic_slice_in_dim(tokens, tensor_index * own_rows, own_rows, 0)
-    resid = own_tokens.astype(jnp.float32) + branch.astype(jnp.float32)
+    resid = own_tokens.astype(jnp.float32) + branch
     normed_two, norm2_pull = jax.vjp(rms_norm, resid, norm2_gain)
     hidden_two = normed_two.astype(jnp.bfloat16)
-    expert_rows = exchange(mul(dispatch, hidden_two, 0, 0).astype(jnp.bfloat16))
+    outgoing = mul(dispatch, hidden_two, 0, 0).astype(jnp.bfloat16)
+    outgoing, other_ids, grad_rows = lax.optimization_barrier((outgoing, other_ids, grad_rows))
+    expert_rows = exchange(outgoing)
+    other_here = exchange(other_ids)
     weights_in = lax.all_gather(expert_in[0], "tensor")
     weights_out = lax.all_gather(expert_out[0], "tensor")
 
@@ -445,7 +508,7 @@
     grad_hidden_two = jnp.dot(dispatch, grad_sent, preferred_element_type=jnp.float32)
     grad_resid_norm, gain_two_part = norm2_pull(grad_hidden_two)
     grad_resid = grad_in + grad_resid_norm
-    grad_branch = lax.all_gather(grad_resid.astype(jnp.bfloat16), "tensor", axis=0, tiled=True)
+    grad_branch = gather(grad_resid.astype(jnp.bfloat16), "tensor", tensor_bits[::-1])
     grad_w_out = lax.psum_scatter(grad_w_out, "tensor", scatter_dimension=0)
     grad_w_in = lax.psum_scatter(grad_w_in, "tensor", scatter_dimension=0)
 
@@ -453,12 +516,18 @@
         tokens, lengths, norm1_gain, qkv_flat, attn_out, rel_bias,
         projected, mixed, log_total, grad_branch,
     )
-    tokens_part, came_back = lax.optimization_barrier((tokens_part, came_back))
+    (tokens_part, qkv_part, out_part, gain_one_part, bias_part, came_back, grad_w_in, grad_w_out) = (
+        lax.optimization_barrier(
+            (tokens_part, qkv_part, out_part, gain_one_part, bias_part, came_back, grad_w_in, grad_w_out)
+        )
+    )
     output = resid + jnp.dot(dispatch, came_back, preferred_element_type=jnp.float32)
-    tokens_shared = lax.psum_scatter(tokens_part, "tensor", scatter_dimension=0, tiled=True)
-    grad_tokens = grad_resid + tokens_shared.astype(jnp.float32)
+    tokens_shared = scatter_sum(
+        tokens_part.reshape(n_tensor, own_rows, width), "tensor", tensor_bits
+    )
+    grad_tokens = grad_resid + tokens_shared
     weights_part = jnp.concatenate([qkv_part, out_part], axis=0).astype(jnp.bfloat16)
-    weights_total = lax.psum(weights_part, "expert").astype(jnp.float32)
+    weights_total = sum_rows(weights_part, "expert").astype(jnp.float32)
     bias_slots = lax.dynamic_update_slice_in_dim(
         jnp.zeros((n_tensor * head_count, bucket_count), jnp.float32),
         bias_part,
@@ -468,7 +537,7 @@
     small = jnp.concatenate(
         [gain_one_part, gain_two_part, router_part.T.reshape(-1), bias_slots.reshape(-1)]
     )
-    small = lax.psum(small, ("expert", "tensor"))
+    small = butterfly(butterfly(small, "tensor"), "expert")
     count = 2 + expert_count
     columns = lax.dynamic_slice_in_dim(
         small[: count * width].reshape(count, width),

time: 703 us -> 535 us (0.76)
  blocking collectives: 144 us -> 9.95 us
  waiting for transfers between devices: 277 us -> 211 us
  starting transfers between devices: 22.9 us -> 48.4 us
  other arithmetic: 18.7 us -> 27.1 us
    all_to_all x1, blocking collectives: 105 us -> 9.95 us  [exchange(): lax.all_to_all(rows.reshape((parts, -1) + rows.shape[1:]), 'expert', spli...]
    ppermute x0 -> x23, waiting for transfers between devices: none -> 87.3 us  [swap(): lax.ppermute(value, axis_name, [(i, i ^ 1 << bit) for i in range(count)])]
    all_to_all x4, waiting for transfers between devices: 163 us -> 102 us  [exchange(): lax.all_to_all(rows.reshape((parts, -1) + rows.shape[1:]), 'expert', spli...]
    psum x1 -> x0, blocking collectives: 38.7 us -> none  [local(): small = lax.psum(small, ('expert', 'tensor'))]
    reduce_scatter x2 -> x0, waiting for transfers between devices: 37.7 us -> none  [the longest x1 37.7 us: local(): lax.psum_scatter(tokens_part, 'tensor', scatter_dimension=0, tiled=True)]
    all_gather x1 -> x0, waiting for transfers between devices: 27.7 us -> none  [local(): lax.all_gather(grad_resid.astype(jnp.bfloat16), 'tensor', axis=0, tiled=T...]
    ppermute x0 -> x23, starting transfers between devices: none -> 26.6 us  [swap(): lax.ppermute(value, axis_name, [(i, i ^ 1 << bit) for i in range(count)])]
    reduce_scatter x1, waiting for transfers between devices: 46.8 us -> 20.5 us  [local(): grad_w_out = lax.psum_scatter(grad_w_out, 'tensor', scatter_dimension=0)]
  transfers between devices with their start and end apart: 12 -> 31, of which waited for: 6 -> 21; matrix products, arithmetic and copies ran while one was open for 15% -> 22% of each run, Pallas kernels for 0% -> 11%
where the time goes in v3:
time: 535 us; the launch traced here: 530 us
  waiting for transfers between devices  211 us (39%)
  matrix products  141 us (26%)
  Pallas kernels  58.9 us (11%)
  starting transfers between devices  48.4 us (9%)
  other arithmetic  27.1 us (5%)
  local copies, waits for them, and re-layouts  18.5 us (3%)
  between operations  14.9 us (3%)
  blocking collectives  9.95 us (2%)
    all_to_all x4, waiting for transfers between devices, exchange(): lax.all_to_all(rows.reshape((parts, -1) + rows.shape[1:]), 'expert', spli...  102 us
    ppermute x23, waiting for transfers between devices, swap(): lax.ppermute(value, axis_name, [(i, i ^ 1 << bit) for i in range(count)])  87.3 us
    dot_general x1, matrix products, local(): jnp.einsum('sd,jfd->jsf', grad_rows, weights_out, preferred_element_type=...  38.2 us
    pallas_call x1, Pallas kernels, attend_back(): pl.pallas_call(functools.partial(backward_kernel, head_count=head_count,...  35.9 us
    ppermute x23, starting transfers between devices, swap(): lax.ppermute(value, axis_name, [(i, i ^ 1 << bit) for i in range(count)])  26.6 us
    pallas_call x1, Pallas kernels, attend(): pl.pallas_call(functools.partial(forward_kernel, head_count=head_count, h...  22.9 us
    all_to_all x4, starting transfers between devices, exchange(): lax.all_to_all(rows.reshape((parts, -1) + rows.shape[1:]), 'expert', spli...  21.3 us
    reduce_scatter x1, waiting for transfers between devices, local(): grad_w_out = lax.psum_scatter(grad_w_out, 'tensor', scatter_dimension=0)  20.5 us
  transfers between devices with their start and end apart: 31, of which 21 were waited for; matrix products, arithmetic and copies ran while one was open for 22% of the time, Pallas kernels for 11%

profile of v3, /device:TPU:0, one launch (start us, length us, event | category | flops | bytes accessed | tf_op | source)
XLA Modules:
  0.0 530.3 jit_solution(13093727577435685830)
XLA Ops:
  14.4 3.5 convolution_convert_fusion.1
  17.9 7.8 %all-to-all-start = ((bf16[8,256,768]{2,1,0:T(8,128)(2,1)}), bf16[8,256,768]{2,1,0:T(8,128)(2,1)}, u32[]{:S(2)}, u32[]{:S(2)}) async-start(bf16[8,256,768]{2,1,0:T(8,128)(2,1)} %bitcast.222), calls=%async_computation | async-start | bytes 6291456 | tf_op jit(solution)/shard_map/all_to_all | solution.py:351
  26.1 22.9 %attend_forward.1 = (bf16[2048,768]{1,0:T(8,128)(2,1)}, bf16[576,2048]{1,0:T(8,128)(2,1)S(1)}, bf16[192,2048]{1,0:T(8,128)(2,1)S(1)}, f32[8,2048]{1,0:T(8,128)S(1)}) custom-call(s32[1,8]{1,0:T(1,128)S(1)} %copy-done.10, bf16[2048,768]{1,0:T(8,128)(2,1)} %tokens_ref.1, f32[1,768]{1,0:T(1,128)S(1)} %broadcast_in_dim.48.gain_ref, ...), custom_call_target="tpu_custom_call" | custom-call | flops 3623878656 | bytes 15728640 | tf_op jit(solution)/shard_map/attend_forward/pallas_call | solution.py:225
  50.4 2.7 dynamic-slice_bitcast_fusion.1
  53.1 3.6 collective-permute-done
  63.0 16.8 %collective-permute-done.1 = bf16[512,768]{1,0:T(8,128)(2,1)S(1)} collective-permute-done((bf16[512,768]{1,0:T(8,128)(2,1)S(1)}, bf16[512,768]{1,0:T(8,128)(2,1)S(1)}, u32[]{:S(2)}, u32[]{:S(2)}) %collective-permute-start.1) | collective-permute-done | bytes 786464 | tf_op jit(solution)/shard_map/ppermute | solution.py:358
  83.0 3.6 convolution_convert_fusion
  86.6 9.8 %all-to-all-done = bf16[8,256,768]{2,1,0:T(8,128)(2,1)} async-done(((bf16[8,256,768]{2,1,0:T(8,128)(2,1)}), bf16[8,256,768]{2,1,0:T(8,128)(2,1)}, u32[]{:S(2)}, u32[]{:S(2)}) %all-to-all-start) | async-done | bytes 3145760 | tf_op jit(solution)/shard_map/all_to_all | solution.py:351
  96.4 9.9 %all_to_all.29 = s32[8,1,256]{2,1,0:T(1,128)S(1)} all-to-all(s32[8,1,256]{2,1,0:T(1,128)S(1)} %bitcast.242), channel_id=1, replica_groups=mesh['expert'=8,'tensor'=4] {'expert'}, dimensions={0} | all-to-all | bytes 16384 | tf_op jit(solution)/shard_map/all_to_all | solution.py:351
  106.4 4.5 all-to-all-start.1
  111.6 69.0 %all-to-all-done.1 = bf16[8,256,768]{2,1,0:T(8,128)(2,1)} async-done(((bf16[8,256,768]{2,1,0:T(8,128)(2,1)}), bf16[8,256,768]{2,1,0:T(8,128)(2,1)}, u32[]{:S(2)}, u32[]{:S(2)}) %all-to-all-start.1) | async-done | bytes 3145760 | tf_op jit(solution)/shard_map/all_to_all | solution.py:351
  180.6 2.8 fusion.25
  183.5 17.5 %fusion.51 = f32[2048,4,768]{0,2,1:T(8,128)} fusion(bf16[2048,768,1]{1,0,2:T(8,128)(2,1)} %bitcast.17, bf16[4,768,768]{2,1,0:T(8,128)(2,1)} %all-gather.3.cloned.1.call-done), kind=kOutput, calls=%fused_computation.149 | convolution fusion | flops 9663676416 | bytes 33030144 | tf_op jit(solution)/shard_map/sd,jdf->jsf/dot_general | solution.py:468
  201.0 38.2 %fusion.6 = (f32[2048]{0:T(1024)S(1)}, bf16[4,2048,768]{1,2,0:T(8,128)(2,1)}, bf16[4,2048,768]{1,2,0:T(8,128)(2,1)}) fusion(f32[2048,4,768]{0,2,1:T(8,128)} %fusion.51, f32[2048]{0:T(1024)S(1)} %add_divide_fusion, bf16[4,768,768]{2,1,0:T(8,128)(2,1)} %all-gather.5.cloned.1.call-done, bf16[2048,768]{1,0:T(8,128)(2,1)} %bitcast.14), kind=kOutput, calls=%fused_computation.12 | convolution fusion | flops 9846126592 | bytes 58212352 | tf_op jit(solution)/shard_map/sd,jfd->jsf/dot_general | solution.py:482
  239.2 13.3 %fusion.52 = f32[2048,768,1]{1,0,2:T(8,128)S(1)} fusion(bf16[4,2048,768]{1,2,0:T(8,128)(2,1)} %get-tuple-element.107, bf16[4,768,768]{2,1,0:T(8,128)(2,1)S(1)} %copy-done.43), kind=kOutput, calls=%fused_computation.150 | convolution fusion | flops 9663676416 | bytes 23592960 | tf_op jit(solution)/shard_map/jsf,jdf->sd/dot_general | solution.py:488
  252.6 2.9 fusion.11
  255.4 4.4 all-to-all-start.3
  259.9 15.5 %convert_bitcast_fusion = bf16[4,768,768]{1,2,0:T(8,128)(2,1)} fusion(bf16[4,2048,768]{1,2,0:T(8,128)(2,1)} %get-tuple-element.107, bf16[2048,768,1]{1,0,2:T(8,128)(2,1)} %bitcast.17), kind=kOutput, calls=%fused_computation.26 | convolution fusion | flops 9666035712 | bytes 20447232 | tf_op jit(solution)/shard_map/sd,jsf->jdf/dot_general | solution.py:500
  275.5 15.7 %fusion.19 = bf16[4,768,768]{2,1,0:T(8,128)(2,1)} fusion(bf16[4,2048,768]{1,2,0:T(8,128)(2,1)} %get-tuple-element.108, bf16[2048,768]{1,0:T(8,128)(2,1)} %bitcast.14, f32[2048]{0:T(1024)S(1)} %add_divide_fusion), kind=kOutput, calls=%fused_computation.39 | convolution fusion | flops 9670754304 | bytes 20455424 | tf_op jit(solution)/shard_map/jsf,sd->jfd/dot_general | solution.py:497
  291.1 16.0 %fusion.10 = bf16[2048,768]{1,0:T(8,128)(2,1)} fusion(bf16[4,2048,768]{1,2,0:T(8,128)(2,1)} %get-tuple-element.108, bf16[4,768,768]{2,1,0:T(8,128)(2,1)} %all-gather.5.cloned.1.call-done, f32[2048]{0:T(1024)S(1)} %add_divide_fusion), kind=kOutput, calls=%fused_computation.22 | convolution fusion | flops 9666822144 | bytes 20455424 | tf_op jit(solution)/shard_map/jsf,jfd->sd/dot_general | solution.py:493
  307.2 22.9 %all-to-all-done.3 = bf16[8,256,768]{2,1,0:T(8,128)(2,1)} async-done(((bf16[8,256,768]{2,1,0:T(8,128)(2,1)}), bf16[8,256,768]{2,1,0:T(8,128)(2,1)}, u32[]{:S(2)}, u32[]{:S(2)}) %all-to-all-start.3) | async-done | bytes 3145760 | tf_op jit(solution)/shard_map/all_to_all | solution.py:351
  330.7 4.6 all-to-all-start.4
  335.4 4.1 multiply_reduce_fusion
  342.1 28.2 %collective-permute-done.2 = bf16[512,768]{1,0:T(8,128)(2,1)} collective-permute-done((bf16[512,768]{1,0:T(8,128)(2,1)S(1)}, bf16[512,768]{1,0:T(8,128)(2,1)}, u32[]{:S(2)}, u32[]{:S(2)}) %collective-permute-start.2) | collective-permute-done | bytes 786464 | tf_op jit(solution)/shard_map/ppermute | solution.py:358
  380.7 35.9 %attend_backward.1 = (bf16[2048,768]{1,0:T(8,128)(2,1)}, f32[576,768]{1,0:T(8,128)S(1)}, f32[192,768]{1,0:T(8,128)S(1)}, f32[8,768]{1,0:T(8,128)S(1)}, f32[8,512]{1,0:T(8,128)S(1)}, /*index=5*/f32[8,256]{1,0:T(8,128)S(1)}) custom-call(s32[1,8]{1,0:T(1,128)S(1)} %copy-done.11, bf16[2048,768]{1,0:T(8,128)(2,1)} %tokens_ref.1, f32[1,768]{1,0:T(1,128)S(1)} %copy-done.5, ...), custom_call_target="tpu_custom_call" | custom-call | flops 7851737088 | bytes 22020096 | tf_op jit(solution)/shard_map/attend_backward/pallas_call | solution.py:274
  417.2 20.5 %reduce-scatter.5.cloned.1.call-done = bf16[1,768,768]{2,1,0:T(8,128)(2,1)} async-done(((bf16[4,768,768]{2,1,0:T(8,128)(2,1)}), bf16[1,768,768]{2,1,0:T(8,128)(2,1)}) %reduce-scatter.5.cloned.1.call-update) | async-done | bytes 1179664 | tf_op jit(solution)/shard_map/reduce_scatter | solution.py:512
  437.7 5.8 %convolution_add_fusion = f32[512,768]{1,0:T(8,128)} fusion(f32[512,768]{1,0:T(8,128)} %copy-done.13, pred[512,2048]{1,0:T(32,128)(4,1)} %copy-done.26, bf16[2048,768]{1,0:T(8,128)(2,1)} %bitcast.37), kind=kOutput, calls=%fused_computation.58 | convolution fusion | flops 1611005952 | bytes 7340032 | tf_op jit(solution)/shard_map/dot_general | solution.py:524
  475.4 3.1 collective-permute-done.18
  484.7 4.1 collective-permute-done.13
  488.9 3.0 collective-permute-start.21
  496.7 2.8 collective-permute-start.22
  509.6 12.2 %collective-permute-done.5 = bf16[512,768]{1,0:T(8,128)(2,1)S(1)} collective-permute-done((bf16[512,768]{1,0:T(8,128)(2,1)S(1)}, bf16[512,768]{1,0:T(8,128)(2,1)S(1)}, u32[]{:S(2)}, u32[]{:S(2)}) %collective-permute-start.5) | collective-permute-done | bytes 786464 | tf_op jit(solution)/shard_map/ppermute | solution.py:358
  (237 shorter events, 87.7 us)
Async XLA Ops:
  7.2 173.4 %copy-start = (bf16[768,8]{0,1:T(8,128)(2,1)S(1)}, bf16[768,8]{0,1:T(8,128)(2,1)}, u32[]{:S(2)}) copy-start(bf16[768,8]{0,1:T(8,128)(2,1)} %param.20) | copy-start | bytes 36868
  7.2 176.2 %all-gather.3.cloned.1.call-start = ((), (), s32[]{:S(2)}) async-start(), calls=%async_computation.7 | async-start | bytes 5898240 | tf_op jit(solution)/shard_map/all_gather | solution.py:465
  17.9 78.5 %all-to-all-start = ((bf16[8,256,768]{2,1,0:T(8,128)(2,1)}), bf16[8,256,768]{2,1,0:T(8,128)(2,1)}, u32[]{:S(2)}, u32[]{:S(2)}) async-start(bf16[8,256,768]{2,1,0:T(8,128)(2,1)} %bitcast.222), calls=%async_computation | async-start | bytes 6291456 | tf_op jit(solution)/shard_map/all_to_all | solution.py:351
  53.1 3.6 collective-permute-start
  60.2 19.6 %collective-permute-start.1 = (bf16[512,768]{1,0:T(8,128)(2,1)S(1)}, bf16[512,768]{1,0:T(8,128)(2,1)S(1)}, u32[]{:S(2)}, u32[]{:S(2)}) collective-permute-start(bf16[512,768]{1,0:T(8,128)(2,1)S(1)} %fusion.26), channel_id=1, source_target_pairs={{0,2},{1,3},{2,0},{3,1},{4,6},{5,7},{6,4},{7,5},{8,10},{9,11},{10,... | collective-permute-start | bytes 2359304 | tf_op jit(solution)/shard_map/ppermute | solution.py:358
  106.4 74.2 %all-to-all-start.1 = ((bf16[8,256,768]{2,1,0:T(8,128)(2,1)}), bf16[8,256,768]{2,1,0:T(8,128)(2,1)}, u32[]{:S(2)}, u32[]{:S(2)}) async-start(bf16[8,256,768]{2,1,0:T(8,128)(2,1)} %bitcast.223), calls=%async_computation.1 | async-start | bytes 6291456 | tf_op jit(solution)/shard_map/all_to_all | solution.py:351
  110.8 90.1 %all-gather.5.cloned.1.call-start = ((), (), s32[]{:S(2)}) async-start(), calls=%async_computation.8 | async-start | bytes 5898240 | tf_op jit(solution)/shard_map/all_gather | solution.py:466
  255.4 74.6 %all-to-all-start.3 = ((bf16[8,256,768]{2,1,0:T(8,128)(2,1)}), bf16[8,256,768]{2,1,0:T(8,128)(2,1)}, u32[]{:S(2)}, u32[]{:S(2)}) async-start(bf16[8,256,768]{2,1,0:T(8,128)(2,1)} %bitcast.216), calls=%async_computation.3 | async-start | bytes 6291456 | tf_op jit(solution)/shard_map/all_to_all | solution.py:351
  259.9 157.4 %reduce-scatter.3.cloned.1.call-start = ((), (), s32[]{:S(2)}) async-start(), calls=%async_computation.9 | async-start | bytes 5898240 | tf_op jit(solution)/shard_map/reduce_scatter | solution.py:513
  330.1 107.6 %reduce-scatter.5.cloned.1.call-start = ((), (), s32[]{:S(2)}) async-start(), calls=%async_computation.10 | async-start | bytes 5898240 | tf_op jit(solution)/shard_map/reduce_scatter | solution.py:512
  330.7 86.5 %all-to-all-start.4 = ((bf16[8,256,768]{2,1,0:T(8,128)(2,1)}), bf16[8,256,768]{2,1,0:T(8,128)(2,1)}, u32[]{:S(2)}, u32[]{:S(2)}) async-start(bf16[8,256,768]{2,1,0:T(8,128)(2,1)} %bitcast.221), calls=%async_computation.4 | async-start | bytes 6291456 | tf_op jit(solution)/shard_map/all_to_all | solution.py:351
  340.7 29.7 %collective-permute-start.2 = (bf16[512,768]{1,0:T(8,128)(2,1)S(1)}, bf16[512,768]{1,0:T(8,128)(2,1)}, u32[]{:S(2)}, u32[]{:S(2)}) collective-permute-start(bf16[512,768]{1,0:T(8,128)(2,1)S(1)} %fusion.46), channel_id=1, source_target_pairs={{0,2},{1,3},{2,0},{3,1},{4,6},{5,7},{6,4},{7,5},{8,10},{9,11},{10,... | collective-permute-start | bytes 2359304 | tf_op jit(solution)/shard_map/ppermute | solution.py:358
  372.9 3.8 collective-permute-start.3
  444.7 59.4 %collective-permute-start.4 = (bf16[2,512,768]{2,1,0:T(8,128)(2,1)}, bf16[2,512,768]{2,1,0:T(8,128)(2,1)}, u32[]{:S(2)}, u32[]{:S(2)}) collective-permute-start(bf16[2,512,768]{2,1,0:T(8,128)(2,1)} %dynamic-slice_bitcast_fusion), channel_id=1, source_target_pairs={{0,1},{1,0},{2,3},{3,2},{4,5},{5,4},{6,7},{7,6},{8,9},{9,8},{10,11... | collective-permute-start | bytes 4718600 | tf_op jit(solution)/shard_map/ppermute | solution.py:358
  444.9 3.3 collective-permute-start.6
  448.2 4.0 collective-permute-start.7
  449.3 20.3 %collective-permute-start.17 = (bf16[2,2,48,768]{3,2,1,0:T(8,128)(2,1)}, bf16[2,2,48,768]{3,2,1,0:T(8,128)(2,1)}, u32[]{:S(2)}, u32[]{:S(2)}) collective-permute-start(bf16[2,2,48,768]{3,2,1,0:T(8,128)(2,1)} %dynamic-slice_bitcast_fusion.2), channel_id=1, source_target_pairs={{0,8},{4,12},{8,0},{12,4},{16,24},{20,28},{24,16},{28,20},{1,9},{5... | collective-permute-start | bytes 884744 | tf_op jit(solution)/shard_map/ppermute | solution.py:358
  452.2 4.2 collective-permute-start.8
  454.4 18.1 %collective-permute-start.11 = (bf16[2,2,48,768]{3,2,1,0:T(8,128)(2,1)}, bf16[2,2,48,768]{3,2,1,0:T(8,128)(2,1)}, u32[]{:S(2)}, u32[]{:S(2)}) collective-permute-start(bf16[2,2,48,768]{3,2,1,0:T(8,128)(2,1)} %dynamic-slice_bitcast_fusion.3), channel_id=1, source_target_pairs={{0,4},{4,0},{8,12},{12,8},{16,20},{20,16},{24,28},{28,24},{1,5},{5... | collective-permute-start | bytes 884744 | tf_op jit(solution)/shard_map/ppermute | solution.py:358
  456.4 4.0 collective-permute-start.9
  461.0 5.9 %collective-permute-start.10 = (f32[9216]{0:T(1024)}, f32[9216]{0:T(1024)}, u32[]{:S(2)}, u32[]{:S(2)}) collective-permute-start(f32[9216]{0:T(1024)} %add.231), channel_id=1, source_target_pairs={{0,16},{4,20},{8,24},{12,28},{16,0},{20,4},{24,8},{28,12},{1,17},{... | collective-permute-start | bytes 110600 | tf_op jit(solution)/shard_map/ppermute | solution.py:358
  470.7 7.8 %collective-permute-start.18 = (bf16[2,48,768]{2,1,0:T(8,128)(2,1)S(1)}, bf16[2,48,768]{2,1,0:T(8,128)(2,1)S(1)}, u32[]{:S(2)}, u32[]{:S(2)}) collective-permute-start(bf16[2,48,768]{2,1,0:T(8,128)(2,1)S(1)} %fusion.31), channel_id=1, source_target_pairs={{0,16},{4,20},{8,24},{12,28},{16,0},{20,4},{24,8},{28,12},{1,17},{... | collective-permute-start | bytes 442376 | tf_op jit(solution)/shard_map/ppermute | solution.py:358
  473.5 6.7 %collective-permute-start.12 = (bf16[2,48,768]{2,1,0:T(8,128)(2,1)S(1)}, bf16[2,48,768]{2,1,0:T(8,128)(2,1)S(1)}, u32[]{:S(2)}, u32[]{:S(2)}) collective-permute-start(bf16[2,48,768]{2,1,0:T(8,128)(2,1)S(1)} %fusion.30), channel_id=1, source_target_pairs={{0,8},{4,12},{8,0},{12,4},{16,24},{20,28},{24,16},{28,20},{1,9},{5... | collective-permute-start | bytes 442376 | tf_op jit(solution)/shard_map/ppermute | solution.py:358
  478.6 4.4 collective-permute-start.19
  480.3 8.5 %collective-permute-start.13 = (bf16[48,768]{1,0:T(8,128)(2,1)S(1)}, bf16[48,768]{1,0:T(8,128)(2,1)S(1)}, u32[]{:S(2)}, u32[]{:S(2)}) collective-permute-start(bf16[48,768]{1,0:T(8,128)(2,1)S(1)} %fusion.34), channel_id=1, source_target_pairs={{0,16},{4,20},{8,24},{12,28},{16,0},{20,4},{24,8},{28,12},{1,17},{... | collective-permute-start | bytes 221192 | tf_op jit(solution)/shard_map/ppermute | solution.py:358
  483.0 5.9 %collective-permute-start.20 = (bf16[48,768]{1,0:T(8,128)(2,1)S(1)}, bf16[48,768]{1,0:T(8,128)(2,1)S(1)}, u32[]{:S(2)}, u32[]{:S(2)}) collective-permute-start(bf16[48,768]{1,0:T(8,128)(2,1)S(1)} %fusion.32), channel_id=1, source_target_pairs={{0,4},{4,0},{8,12},{12,8},{16,20},{20,16},{24,28},{28,24},{1,5},{5... | collective-permute-start | bytes 221192 | tf_op jit(solution)/shard_map/ppermute | solution.py:358
  488.8 5.7 %collective-permute-start.14 = (bf16[48,768]{1,0:T(8,128)(2,1)S(1)}, bf16[48,768]{1,0:T(8,128)(2,1)S(1)}, u32[]{:S(2)}, u32[]{:S(2)}) collective-permute-start(bf16[48,768]{1,0:T(8,128)(2,1)S(1)} %fusion.33), channel_id=1, source_target_pairs={{0,16},{4,20},{8,24},{12,28},{16,0},{20,4},{24,8},{28,12},{1,17},{... | collective-permute-start | bytes 221192 | tf_op jit(solution)/shard_map/ppermute | solution.py:358
  488.9 7.7 %collective-permute-start.21 = (bf16[2,48,768]{2,1,0:T(8,128)(2,1)S(1)}, bf16[2,48,768]{2,1,0:T(8,128)(2,1)S(1)}, u32[]{:S(2)}, u32[]{:S(2)}) collective-permute-start(bf16[2,48,768]{2,1,0:T(8,128)(2,1)S(1)} %pad_maximum_fusion.8), channel_id=1, source_target_pairs={{0,16},{4,20},{8,24},{12,28},{16,0},{20,4},{24,8},{28,12},{1,17},{... | collective-permute-start | bytes 442376 | tf_op jit(solution)/shard_map/ppermute | solution.py:358
  494.6 5.6 %collective-permute-start.15 = (bf16[2,48,768]{2,1,0:T(8,128)(2,1)S(1)}, bf16[2,48,768]{2,1,0:T(8,128)(2,1)S(1)}, u32[]{:S(2)}, u32[]{:S(2)}) collective-permute-start(bf16[2,48,768]{2,1,0:T(8,128)(2,1)S(1)} %pad_maximum_fusion.7), channel_id=1, source_target_pairs={{0,8},{4,12},{8,0},{12,4},{16,24},{20,28},{24,16},{28,20},{1,9},{5... | collective-permute-start | bytes 442376 | tf_op jit(solution)/shard_map/ppermute | solution.py:358
  496.7 7.5 %collective-permute-start.22 = (bf16[2,2,48,768]{3,2,1,0:T(8,128)(2,1)S(1)}, bf16[2,2,48,768]{3,2,1,0:T(8,128)(2,1)S(1)}, u32[]{:S(2)}, u32[]{:S(2)}) collective-permute-start(bf16[2,2,48,768]{3,2,1,0:T(8,128)(2,1)S(1)} %pad_maximum_fusion.6), channel_id=1, source_target_pairs={{0,8},{4,12},{8,0},{12,4},{16,24},{20,28},{24,16},{28,20},{1,9},{5... | collective-permute-start | bytes 884744 | tf_op jit(solution)/shard_map/ppermute | solution.py:358
  500.3 6.8 %collective-permute-start.16 = (bf16[2,2,48,768]{3,2,0,1:T(8,128)(2,1)S(1)}, bf16[2,2,48,768]{3,2,0,1:T(8,128)(2,1)S(1)}, u32[]{:S(2)}, u32[]{:S(2)}) collective-permute-start(bf16[2,2,48,768]{3,2,0,1:T(8,128)(2,1)S(1)} %pad_maximum_fusion.5), channel_id=1, source_target_pairs={{0,4},{4,0},{8,12},{12,8},{16,20},{20,16},{24,28},{28,24},{1,5},{5... | collective-permute-start | bytes 884744 | tf_op jit(solution)/shard_map/ppermute | solution.py:358
  506.0 15.8 %collective-permute-start.5 = (bf16[512,768]{1,0:T(8,128)(2,1)S(1)}, bf16[512,768]{1,0:T(8,128)(2,1)S(1)}, u32[]{:S(2)}, u32[]{:S(2)}) collective-permute-start(bf16[512,768]{1,0:T(8,128)(2,1)S(1)} %fusion.27), channel_id=1, source_target_pairs={{0,2},{1,3},{2,0},{3,1},{4,6},{5,7},{6,4},{7,5},{8,10},{9,11},{10,... | collective-permute-start | bytes 2359304 | tf_op jit(solution)/shard_map/ppermute | solution.py:358
  (43 other events, 612.4 us)
Sparse Core Ops, SparseCore 0:
  9.6 40.1 all-gather.2
  113.2 38.7 all-gather.4
  330.2 55.9 reduce-scatter.2
  388.7 48.9 reduce-scatter.4

commit v4 on v3

--- a/solution.py
+++ b/solution.py
@@ -12,6 +12,8 @@
 EPSILON = 1e-06
 BLOCKED = -1e30
 VMEM_LIMIT = 48 * 2**20
+LANES = 128
+SPARE = 16
 
 
 def mul(left, right, left_dim, right_dim):
@@ -56,7 +58,7 @@
 
 
 def forward_kernel(
-    lengths_ref, tokens_ref, gain_ref, qkv_ref, out_ref, bias_ref,
+    place_ref, lengths_ref, tokens_ref, gain_ref, qkv_ref, out_ref, bias_ref,
     branch_ref, proj_ref, mixed_ref, log_ref,
     keys_ref, values_ref, spread_ref,
     *, head_count, head_dim, slots,
@@ -113,11 +115,11 @@
 
 
 def backward_kernel(
-    lengths_ref, tokens_ref, gain_ref, qkv_ref, out_ref, bias_ref,
-    proj_ref, before_ref, mixed_ref, log_ref, grad_ref,
+    place_ref, lengths_ref, tokens_ref, gain_ref, qkv_ref, out_ref, bias_ref,
+    proj_ref, before_ref, mixed_ref, log_ref, near_grad_ref, away_grad_ref,
     part_ref, qkv_grad_ref, out_grad_ref, gain_grad_ref, bias_grad_ref, far_grad_ref,
     spread_ref, near_ref, far_ref, carry_ref, pieces_ref,
-    *, head_count, head_dim, slots, block_count,
+    *, head_count, head_dim, slots, block_count, placed,
 ):
     step = pl.program_id(0)
     block_index = block_count - 1 - step
@@ -139,7 +141,8 @@
         carry_ref[:, BLOCK:] = carry_ref[:, :BLOCK]
         carry_ref[:, :BLOCK] = jnp.zeros_like(carry_ref[:, :BLOCK])
 
-    grad_branch = grad_ref[...]
+    close = placed(block_index, place_ref) < block_count // 2
+    grad_branch = jnp.where(close, near_grad_ref[0], away_grad_ref[0])
     out_grad_ref[...] += mul(mixed_ref[...], grad_branch, 1, 0)
     grad_mixed = mul(out_ref[...], grad_branch, 1, 1).astype(jnp.bfloat16)
     scale = head_dim**-0.5
@@ -199,7 +202,14 @@
 
 
 def whole(shape):
-    return pl.BlockSpec(shape, lambda step: (0,) * len(shape))
+    return pl.BlockSpec(shape, lambda *steps: (0,) * len(shape))
+
+
+def reversed_bits(value, count):
+    result = value * 0
+    for bit in range(count):
+        result = result + ((value >> bit) & 1) * 2 ** (count - 1 - bit)
+    return result
 
 
 def bias_line(rel_bias):
@@ -216,42 +226,50 @@
     return jnp.concatenate([line, jnp.zeros((8 - head_count, 2 * HALF), jnp.float32)], axis=0)
 
 
-def attend(tokens, lengths, gain, qkv_flat, attn_out, rel_bias):
+def attend(place, tokens, lengths, gain, qkv_flat, attn_out, rel_bias):
     rows, width = tokens.shape
     inner = attn_out.shape[0]
     head_count = rel_bias.shape[0]
     head_dim = inner // head_count
     block_count = rows // BLOCK
+    bits = (block_count - 1).bit_length()
+
+    def placed(block, at):
+        return reversed_bits(block ^ at[0], bits)
+
     return pl.pallas_call(
         functools.partial(
             forward_kernel, head_count=head_count, head_dim=head_dim, slots=lengths.shape[1]
         ),
-        grid=(block_count,),
-        in_specs=[
-            pl.BlockSpec(memory_space=pltpu.SMEM),
-            pl.BlockSpec((BLOCK, width), lambda step: (step, 0)),
-            whole((1, width)),
-            whole(qkv_flat.shape),
-            whole(attn_out.shape),
-            whole((8, 2 * HALF)),
-        ],
-        out_specs=[
-            pl.BlockSpec((BLOCK, width), lambda step: (step, 0)),
-            pl.BlockSpec((3 * inner, BLOCK), lambda step: (0, step)),
-            pl.BlockSpec((inner, BLOCK), lambda step: (0, step)),
-            pl.BlockSpec((8, BLOCK), lambda step: (0, step)),
-        ],
+        grid_spec=pltpu.PrefetchScalarGridSpec(
+            num_scalar_prefetch=1,
+            grid=(block_count,),
+            in_specs=[
+                pl.BlockSpec(memory_space=pltpu.SMEM),
+                pl.BlockSpec((BLOCK, width), lambda step, at: (step, 0)),
+                whole((1, width)),
+                whole(qkv_flat.shape),
+                whole(attn_out.shape),
+                whole((8, 2 * HALF)),
+            ],
+            out_specs=[
+                pl.BlockSpec((BLOCK, width), lambda step, at: (placed(step, at), 0)),
+                pl.BlockSpec((3 * inner, BLOCK), lambda step, at: (0, step)),
+                pl.BlockSpec((inner, BLOCK), lambda step, at: (0, step)),
+                pl.BlockSpec((8, BLOCK), lambda step, at: (0, step)),
+            ],
+            scratch_shapes=[
+                pltpu.VMEM((head_count, 2 * BLOCK, head_dim), jnp.bfloat16),
+                pltpu.VMEM((inner, 2 * BLOCK), jnp.bfloat16),
+                pltpu.VMEM((head_count, 2 * HALF, HALF), jnp.float32),
+            ],
+        ),
         out_shape=[
             jax.ShapeDtypeStruct((rows, width), jnp.bfloat16),
             jax.ShapeDtypeStruct((3 * inner, rows), jnp.bfloat16),
             jax.ShapeDtypeStruct((inner, rows), jnp.bfloat16),
             jax.ShapeDtypeStruct((8, rows), jnp.float32),
         ],
-        scratch_shapes=[
-            pltpu.VMEM((head_count, 2 * BLOCK, head_dim), jnp.bfloat16),
-            pltpu.VMEM((inner, 2 * BLOCK), jnp.bfloat16),
-            pltpu.VMEM((head_count, 2 * HALF, HALF), jnp.float32),
-        ],
         compiler_params=pltpu.CompilerParams(vmem_limit_bytes=VMEM_LIMIT),
         cost_estimate=pl.CostEstimate(
             flops=2 * rows * width * inner * 4 + 4 * rows * 768 * inner,
@@ -259,11 +277,12 @@
             transcendentals=rows * 768 * head_count,
         ),
         name="attend_forward",
-    )(lengths, tokens, gain[None, :], qkv_flat, attn_out, bias_line(rel_bias))
+    )(place, lengths, tokens, gain[None, :], qkv_flat, attn_out, bias_line(rel_bias))
 
 
 def attend_back(
-    tokens, lengths, gain, qkv_flat, attn_out, rel_bias, projected, mixed, log_total, grad_branch
+    place, tokens, lengths, gain, qkv_flat, attn_out, rel_bias, projected, mixed, log_total, near_grad,
+    away_grad,
 ):
     rows, width = tokens.shape
     inner = attn_out.shape[0]
@@ -271,6 +290,11 @@
     head_dim = inner // head_count
     block_count = rows // BLOCK
     last = block_count - 1
+    bits = last.bit_length()
+
+    def placed(block, at):
+        return reversed_bits(block ^ at[0], bits)
+
     part, qkv_grad, out_grad, gain_grad, bias_grad, far_grad = pl.pallas_call(
         functools.partial(
             backward_kernel,
@@ -278,29 +302,53 @@
             head_dim=head_dim,
             slots=lengths.shape[1],
             block_count=block_count,
-        ),
-        grid=(block_count,),
-        in_specs=[
-            pl.BlockSpec(memory_space=pltpu.SMEM),
-            pl.BlockSpec((BLOCK, width), lambda step: (last - step, 0)),
-            whole((1, width)),
-            whole(qkv_flat.shape),
-            whole(attn_out.shape),
-            whole((8, 2 * HALF)),
-            pl.BlockSpec((3 * inner, BLOCK), lambda step: (0, last - step)),
-            pl.BlockSpec((3 * inner, BLOCK), lambda step: (0, jnp.maximum(last - step - 1, 0))),
-            pl.BlockSpec((inner, BLOCK), lambda step: (0, last - step)),
-            pl.BlockSpec((8, BLOCK), lambda step: (0, last - step)),
-            pl.BlockSpec((BLOCK, width), lambda step: (last - step, 0)),
-        ],
-        out_specs=[
-            pl.BlockSpec((BLOCK, width), lambda step: (last - step, 0)),
-            whole((3 * inner, width)),
-            whole((inner, width)),
-            whole((8, width)),
-            whole((8, 2 * HALF)),
-            whole((8, HALF)),
-        ],
+            placed=placed,
+        ),
+        grid_spec=pltpu.PrefetchScalarGridSpec(
+            num_scalar_prefetch=1,
+            grid=(block_count,),
+            in_specs=[
+                pl.BlockSpec(memory_space=pltpu.SMEM),
+                pl.BlockSpec((BLOCK, width), lambda step, at: (last - step, 0)),
+                whole((1, width)),
+                whole(qkv_flat.shape),
+                whole(attn_out.shape),
+                whole((8, 2 * HALF)),
+                pl.BlockSpec((3 * inner, BLOCK), lambda step, at: (0, last - step)),
+                pl.BlockSpec(
+                    (3 * inner, BLOCK), lambda step, at: (0, jnp.maximum(last - step - 1, 0))
+                ),
+                pl.BlockSpec((inner, BLOCK), lambda step, at: (0, last - step)),
+                pl.BlockSpec((8, BLOCK), lambda step, at: (0, last - step)),
+                pl.BlockSpec(
+                    (1, BLOCK, width),
+                    lambda step, at: (
+                        jnp.minimum(placed(last - step, at), block_count // 2 - 1), 0, 0
+                    ),
+                ),
+                pl.BlockSpec(
+                    (1, BLOCK, width),
+                    lambda step, at: (
+                        jnp.maximum(placed(last - step, at) - block_count // 2, 0), 0, 0
+                    ),
+                ),
+            ],
+            out_specs=[
+                pl.BlockSpec((BLOCK, width), lambda step, at: (last - step, 0)),
+                whole((3 * inner, width)),
+                whole((inner, width)),
+                whole((8, width)),
+                whole((8, 2 * HALF)),
+                whole((8, HALF)),
+            ],
+            scratch_shapes=[
+                pltpu.VMEM((head_count, 2 * HALF, HALF), jnp.float32),
+                pltpu.VMEM((head_count, 2 * HALF, HALF), jnp.float32),
+                pltpu.VMEM((8, HALF), jnp.float32),
+                pltpu.VMEM((2 * inner, 2 * BLOCK), jnp.float32),
+                pltpu.VMEM((3 * inner, BLOCK), jnp.bfloat16),
+            ],
+        ),
         out_shape=[
             jax.ShapeDtypeStruct((rows, width), jnp.bfloat16),
             jax.ShapeDtypeStruct((3 * inner, width), jnp.float32),
@@ -309,13 +357,6 @@
             jax.ShapeDtypeStruct((8, 2 * HALF), jnp.float32),
             jax.ShapeDtypeStruct((8, HALF), jnp.float32),
         ],
-        scratch_shapes=[
-            pltpu.VMEM((head_count, 2 * HALF, HALF), jnp.float32),
-            pltpu.VMEM((head_count, 2 * HALF, HALF), jnp.float32),
-            pltpu.VMEM((8, HALF), jnp.float32),
-            pltpu.VMEM((2 * inner, 2 * BLOCK), jnp.float32),
-            pltpu.VMEM((3 * inner, BLOCK), jnp.bfloat16),
-        ],
         compiler_params=pltpu.CompilerParams(vmem_limit_bytes=VMEM_LIMIT),
         cost_estimate=pl.CostEstimate(
             flops=2 * rows * width * inner * 8 + 10 * rows * 768 * inner,
@@ -324,8 +365,8 @@
         ),
         name="attend_backward",
     )(
-        lengths, tokens, gain[None, :], qkv_flat, attn_out, bias_line(rel_bias),
-        projected, projected, mixed, log_total, grad_branch,
+        place, lengths, tokens, gain[None, :], qkv_flat, attn_out, bias_line(rel_bias),
+        projected, projected, mixed, log_total, near_grad, away_grad,
     )
     near_grad = bias_grad[:head_count, HALF : HALF + bucket_count - 1]
     rest = jnp.sum(bias_grad[:head_count], axis=1) - jnp.sum(near_grad, axis=1)
@@ -334,23 +375,275 @@
     return part, qkv_grad, out_grad, jnp.sum(gain_grad, axis=0), bias_part
 
 
+GELU_ONE = 0.7978845608028654
+GELU_TWO = 0.044715
+
+
+def shard_at(place_ref, position, shards):
+    offset = 0
+    bits = (shards - 1).bit_length()
+    for bit in range(bits):
+        offset += ((position >> bit) & 1) * 2 ** (bits - 1 - bit)
+    return place_ref[0] ^ offset
+
+
+def expert_kernel(
+    place_ref, rows_ref, grads_ref, gap_ref, weights_ref, router_ref, *rest, sub
+):
+    sent_ref, act_ref, pre_ref, logit_ref = rest[-4:]
+    shards = weights_ref.shape[0]
+    sources, slots, width = rows_ref.shape
+    step = max(1, sub // slots)
+
+    @pl.loop(0, sources // step)
+    def _(index):
+        part = pl.ds(index * step, step)
+        rows = rows_ref[part].reshape(step * slots, width)
+        gap = gap_ref[part, 0].reshape(step * slots, gap_ref.shape[3]).astype(jnp.float32)
+        logits = mul(rows, router_ref[...], 1, 0)
+        logit_gap = jnp.sum(gap * logits, axis=-1, keepdims=True)
+        gate = 1.0 / (1.0 + jnp.exp(-logit_gap))
+        other_gate = 1.0 / (1.0 + jnp.exp(logit_gap))
+        sent = jnp.zeros((step * slots, width), jnp.float32)
+        gate_grads = jnp.zeros((step * slots, 1), jnp.float32)
+        for shard in range(shards):
+            weights = weights_ref[shard_at(place_ref, shard, shards)]
+            pre = mul(rows, weights, 1, 0)
+            grads = grads_ref[shard, part, 0].reshape(step * slots, weights.shape[1])
+            grads = grads.astype(jnp.float32)
+            square = pre * pre
+            bent = jnp.tanh(pre * (GELU_ONE + GELU_ONE * GELU_TWO * square))
+            share = 0.5 + 0.5 * bent
+            act = pre * share
+            slope = share + act * (1.0 - share) * (
+                2.0 * GELU_ONE + 6.0 * GELU_ONE * GELU_TWO * square
+            )
+            gate_grads += jnp.sum(act * grads, axis=-1, keepdims=True)
+            act_ref[shard, part, 0] = (
+                (gate * act).astype(jnp.bfloat16).reshape(step, slots, weights.shape[1])
+            )
+            grad_pre = (gate * grads * slope).astype(jnp.bfloat16)
+            pre_ref[shard, part, 0] = grad_pre.reshape(step, slots, weights.shape[1])
+            sent += mul(grad_pre, weights, 1, 1)
+        logit_grads = (gate * other_gate * gate_grads * gap).astype(jnp.bfloat16)
+        logit_ref[part, 0] = logit_grads.reshape(step, slots, gap.shape[1])
+        sent += mul(logit_grads, router_ref[...], 1, 1)
+        sent_ref[part] = sent.astype(jnp.bfloat16).reshape(step, slots, width)
+
+
+def serve(place, rows, act_grads, hot_gap, weights_in, router_wide, which, before, sub=256, tile=512):
+    sources, slots, width = rows.shape
+    shards = weights_in.shape[0]
+    hidden = weights_in.shape[2]
+    group = min(sources, max(1, tile // slots))
+    wide = pl.BlockSpec((shards, group, 1, slots, hidden), lambda step, at: (0, step, which, 0, 0))
+    lanes = pl.BlockSpec((group, 1, slots, hot_gap.shape[3]), lambda step, at: (step, which, 0, 0))
+    narrow = pl.BlockSpec((group, slots, width), lambda step, at: (step, 0, 0))
+    kept = [] if before is None else list(before)
+    return pl.pallas_call(
+        functools.partial(expert_kernel, sub=sub),
+        grid_spec=pltpu.PrefetchScalarGridSpec(
+            num_scalar_prefetch=1,
+            grid=(sources // group,),
+            in_specs=[narrow, wide, lanes, whole(weights_in.shape), whole(router_wide.shape)]
+            + [pl.BlockSpec(memory_space=pl.ANY)] * len(kept),
+            out_specs=[narrow, wide, wide, lanes],
+        ),
+        out_shape=[
+            jax.ShapeDtypeStruct(rows.shape, jnp.bfloat16),
+            jax.ShapeDtypeStruct(act_grads.shape, jnp.bfloat16),
+            jax.ShapeDtypeStruct(act_grads.shape, jnp.bfloat16),
+            jax.ShapeDtypeStruct(hot_gap.shape, jnp.bfloat16),
+        ],
+        input_output_aliases={6 + index: 1 + index for index in range(len(kept))},
+        compiler_params=pltpu.CompilerParams(vmem_limit_bytes=VMEM_LIMIT),
+        cost_estimate=pl.CostEstimate(
+            flops=4 * sources * slots * width * shards * hidden,
+            bytes_accessed=6 * sources * slots * shards * hidden,
+            transcendentals=sources * slots * shards * hidden,
+        ),
+        name="expert_middle",
+    )(place, rows, act_grads, hot_gap, weights_in, router_wide, *kept)
+
+
+def act_grads_kernel(place_ref, rows_ref, weights_ref, out_ref):
+    shards = weights_ref.shape[0]
+    rows = rows_ref[...].reshape(-1, rows_ref.shape[2])
+    for shard in range(shards):
+        out_ref[shard] = mul(rows, weights_ref[shard_at(place_ref, shard, shards)], 1, 1).astype(
+            jnp.bfloat16
+        )
+
+
+def slot_group(sources, capacity):
+    return min(sources, max(1, BLOCK // capacity))
+
+
+def act_grads_of(place, landed, weights, capacity):
+    sources, _, width = landed.shape
+    shards, hidden, _ = weights.shape
+    group = slot_group(sources, capacity)
+    tile = group * capacity
+    return pl.pallas_call(
+        act_grads_kernel,
+        grid_spec=pltpu.PrefetchScalarGridSpec(
+            num_scalar_prefetch=1,
+            grid=(sources // group,),
+            in_specs=[
+                pl.BlockSpec((group, capacity, width), lambda step, at: (step, 0, 0)),
+                whole(weights.shape),
+            ],
+            out_specs=pl.BlockSpec((shards, tile, hidden), lambda step, at: (0, step, 0)),
+        ),
+        out_shape=jax.ShapeDtypeStruct((shards, sources * capacity, hidden), jnp.bfloat16),
+        compiler_params=pltpu.CompilerParams(vmem_limit_bytes=VMEM_LIMIT),
+        cost_estimate=pl.CostEstimate(
+            flops=2 * sources * capacity * width * shards * hidden,
+            bytes_accessed=2 * sources * capacity * shards * hidden,
+            transcendentals=0,
+        ),
+        name="act_grads",
+    )(place, landed, weights)
+
+
+def result_kernel(place_ref, act_ref, weights_ref, out_ref):
+    shards = weights_ref.shape[0]
+    total = mul(act_ref[0], weights_ref[shard_at(place_ref, 0, shards)], 1, 0)
+    for shard in range(1, shards):
+        total += mul(act_ref[shard], weights_ref[shard_at(place_ref, shard, shards)], 1, 0)
+    out_ref[...] = total.astype(jnp.bfloat16)
+
+
+def result_of(place, act, weights):
+    shards, rows, hidden = act.shape
+    width = weights.shape[2]
+    return pl.pallas_call(
+        result_kernel,
+        grid_spec=pltpu.PrefetchScalarGridSpec(
+            num_scalar_prefetch=1,
+            grid=(rows // BLOCK,),
+            in_specs=[
+                pl.BlockSpec((shards, BLOCK, hidden), lambda step, at: (0, step, 0)),
+                whole(weights.shape),
+            ],
+            out_specs=pl.BlockSpec((BLOCK, width), lambda step, at: (step, 0)),
+        ),
+        out_shape=jax.ShapeDtypeStruct((rows, width), jnp.bfloat16),
+        compiler_params=pltpu.CompilerParams(vmem_limit_bytes=VMEM_LIMIT),
+        cost_estimate=pl.CostEstimate(
+            flops=2 * rows * width * shards * hidden,
+            bytes_accessed=2 * rows * shards * hidden,
+            transcendentals=0,
+        ),
+        name="expert_result",
+    )(place, act, weights)
+
+
+def out_weights_kernel(act_ref, landed_ref, out_ref):
+    capacity = act_ref.shape[1] // landed_ref.shape[0]
+    rows = landed_ref[:, :capacity].reshape(act_ref.shape[1], landed_ref.shape[2])
+    out_ref[0] = mul(act_ref[0], rows, 0, 0).astype(jnp.bfloat16)
+
+
+def out_weights_of(act, landed):
+    shards, rows, hidden = act.shape
+    width = landed.shape[2]
+    return pl.pallas_call(
+        out_weights_kernel,
+        grid=(shards,),
+        in_specs=[
+            pl.BlockSpec((1, rows, hidden), lambda step: (step, 0, 0)),
+            whole(landed.shape),
+        ],
+        out_specs=pl.BlockSpec((1, hidden, width), lambda step: (step, 0, 0)),
+        out_shape=jax.ShapeDtypeStruct((shards, hidden, width), jnp.bfloat16),
+        compiler_params=pltpu.CompilerParams(vmem_limit_bytes=VMEM_LIMIT),
+        cost_estimate=pl.CostEstimate(
+            flops=2 * rows * width * shards * hidden,
+            bytes_accessed=2 * rows * shards * hidden,
+            transcendentals=0,
+        ),
+        name="out_weights",
+    )(act, landed)
+
+
+def in_weights_kernel(first_ref, last_ref, grads_ref, logits_ref, out_ref, router_ref):
+    sources, slots, width = first_ref.shape
+    first = first_ref[...].reshape(sources * slots, width)
+    last = last_ref[...].reshape(sources * slots, width)
+    hidden = grads_ref.shape[4]
+    out_ref[0] = (
+        mul(first, grads_ref[0, :, 0].reshape(sources * slots, hidden), 0, 0)
+        + mul(last, grads_ref[0, :, 1].reshape(sources * slots, hidden), 0, 0)
+    ).astype(jnp.bfloat16)
+
+    @pl.when(pl.program_id(0) == 0)
+    def _():
+        lanes = logits_ref.shape[3]
+        router_ref[...] = mul(
+            first, logits_ref[:, 0].reshape(sources * slots, lanes), 0, 0
+        ) + mul(last, logits_ref[:, 1].reshape(sources * slots, lanes), 0, 0)
+
+
+def in_weights_of(first, last, grads, logit_grads):
+    shards, sources, _, slots, hidden = grads.shape
+    width = first.shape[2]
+    lanes = logit_grads.shape[3]
+    return pl.pallas_call(
+        in_weights_kernel,
+        grid=(shards,),
+        in_specs=[
+            whole(first.shape),
+            whole(last.shape),
+            pl.BlockSpec((1,) + grads.shape[1:], lambda step: (step, 0, 0, 0, 0)),
+            whole(logit_grads.shape),
+        ],
+        out_specs=[
+            pl.BlockSpec((1, width, hidden), lambda step: (step, 0, 0)),
+            whole((width, lanes)),
+        ],
+        out_shape=[
+            jax.ShapeDtypeStruct((shards, width, hidden), jnp.bfloat16),
+            jax.ShapeDtypeStruct((width, lanes), jnp.float32),
+        ],
+        compiler_params=pltpu.CompilerParams(vmem_limit_bytes=VMEM_LIMIT),
+        cost_estimate=pl.CostEstimate(
+            flops=4 * sources * slots * width * shards * hidden,
+            bytes_accessed=4 * sources * slots * shards * hidden,
+            transcendentals=0,
+        ),
+        name="in_weights",
+    )(first, last, grads, logit_grads)
+
+
 def rms_norm(values, gain):
     return values * lax.rsqrt(jnp.mean(values * values, axis=-1, keepdims=True) + EPSILON) * gain
 
 
-def gelu_tanh(values):
-    return (
-        0.5
-        * values
-        * (1.0 + jnp.tanh(0.7978845608028654 * (values + 0.044715 * values * values * values)))
-    )
-
-
-def exchange(rows):
-    parts = lax.axis_size("expert")
-    return lax.all_to_all(
-        rows.reshape((parts, -1) + rows.shape[1:]), "expert", split_axis=0, concat_axis=0, tiled=True
-    ).reshape(rows.shape)
+def exchange(pieces):
+    return lax.all_to_all(pieces, "expert", split_axis=0, concat_axis=0, tiled=True)
+
+
+def halved(pieces, axis_name, bit):
+    half = pieces.shape[0] // 2
+    return pieces[:half], swap(pieces[half:].astype(jnp.bfloat16), axis_name, bit)
+
+
+def joined(keep, got):
+    return keep.astype(jnp.float32) + got.astype(jnp.float32)
+
+
+def spread_sum(pieces, axis_name):
+    for bit in range(bit_count(axis_name)):
+        pieces = joined(*halved(pieces, axis_name, bit))
+    return pieces[0]
+
+
+def collect(piece, axis_name):
+    pieces = piece[None]
+    for bit in reversed(range(1, bit_count(axis_name))):
+        pieces = jnp.concatenate([pieces, swap(pieces, axis_name, bit)], axis=0)
+    return pieces, swap(pieces, axis_name, 0)
 
 
 def swap(value, axis_name, bit):
@@ -363,8 +656,11 @@
 
 
 def scatter_sum(pieces, axis_name, order):
+    count = (pieces.shape[0] - 1).bit_length()
     bits = sorted(order, reverse=True)
-    total = pieces.reshape((2,) * len(bits) + pieces.shape[1:])
+    if count > len(bits):
+        bits = list(range(count))[::-1]
+    total = pieces.reshape((2,) * count + pieces.shape[1:])
     for bit in order:
         dim = bits.index(bit)
         bits.remove(bit)
@@ -376,18 +672,16 @@
     return total
 
 
-def gather(piece, axis_name, order):
-    bits = []
-    whole_value = piece
+def gather(value, axis_name, order, done=()):
+    bits = list(done)
     for bit in order:
+        value = value.reshape((2,) * len(bits) + value.shape[value.ndim - 2 :])
         bits = sorted(bits + [bit], reverse=True)
         dim = bits.index(bit)
-        got = swap(whole_value, axis_name, bit)
+        got = swap(value, axis_name, bit)
         first = own_bit(axis_name, bit) == 0
-        whole_value = jnp.stack(
-            [jnp.where(first, whole_value, got), jnp.where(first, got, whole_value)], axis=dim
-        )
-    return whole_value.reshape((-1,) + piece.shape[1:])
+        value = jnp.stack([jnp.where(first, value, got), jnp.where(first, got, value)], axis=dim)
+    return value
 
 
 def butterfly(value, axis_name):
@@ -400,16 +694,23 @@
     return (lax.axis_size(axis_name) - 1).bit_length()
 
 
-def sum_rows(rows, axis_name):
+def scatter_rows(rows, axis_name):
     bits = list(range(bit_count(axis_name)))
     parts = lax.axis_size(axis_name)
-    results = []
-    for half, turn in zip(jnp.split(rows, 2, axis=0), (0, 1)):
-        order = bits[turn:] + bits[:turn]
-        pieces = half.reshape((parts, -1) + rows.shape[1:])
-        own = scatter_sum(pieces, axis_name, order).astype(jnp.bfloat16)
-        results.append(gather(own, axis_name, order[::-1]))
-    return jnp.concatenate(results, axis=0)
+    orders = [bits[turn:] + bits[:turn] for turn in (0, 1)]
+    owned = [
+        scatter_sum(half.reshape((parts, -1) + rows.shape[1:]), axis_name, order).astype(jnp.bfloat16)
+        for half, order in zip(jnp.split(rows, 2, axis=0), orders)
+    ]
+    return owned, orders
+
+
+def gather_rows(begun, orders, axis_name):
+    halves = [
+        gather(part, axis_name, order[::-1][1:], order[::-1][:1])
+        for part, order in zip(begun, orders)
+    ]
+    return jnp.concatenate([half.reshape(-1, half.shape[-1]) for half in halves], axis=0)
 
 
 def local(
@@ -439,95 +740,110 @@
     counts = jnp.sum(route_hot, axis=1)
     before = jnp.cumsum(counts, axis=0) - counts
     slot_rank = jnp.sum(route_hot * before[:, None, :], axis=-1)
+    expert_index = lax.axis_index("expert")
     slot_index = routes * capacity + slot_rank
+    half_slots = capacity // 2
+
+    def named(slot_ids):
+        match = slot_index[:, :, None] == slot_ids[None, None, :]
+        return (match[:, 0] | match[:, 1]).astype(jnp.bfloat16)
+
     slot_ids = jnp.arange(expert_count * capacity, dtype=jnp.int32)
-    slot_match = slot_index[:, :, None] == slot_ids[None, None, :]
-    dispatch = (slot_match[:, 0] | slot_match[:, 1]).astype(jnp.bfloat16)
-    other_ids = jnp.sum(jnp.where(slot_match, routes[:, ::-1, None] + 1, 0), axis=(0, 1))
-    grad_slots = mul(dispatch, out_grad, 0, 0).astype(jnp.bfloat16)
-    grad_rows = exchange(grad_slots)
+    split_ids = slot_ids.reshape(expert_count, 2, half_slots)
+    extra = jnp.full((expert_count, SPARE), -1, jnp.int32)
+    long_ids = jnp.concatenate([slot_ids.reshape(expert_count, capacity), extra], axis=1)
+    grad_slots = mul(named(long_ids.reshape(-1)), out_grad, 0, 0).astype(jnp.bfloat16)
+    other_ids = jnp.sum(
+        jnp.where(
+            slot_index[:, :, None] == slot_ids[None, None, :], routes[:, ::-1, None] + 1, 0
+        ),
+        axis=(0, 1),
+    ).astype(jnp.bfloat16)
+    grad_slots = lax.dynamic_update_slice(
+        grad_slots.reshape(expert_count, capacity + SPARE, width),
+        other_ids.reshape(expert_count, 1, capacity),
+        (0, capacity, 0),
+    )
+    landed = exchange(grad_slots)
     tokens, _ = lax.optimization_barrier((tokens, grad_slots))
-    tensor_bits = list(range(bit_count("tensor")))
+    place = tensor_index.astype(jnp.int32)[None]
+    halves = [named(split_ids[:, which].reshape(-1)) for which in range(2)]
+    dispatch = named(slot_ids)
 
     qkv_flat = attn_qkv.transpose(1, 2, 0).reshape(3 * inner, width)
     branch, projected, mixed, log_total = attend(
-        tokens, lengths, norm1_gain, qkv_flat, attn_out, rel_bias
-    )
-    branch = scatter_sum(branch.reshape(n_tensor, own_rows, width), "tensor", tensor_bits)
+        place, tokens, lengths, norm1_gain, qkv_flat, attn_out, rel_bias
+    )
+    branch = spread_sum(branch.reshape(n_tensor, own_rows, width), "tensor")
     own_tokens = lax.dynamic_slice_in_dim(tokens, tensor_index * own_rows, own_rows, 0)
     resid = own_tokens.astype(jnp.float32) + branch
     normed_two, norm2_pull = jax.vjp(rms_norm, resid, norm2_gain)
     hidden_two = normed_two.astype(jnp.bfloat16)
-    outgoing = mul(dispatch, hidden_two, 0, 0).astype(jnp.bfloat16)
-    outgoing, other_ids, grad_rows = lax.optimization_barrier((outgoing, other_ids, grad_rows))
-    expert_rows = exchange(outgoing)
-    other_here = exchange(other_ids)
+    outgoing = [mul(half, hidden_two, 0, 0).astype(jnp.bfloat16) for half in halves]
+    outgoing, landed, expert_in = lax.optimization_barrier((outgoing, landed, expert_in))
+    outgoing = [rows.reshape(expert_count, half_slots, width) for rows in outgoing]
+    first_rows = exchange(outgoing[0])
+    other_here = landed[:, capacity, :capacity].reshape(-1).astype(jnp.int32)
+    weights_out = lax.all_gather(expert_out[0], "tensor")
     weights_in = lax.all_gather(expert_in[0], "tensor")
-    weights_out = lax.all_gather(expert_out[0], "tensor")
-
-    pre = jnp.einsum("sd,jdf->jsf", expert_rows, weights_in, preferred_element_type=jnp.float32)
-    act_value, gelu_pull = jax.vjp(gelu_tanh, pre)
-    act = act_value.astype(jnp.bfloat16)
-    slot_logits = jnp.dot(expert_rows, router, preferred_element_type=jnp.float32)
-    own_hot = (jnp.arange(expert_count, dtype=jnp.int32) == lax.axis_index("expert")).astype(
-        jnp.float32
-    )
-    other_hot = (other_here[:, None] == jnp.arange(1, expert_count + 1, dtype=jnp.int32)).astype(
-        jnp.float32
-    )
-    hot_gap = own_hot[None, :] - other_hot
-    logit_gap = jnp.sum(hot_gap * slot_logits, axis=-1, keepdims=True)
-    gate = 1.0 / (1.0 + jnp.exp(-logit_gap))
-    other_gate = 1.0 / (1.0 + jnp.exp(logit_gap))
-    act_grads = jnp.einsum("sd,jfd->jsf", grad_rows, weights_out, preferred_element_type=jnp.float32)
-    gate_grads = jnp.sum(act_value * act_grads, axis=(0, 2))[:, None]
-    grad_logits = (gate * other_gate * gate_grads * hot_gap).astype(jnp.bfloat16)
-    grad_pre = gelu_pull(gate[None] * act_grads)[0].astype(jnp.bfloat16)
-    grad_sent = exchange(
-        (
-            jnp.einsum("jsf,jdf->sd", grad_pre, weights_in, preferred_element_type=jnp.float32)
-            + mul(grad_logits, router, 1, 1)
-        ).astype(jnp.bfloat16)
-    )
-    result = (
-        gate * jnp.einsum("jsf,jfd->sd", act, weights_out, preferred_element_type=jnp.float32)
+    act_grads = act_grads_of(place, landed, weights_out, capacity)
+    shards, _, hidden = act_grads.shape
+    act_grads = act_grads.reshape(shards, expert_count, 2, half_slots, hidden)
+    lanes = jnp.arange(LANES, dtype=jnp.int32)
+    hot_gap = (
+        (lanes == expert_index).astype(jnp.int32)[None, :]
+        - (other_here[:, None] == lanes[None, :] + 1).astype(jnp.int32)
     ).astype(jnp.bfloat16)
-    router_part = mul(expert_rows, grad_logits, 0, 0)
-    gated_rows = (gate * grad_rows.astype(jnp.float32)).astype(jnp.bfloat16)
-    grad_w_out = jnp.einsum(
-        "jsf,sd->jfd", act, gated_rows, preferred_element_type=jnp.float32
-    ).astype(jnp.bfloat16)
-    grad_w_in = jnp.einsum(
-        "sd,jsf->jdf", expert_rows, grad_pre, preferred_element_type=jnp.float32
-    ).astype(jnp.bfloat16)
-    grad_sent, result, grad_w_in, grad_w_out = lax.optimization_barrier(
-        (grad_sent, result, grad_w_in, grad_w_out)
-    )
-    came_back = exchange(result)
+    hot_gap = hot_gap.reshape(expert_count, 2, half_slots, LANES)
+    router_wide = jnp.pad(router, ((0, 0), (0, LANES - expert_count)))
+    first_rows, act_grads, hot_gap, weights_in, last = lax.optimization_barrier(
+        (first_rows, act_grads, hot_gap, weights_in, outgoing[1])
+    )
+    last_rows = exchange(last)
+    sent_one, *kept = serve(place, first_rows, act_grads, hot_gap, weights_in, router_wide, 0, None)
+    grad_sent_one = exchange(sent_one)
+    sent_two, act, grad_pre, logit_grads = serve(
+        place, last_rows, act_grads, hot_gap, weights_in, router_wide, 1, kept
+    )
+    act = act.reshape(shards, -1, hidden)
+    grad_w_out = out_weights_of(act, landed)
+    sent_two, grad_w_out, grad_pre = lax.optimization_barrier((sent_two, grad_w_out, grad_pre))
+    grad_sent_two = exchange(sent_two)
+    grad_w_out = spread_sum(grad_w_out, "tensor")
+    grad_w_in, router_part = in_weights_of(first_rows, last_rows, grad_pre, logit_grads)
+    router_part = router_part[:, :expert_count]
+    act, grad_w_in = lax.optimization_barrier((act, grad_w_in))
+    result = result_of(place, act, weights_out)
+    grad_sent_one, grad_sent_two, result, dispatch, grad_w_out = lax.optimization_barrier(
+        (grad_sent_one, grad_sent_two, result, dispatch, grad_w_out)
+    )
     grad_in = out_grad.astype(jnp.float32)
-    grad_hidden_two = jnp.dot(dispatch, grad_sent, preferred_element_type=jnp.float32)
+    grad_hidden_two = mul(halves[0], grad_sent_one.reshape(-1, width), 1, 0) + mul(
+        halves[1], grad_sent_two.reshape(-1, width), 1, 0
+    )
     grad_resid_norm, gain_two_part = norm2_pull(grad_hidden_two)
     grad_resid = grad_in + grad_resid_norm
-    grad_branch = gather(grad_resid.astype(jnp.bfloat16), "tensor", tensor_bits[::-1])
-    grad_w_out = lax.psum_scatter(grad_w_out, "tensor", scatter_dimension=0)
-    grad_w_in = lax.psum_scatter(grad_w_in, "tensor", scatter_dimension=0)
+    grad_sharp = grad_resid.astype(jnp.bfloat16)
+    grad_sharp, result = lax.optimization_barrier((grad_sharp, result))
+    came_back = exchange(result.reshape(expert_count, capacity, width)).reshape(-1, width)
+    near_grad, away_grad = collect(grad_sharp, "tensor")
+    tensor_bits = bit_count("tensor")
+    for bit in range(tensor_bits - 1):
+        grad_w_in = joined(*halved(grad_w_in, "tensor", bit))
+    near_grad, away_grad, grad_w_in = lax.optimization_barrier((near_grad, away_grad, grad_w_in))
+    grad_w_in, grad_w_in_got = halved(grad_w_in, "tensor", tensor_bits - 1)
 
     tokens_part, qkv_part, out_part, gain_one_part, bias_part = attend_back(
-        tokens, lengths, norm1_gain, qkv_flat, attn_out, rel_bias,
-        projected, mixed, log_total, grad_branch,
-    )
-    (tokens_part, qkv_part, out_part, gain_one_part, bias_part, came_back, grad_w_in, grad_w_out) = (
+        place, tokens, lengths, norm1_gain, qkv_flat, attn_out, rel_bias,
+        projected, mixed, log_total, near_grad, away_grad,
+    )
+    tokens_part, qkv_part, out_part, gain_one_part, bias_part, came_back, grad_w_in_got = (
         lax.optimization_barrier(
-            (tokens_part, qkv_part, out_part, gain_one_part, bias_part, came_back, grad_w_in, grad_w_out)
+            (tokens_part, qkv_part, out_part, gain_one_part, bias_part, came_back, grad_w_in_got)
         )
     )
-    output = resid + jnp.dot(dispatch, came_back, preferred_element_type=jnp.float32)
-    tokens_shared = scatter_sum(
-        tokens_part.reshape(n_tensor, own_rows, width), "tensor", tensor_bits
-    )
-    grad_tokens = grad_resid + tokens_shared
+    tokens_shared = lax.psum_scatter(tokens_part, "tensor", scatter_dimension=0, tiled=True)
     weights_part = jnp.concatenate([qkv_part, out_part], axis=0).astype(jnp.bfloat16)
-    weights_total = sum_rows(weights_part, "expert").astype(jnp.float32)
     bias_slots = lax.dynamic_update_slice_in_dim(
         jnp.zeros((n_tensor * head_count, bucket_count), jnp.float32),
         bias_part,
@@ -537,7 +853,16 @@
     small = jnp.concatenate(
         [gain_one_part, gain_two_part, router_part.T.reshape(-1), bias_slots.reshape(-1)]
     )
-    small = butterfly(butterfly(small, "tensor"), "expert")
+    small = butterfly(small, "tensor")
+    owned, orders = scatter_rows(weights_part, "expert")
+    owned, small = lax.optimization_barrier((owned, small))
+    small = butterfly(small, "expert")
+    begun = [gather(own, "expert", order[::-1][:1]) for own, order in zip(owned, orders)]
+    begun, came_back, grad_w_in = lax.optimization_barrier((begun, came_back, grad_w_in))
+    weights_total = gather_rows(begun, orders, "expert").astype(jnp.float32)
+    output = resid + jnp.dot(dispatch, came_back, preferred_element_type=jnp.float32)
+    grad_tokens = grad_resid + tokens_shared.astype(jnp.float32)
+    grad_w_in = joined(grad_w_in, grad_w_in_got)
     count = 2 + expert_count
     columns = lax.dynamic_slice_in_dim(
         small[: count * width].reshape(count, width),
@@ -560,8 +885,8 @@
         bias_total,
         columns[1],
         columns[2:].T,
-        grad_w_in.astype(jnp.float32)[None],
-        grad_w_out.astype(jnp.float32)[None],
+        grad_w_in,
+        grad_w_out[None],
     )
 
 

time: 535 us -> 440 us (0.82)
  matrix products: 141 us -> 20.3 us
  Pallas kernels: 58.9 us -> 163 us
  waiting for transfers between devices: 211 us -> 123 us
  blocking collectives: 9.95 us -> 0 us
  local copies, waits for them, and re-layouts: 18.5 us -> 26.9 us
  other arithmetic: 27.1 us -> 34.9 us
    dot_general x8 -> x0, matrix products: 123 us -> none  [the longest x1 38.2 us: local(): jnp.einsum('sd,jfd->jsf', grad_rows, weights_out, preferred_element_type=...]
    pallas_call x0 -> x6, Pallas kernels: none -> 104 us  [the longest x2 44.9 us: serve(): pl.pallas_call(functools.partial(expert_kernel, sub=sub), grid_spec=pltpu...]
    all_to_all x4 -> x6, waiting for transfers between devices: 102 us -> 49.9 us  [exchange(): lax.all_to_all(pieces, 'expert', split_axis=0, concat_axis=0, tiled=True)]
    reduce_scatter x2 -> x1, waiting for transfers between devices: 20.5 us -> 0.01 us  [local(): lax.psum_scatter(tokens_part, 'tensor', scatter_dimension=0, tiled=True)]
    ppermute x23 -> x25, waiting for transfers between devices: 87.3 us -> 72.2 us  [swap(): lax.ppermute(value, axis_name, [(i, i ^ 1 << bit) for i in range(count)])]
    slice x1 -> x10, local copies, waits for them, and re-layouts: 0.21 us -> 12.1 us  [the longest x6 11.8 us: halved(): pieces[half:].astype(jnp.bfloat16)]
    all_to_all x4 -> x6, starting transfers between devices: 21.3 us -> 32.1 us  [exchange(): lax.all_to_all(pieces, 'expert', split_axis=0, concat_axis=0, tiled=True)]
    add x3 -> x6, other arithmetic: 1.74 us -> 12.2 us  [the longest x4 9.16 us: joined(): return keep.astype(jnp.float32) + got.astype(jnp.float32)]
  transfers between devices with their start and end apart: 31 -> 34, of which waited for: 21 -> 18; matrix products, arithmetic and copies ran while one was open for 22% -> 15% of each run, Pallas kernels for 11% -> 37%
where the time goes in v4:
time: 440 us; the launch traced here: 435 us
  Pallas kernels  163 us (37%)
  waiting for transfers between devices  123 us (28%)
  starting transfers between devices  52.7 us (12%)
  other arithmetic  34.9 us (8%)
  local copies, waits for them, and re-layouts  26.9 us (6%)
  matrix products  20.3 us (5%)
  between operations  14.8 us (3%)
    ppermute x25, waiting for transfers between devices, swap(): lax.ppermute(value, axis_name, [(i, i ^ 1 << bit) for i in range(count)])  72.2 us
    all_to_all x6, waiting for transfers between devices, exchange(): lax.all_to_all(pieces, 'expert', split_axis=0, concat_axis=0, tiled=True)  49.9 us
    pallas_call x2, Pallas kernels, serve(): pl.pallas_call(functools.partial(expert_kernel, sub=sub), grid_spec=pltpu...  44.9 us
    pallas_call x1, Pallas kernels, attend_back(): pl.pallas_call(functools.partial(backward_kernel, head_count=head_count,...  36.4 us
    all_to_all x6, starting transfers between devices, exchange(): lax.all_to_all(pieces, 'expert', split_axis=0, concat_axis=0, tiled=True)  32.1 us
    pallas_call x1, Pallas kernels, attend(): pl.pallas_call(functools.partial(forward_kernel, head_count=head_count, h...  22.9 us
    ppermute x25, starting transfers between devices, swap(): lax.ppermute(value, axis_name, [(i, i ^ 1 << bit) for i in range(count)])  19.9 us
    pallas_call x1, Pallas kernels, act_grads_of(): pl.pallas_call(act_grads_kernel, grid_spec=pltpu.PrefetchScalarGridSpec(n...  15.4 us
  transfers between devices with their start and end apart: 34, of which 18 were waited for; matrix products, arithmetic and copies ran while one was open for 15% of the time, Pallas kernels for 37%

profile of v4, /device:TPU:0, one launch (start us, length us, event | category | flops | bytes accessed | tf_op | source)
XLA Modules:
  0.0 435.2 jit_solution(11881761014843821004)
XLA Ops:
  15.7 4.1 convolution_convert_fusion
  21.4 7.4 %all-to-all-start = ((bf16[8,272,768]{2,1,0:T(8,128)(2,1)}), bf16[8,272,768]{2,1,0:T(8,128)(2,1)S(1)}, u32[]{:S(2)}, u32[]{:S(2)}) async-start(bf16[8,272,768]{2,1,0:T(8,128)(2,1)} %dynamic_update_slice.6), calls=%async_computation | async-start | bytes 6684672 | tf_op jit(solution)/shard_map/all_to_all | solution.py:624
  31.9 22.9 %attend_forward.1 = (bf16[2048,768]{1,0:T(8,128)(2,1)}, bf16[576,2048]{1,0:T(8,128)(2,1)S(1)}, bf16[192,2048]{1,0:T(8,128)(2,1)S(1)}, f32[8,2048]{1,0:T(8,128)S(1)}) custom-call(s32[1]{0:T(128)} %bitcast.6.place_ref, s32[1,8]{1,0:T(1,128)S(1)} %copy-done.8, bf16[2048,768]{1,0:T(8,128)(2,1)} %tokens_ref.1, f32[1,768]{1,0:T(1,128)S(1)} %broadcast_in_dim.27.gain_ref, ...), custom_call_target="tpu_custom_call" | custom-call | flops 3623878656 | bytes 15728640 | tf_op jit(solution)/shard_map/attend_forward/pallas_call | solution.py:240
  54.8 3.2 fusion.25
  58.2 3.4 collective-permute-done
  67.4 17.1 %collective-permute-done.1 = bf16[1,512,768]{2,1,0:T(8,128)(2,1)} collective-permute-done((bf16[1,512,768]{2,1,0:T(8,128)(2,1)}, bf16[1,512,768]{2,1,0:T(8,128)(2,1)}, u32[]{:S(2)}, u32[]{:S(2)}) %collective-permute-start.1) | collective-permute-done | bytes 786464 | tf_op jit(solution)/shard_map/ppermute | solution.py:651
  91.8 11.9 %all-to-all-done.rows_ref.landed_ref = bf16[8,272,768]{2,1,0:T(8,128)(2,1)S(1)} async-done(((bf16[8,272,768]{2,1,0:T(8,128)(2,1)}), bf16[8,272,768]{2,1,0:T(8,128)(2,1)S(1)}, u32[]{:S(2)}, u32[]{:S(2)}) %all-to-all-start) | async-done | bytes 3342368 | tf_op jit(solution)/shard_map/all_to_all | solution.py:624
  103.7 4.3 all-to-all-start.1
  109.2 15.4 %act_grads.1 = bf16[4,2048,768]{2,1,0:T(8,128)(2,1)} custom-call(s32[1]{0:T(128)} %bitcast.6.place_ref, bf16[8,272,768]{2,1,0:T(8,128)(2,1)S(1)} %all-to-all-done.rows_ref.landed_ref, bf16[4,768,768]{2,1,0:T(8,128)(2,1)} %all-gather.3.cloned.1.call-done.weights_ref), custom_call_target="tpu_custom_call" | custom-call | flops 9663676416 | bytes 12582912 | tf_op jit(solution)/shard_map/act_grads/pallas_call | solution.py:487
  124.6 20.1 %all-to-all-done.1.rows_ref.first_ref = bf16[8,128,768]{2,1,0:T(8,128)(2,1)} async-done(((bf16[8,128,768]{2,1,0:T(8,128)(2,1)}), bf16[8,128,768]{2,1,0:T(8,128)(2,1)}, u32[]{:S(2)}, u32[]{:S(2)}) %all-to-all-start.1) | async-done | bytes 1572896 | tf_op jit(solution)/shard_map/all_to_all | solution.py:624
  144.7 3.9 all-to-all-start.3
  148.9 22.2 %expert_middle.2 = (bf16[8,128,768]{2,1,0:T(8,128)(2,1)S(1)}, bf16[4,8,2,128,768]{4,3,2,1,0:T(8,128)(2,1)}, bf16[4,8,2,128,768]{4,3,2,1,0:T(8,128)(2,1)}, bf16[8,2,128,128]{3,2,1,0:T(8,128)(2,1)S(1)}) custom-call(s32[1]{0:T(128)} %bitcast.6.place_ref, bf16[8,128,768]{2,1,0:T(8,128)(2,1)} %all-to-all-done.1.rows_ref.first_ref, ...), custom_call_target="tpu_custom_call" | custom-call | flops 9663676416 | bytes 18874368 | tf_op jit(solution)/shard_map/expert_middle/pallas_call | solution.py:443
  172.2 13.6 %all-to-all-done.3.rows_ref.last_ref = bf16[8,128,768]{2,1,0:T(8,128)(2,1)S(1)} async-done(((bf16[8,128,768]{2,1,0:T(8,128)(2,1)}), bf16[8,128,768]{2,1,0:T(8,128)(2,1)S(1)}, u32[]{:S(2)}, u32[]{:S(2)}) %all-to-all-start.3) | async-done | bytes 1572896 | tf_op jit(solution)/shard_map/all_to_all | solution.py:624
  185.8 4.3 all-to-all-start.2
  190.1 22.7 %expert_middle.3 = (bf16[8,128,768]{2,1,0:T(8,128)(2,1)}, bf16[4,8,2,128,768]{4,3,2,1,0:T(8,128)(2,1)}, bf16[4,8,2,128,768]{4,3,2,1,0:T(8,128)(2,1)}, bf16[8,2,128,128]{3,2,1,0:T(8,128)(2,1)S(1)}) custom-call(s32[1]{0:T(128)} %bitcast.6.place_ref, ...), custom_call_target="tpu_custom_call", output_to_operand_aliasing={{1}: (6, {}), {2}: (7, {}), {3}: (8, {})} | custom-call | flops 9663676416 | bytes 18874368 | tf_op jit(solution)/shard_map/expert_middle/pallas_call | solution.py:443
  212.8 13.5 %out_weights.1 = bf16[4,768,768]{2,1,0:T(8,128)(2,1)} custom-call(bf16[4,2048,768]{2,1,0:T(8,128)(2,1)} %bitcast.131, bf16[8,272,768]{2,1,0:T(8,128)(2,1)S(1)} %copy-done.1), custom_call_target="tpu_custom_call" | custom-call | flops 9663676416 | bytes 12582912 | tf_op jit(solution)/shard_map/out_weights/pallas_call | solution.py:551
  226.4 3.2 slice.160
  231.9 6.2 %all-to-all-start.4 = ((bf16[8,128,768]{2,1,0:T(8,128)(2,1)}), bf16[8,128,768]{2,1,0:T(8,128)(2,1)}, u32[]{:S(2)}, u32[]{:S(2)}) async-start(bf16[8,128,768]{2,1,0:T(8,128)(2,1)} %get-tuple-element.87), calls=%async_computation.4 | async-start | bytes 3145728 | tf_op jit(solution)/shard_map/all_to_all | solution.py:624
  238.1 3.6 fusion.5
  246.2 14.9 %in_weights.1 = (bf16[4,768,768]{2,1,0:T(8,128)(2,1)}, f32[768,128]{1,0:T(8,128)S(1)}) custom-call(bf16[8,128,768]{2,1,0:T(8,128)(2,1)} %all-to-all-done.1.rows_ref.first_ref, bf16[8,128,768]{2,1,0:T(8,128)(2,1)S(1)} %all-to-all-done.3.rows_ref.last_ref, bf16[4,8,2,128,768]{4,3,2,1,0:T(8,128)(2,1)} %get-tuple-element.88.grads_ref, ...), custom_call_target="tpu_custom_call" | custom-call | flops 9663676416 | bytes 12582912 | tf_op jit(solution)/shard_map/in_weights/pallas_call | solution.py:592
  261.2 14.8 %expert_result.1 = bf16[2048,768]{1,0:T(8,128)(2,1)} custom-call(s32[1]{0:T(128)} %bitcast.6.place_ref, bf16[4,2048,768]{2,1,0:T(8,128)(2,1)} %bitcast.132, bf16[4,768,768]{2,1,0:T(8,128)(2,1)} %all-gather.3.cloned.1.call-done.weights_ref), custom_call_target="tpu_custom_call" | custom-call | flops 9663676416 | bytes 12582912 | tf_op jit(solution)/shard_map/expert_result/pallas_call | solution.py:520
  284.9 6.0 %all-to-all-start.5 = ((bf16[8,256,768]{2,1,0:T(8,128)(2,1)}), bf16[8,256,768]{2,1,0:T(8,128)(2,1)}, u32[]{:S(2)}, u32[]{:S(2)}) async-start(bf16[8,256,768]{2,1,0:T(8,128)(2,1)} %bitcast.28), calls=%async_computation.5 | async-start | bytes 6291456 | tf_op jit(solution)/shard_map/all_to_all | solution.py:624
  294.7 19.4 %collective-permute-done.4 = bf16[1,512,768]{2,1,0:T(8,128)(2,1)S(1)} collective-permute-done((bf16[1,512,768]{2,1,0:T(8,128)(2,1)S(1)}, bf16[1,512,768]{2,1,0:T(8,128)(2,1)S(1)}, u32[]{:S(2)}, u32[]{:S(2)}) %collective-permute-start.4) | collective-permute-done | bytes 786464 | tf_op jit(solution)/shard_map/ppermute | solution.py:651
  320.4 36.4 %attend_backward.1 = (bf16[2048,768]{1,0:T(8,128)(2,1)}, f32[576,768]{1,0:T(8,128)}, f32[192,768]{1,0:T(8,128)S(1)}, f32[8,768]{1,0:T(8,128)S(1)}, f32[8,512]{1,0:T(8,128)S(1)}, /*index=5*/f32[8,256]{1,0:T(8,128)S(1)}) custom-call(s32[1]{0:T(128)} %bitcast.6.place_ref, s32[1,8]{1,0:T(1,128)S(1)} %copy-done.8, bf16[2048,768]{1,0:T(8,128)(2,1)} %tokens_ref.1, ...), custom_call_target="tpu_custom_call" | custom-call | flops 7851737088 | bytes 22020096 | tf_op jit(solution)/shard_map/attend_backward/pallas_call | solution.py:298
  357.3 4.2 all-to-all-done.5
  366.0 3.3 collective-permute-done.15
  369.3 3.9 collective-permute-done.8
  376.3 4.3 collective-permute-done.9
  381.0 5.2 %collective-permute-done.12 = bf16[2,48,768]{2,1,0:T(8,128)(2,1)S(1)} collective-permute-done((bf16[2,48,768]{2,1,0:T(8,128)(2,1)S(1)}, bf16[2,48,768]{2,1,0:T(8,128)(2,1)S(1)}, u32[]{:S(2)}, u32[]{:S(2)}) %collective-permute-start.12) | collective-permute-done | bytes 147488 | tf_op jit(solution)/shard_map/ppermute | solution.py:651
  387.3 3.8 collective-permute-done.13
  405.1 5.0 %convolution_add_fusion.1 = f32[512,768]{1,0:T(8,128)} fusion(f32[512,768]{1,0:T(8,128)S(1)} %copy-done.15, bf16[512,2048]{1,0:T(8,128)(2,1)S(1)} %copy-done.21, bf16[2048,768]{1,0:T(8,128)(2,1)} %bitcast.29), kind=kOutput, calls=%fused_computation.39 | convolution fusion | flops 1611005952 | bytes 8388608 | tf_op jit(solution)/shard_map/dot_general | solution.py:863
  416.3 5.6 %collective-permute-done.24 = bf16[2,2,48,768]{3,2,1,0:T(8,128)(2,1)S(1)} collective-permute-done((bf16[2,2,48,768]{3,2,1,0:T(8,128)(2,1)S(1)}, bf16[2,2,48,768]{3,2,1,0:T(8,128)(2,1)S(1)}, u32[]{:S(2)}, u32[]{:S(2)}) %collective-permute-start.24) | collective-permute-done | bytes 294944 | tf_op jit(solution)/shard_map/ppermute | solution.py:651
  (225 shorter events, 90.3 us)
Async XLA Ops:
  7.2 102.1 %all-gather.3.cloned.1.call-start = ((), (), s32[]{:S(2)}) async-start(), calls=%async_computation.7 | async-start | bytes 5898240 | tf_op jit(solution)/shard_map/all_gather | solution.py:787
  21.4 82.4 %all-to-all-start = ((bf16[8,272,768]{2,1,0:T(8,128)(2,1)}), bf16[8,272,768]{2,1,0:T(8,128)(2,1)S(1)}, u32[]{:S(2)}, u32[]{:S(2)}) async-start(bf16[8,272,768]{2,1,0:T(8,128)(2,1)} %dynamic_update_slice.6), calls=%async_computation | async-start | bytes 6684672 | tf_op jit(solution)/shard_map/all_to_all | solution.py:624
  28.8 115.9 %all-gather.5.cloned.1.call-start = ((), (), s32[]{:S(2)}) async-start(), calls=%async_computation.8 | async-start | bytes 5898240 | tf_op jit(solution)/shard_map/all_gather | solution.py:788
  64.6 19.9 %collective-permute-start.1 = (bf16[1,512,768]{2,1,0:T(8,128)(2,1)}, bf16[1,512,768]{2,1,0:T(8,128)(2,1)}, u32[]{:S(2)}, u32[]{:S(2)}) collective-permute-start(bf16[1,512,768]{2,1,0:T(8,128)(2,1)} %slice.254), channel_id=1, source_target_pairs={{0,2},{1,3},{2,0},{3,1},{4,6},{5,7},{6,4},{7,5},{8,10},{9,11},{10,... | collective-permute-start | bytes 2359304 | tf_op jit(solution)/shard_map/ppermute | solution.py:651
  103.7 41.0 %all-to-all-start.1 = ((bf16[8,128,768]{2,1,0:T(8,128)(2,1)}), bf16[8,128,768]{2,1,0:T(8,128)(2,1)}, u32[]{:S(2)}, u32[]{:S(2)}) async-start(bf16[8,128,768]{2,1,0:T(8,128)(2,1)} %bitcast.147), calls=%async_computation.1 | async-start | bytes 3145728 | tf_op jit(solution)/shard_map/all_to_all | solution.py:624
  144.7 41.1 %all-to-all-start.3 = ((bf16[8,128,768]{2,1,0:T(8,128)(2,1)}), bf16[8,128,768]{2,1,0:T(8,128)(2,1)S(1)}, u32[]{:S(2)}, u32[]{:S(2)}) async-start(bf16[8,128,768]{2,1,0:T(8,128)(2,1)} %bitcast.146), calls=%async_computation.3 | async-start | bytes 3145728 | tf_op jit(solution)/shard_map/all_to_all | solution.py:624
  185.8 46.1 %all-to-all-start.2 = ((bf16[8,128,768]{2,1,0:T(8,128)(2,1)}), bf16[8,128,768]{2,1,0:T(8,128)(2,1)}, u32[]{:S(2)}, u32[]{:S(2)}) async-start(bf16[8,128,768]{2,1,0:T(8,128)(2,1)} %copy-done.3), calls=%async_computation.2 | async-start | bytes 3145728 | tf_op jit(solution)/shard_map/all_to_all | solution.py:624
  229.6 12.1 %collective-permute-start.2 = (bf16[2,768,768]{2,1,0:T(8,128)(2,1)}, bf16[2,768,768]{2,1,0:T(8,128)(2,1)}, u32[]{:S(2)}, u32[]{:S(2)}) collective-permute-start(bf16[2,768,768]{2,1,0:T(8,128)(2,1)} %slice.160), channel_id=1, source_target_pairs={{0,1},{1,0},{2,3},{3,2},{4,5},{5,4},{6,7},{7,6},{8,9},{9,8},{10,11... | collective-permute-start | bytes 7077896 | tf_op jit(solution)/shard_map/ppermute | solution.py:651
  231.9 45.7 %all-to-all-start.4 = ((bf16[8,128,768]{2,1,0:T(8,128)(2,1)}), bf16[8,128,768]{2,1,0:T(8,128)(2,1)}, u32[]{:S(2)}, u32[]{:S(2)}) async-start(bf16[8,128,768]{2,1,0:T(8,128)(2,1)} %get-tuple-element.87), calls=%async_computation.4 | async-start | bytes 3145728 | tf_op jit(solution)/shard_map/all_to_all | solution.py:624
  244.7 31.3 %collective-permute-start.3 = (bf16[1,768,768]{2,1,0:T(8,128)(2,1)S(1)}, bf16[1,768,768]{2,1,0:T(8,128)(2,1)S(1)}, u32[]{:S(2)}, u32[]{:S(2)}) collective-permute-start(bf16[1,768,768]{2,1,0:T(8,128)(2,1)S(1)} %slice.253), channel_id=1, source_target_pairs={{0,2},{1,3},{2,0},{3,1},{4,6},{5,7},{6,4},{7,5},{8,10},{9,11},{10,... | collective-permute-start | bytes 3538952 | tf_op jit(solution)/shard_map/ppermute | solution.py:651
  284.9 76.6 %all-to-all-start.5 = ((bf16[8,256,768]{2,1,0:T(8,128)(2,1)}), bf16[8,256,768]{2,1,0:T(8,128)(2,1)}, u32[]{:S(2)}, u32[]{:S(2)}) async-start(bf16[8,256,768]{2,1,0:T(8,128)(2,1)} %bitcast.28), calls=%async_computation.5 | async-start | bytes 6291456 | tf_op jit(solution)/shard_map/all_to_all | solution.py:624
  290.9 133.8 %reduce-scatter.2.cloned.1.call-start = ((), (), s32[]{:S(2)}) async-start(), calls=%async_computation.9 | async-start | bytes 3932160 | tf_op jit(solution)/shard_map/reduce_scatter | solution.py:845
  294.2 20.4 %collective-permute-start.6 = (bf16[2,768,768]{2,1,0:T(8,128)(2,1)}, bf16[2,768,768]{2,1,0:T(8,128)(2,1)}, u32[]{:S(2)}, u32[]{:S(2)}) collective-permute-start(bf16[2,768,768]{2,1,0:T(8,128)(2,1)} %slice.164), channel_id=1, source_target_pairs={{0,1},{1,0},{2,3},{3,2},{4,5},{5,4},{6,7},{7,6},{8,9},{9,8},{10,11... | collective-permute-start | bytes 7077896 | tf_op jit(solution)/shard_map/ppermute | solution.py:651
  294.2 20.0 %collective-permute-start.4 = (bf16[1,512,768]{2,1,0:T(8,128)(2,1)S(1)}, bf16[1,512,768]{2,1,0:T(8,128)(2,1)S(1)}, u32[]{:S(2)}, u32[]{:S(2)}) collective-permute-start(bf16[1,512,768]{2,1,0:T(8,128)(2,1)S(1)} %bitcast.138), channel_id=1, source_target_pairs={{0,2},{1,3},{2,0},{3,1},{4,6},{5,7},{6,4},{7,5},{8,10},{9,11},{10,... | collective-permute-start | bytes 2359304 | tf_op jit(solution)/shard_map/ppermute | solution.py:651
  314.3 3.6 collective-permute-start.5
  319.0 38.3 %collective-permute-start.7 = (bf16[1,768,768]{2,1,0:T(8,128)(2,1)}, bf16[1,768,768]{2,1,0:T(8,128)(2,1)}, u32[]{:S(2)}, u32[]{:S(2)}) collective-permute-start(bf16[1,768,768]{2,1,0:T(8,128)(2,1)} %slice.252), channel_id=1, source_target_pairs={{0,2},{1,3},{2,0},{3,1},{4,6},{5,7},{6,4},{7,5},{8,10},{9,11},{10,... | collective-permute-start | bytes 3538952 | tf_op jit(solution)/shard_map/ppermute | solution.py:651
  363.7 9.5 %collective-permute-start.8 = (bf16[2,2,48,768]{3,2,1,0:T(8,128)(2,1)S(1)}, bf16[2,2,48,768]{3,2,1,0:T(8,128)(2,1)S(1)}, u32[]{:S(2)}, u32[]{:S(2)}) collective-permute-start(bf16[2,2,48,768]{3,2,1,0:T(8,128)(2,1)S(1)} %dynamic-slice_bitcast_fusion.1), channel_id=1, source_target_pairs={{0,4},{4,0},{8,12},{12,8},{16,20},{20,16},{24,28},{28,24},{1,5},{5... | collective-permute-start | bytes 884744 | tf_op jit(solution)/shard_map/ppermute | solution.py:651
  365.3 4.0 collective-permute-start.15
  365.9 8.9 %collective-permute-start.11 = (bf16[2,2,48,768]{3,2,1,0:T(8,128)(2,1)S(1)}, bf16[2,2,48,768]{3,2,1,0:T(8,128)(2,1)S(1)}, u32[]{:S(2)}, u32[]{:S(2)}) collective-permute-start(bf16[2,2,48,768]{3,2,1,0:T(8,128)(2,1)S(1)} %dynamic-slice_bitcast_fusion), channel_id=1, source_target_pairs={{0,8},{4,12},{8,0},{12,4},{16,24},{20,28},{24,16},{28,20},{1,9},{5... | collective-permute-start | bytes 884744 | tf_op jit(solution)/shard_map/ppermute | solution.py:651
  373.3 7.4 %collective-permute-start.9 = (bf16[2,48,768]{2,1,0:T(8,128)(2,1)S(1)}, bf16[2,48,768]{2,1,0:T(8,128)(2,1)S(1)}, u32[]{:S(2)}, u32[]{:S(2)}) collective-permute-start(bf16[2,48,768]{2,1,0:T(8,128)(2,1)S(1)} %fusion.11), channel_id=1, source_target_pairs={{0,8},{4,12},{8,0},{12,4},{16,24},{20,28},{24,16},{28,20},{1,9},{5... | collective-permute-start | bytes 442376 | tf_op jit(solution)/shard_map/ppermute | solution.py:651
  374.9 11.3 %collective-permute-start.12 = (bf16[2,48,768]{2,1,0:T(8,128)(2,1)S(1)}, bf16[2,48,768]{2,1,0:T(8,128)(2,1)S(1)}, u32[]{:S(2)}, u32[]{:S(2)}) collective-permute-start(bf16[2,48,768]{2,1,0:T(8,128)(2,1)S(1)} %fusion.12), channel_id=1, source_target_pairs={{0,16},{4,20},{8,24},{12,28},{16,0},{20,4},{24,8},{28,12},{1,17},{... | collective-permute-start | bytes 442376 | tf_op jit(solution)/shard_map/ppermute | solution.py:651
  380.7 6.5 %collective-permute-start.10 = (bf16[48,768]{1,0:T(8,128)(2,1)S(1)}, bf16[48,768]{1,0:T(8,128)(2,1)S(1)}, u32[]{:S(2)}, u32[]{:S(2)}) collective-permute-start(bf16[48,768]{1,0:T(8,128)(2,1)S(1)} %fusion.15), channel_id=1, source_target_pairs={{0,16},{4,20},{8,24},{12,28},{16,0},{20,4},{24,8},{28,12},{1,17},{... | collective-permute-start | bytes 221192 | tf_op jit(solution)/shard_map/ppermute | solution.py:651
  386.3 4.8 %collective-permute-start.13 = (bf16[48,768]{1,0:T(8,128)(2,1)S(1)}, bf16[48,768]{1,0:T(8,128)(2,1)S(1)}, u32[]{:S(2)}, u32[]{:S(2)}) collective-permute-start(bf16[48,768]{1,0:T(8,128)(2,1)S(1)} %fusion.16), channel_id=1, source_target_pairs={{0,4},{4,0},{8,12},{12,8},{16,20},{20,16},{24,28},{28,24},{1,5},{5... | collective-permute-start | bytes 221192 | tf_op jit(solution)/shard_map/ppermute | solution.py:651
  391.1 6.7 %collective-permute-start.16 = (bf16[48,768]{1,0:T(8,128)(2,1)S(1)}, bf16[48,768]{1,0:T(8,128)(2,1)S(1)}, u32[]{:S(2)}, u32[]{:S(2)}) collective-permute-start(bf16[48,768]{1,0:T(8,128)(2,1)S(1)} %fusion.14), channel_id=1, source_target_pairs={{0,16},{4,20},{8,24},{12,28},{16,0},{20,4},{24,8},{28,12},{1,17},{... | collective-permute-start | bytes 221192 | tf_op jit(solution)/shard_map/ppermute | solution.py:651
  391.2 4.0 collective-permute-start.18
  392.6 5.3 %collective-permute-start.17 = (bf16[48,768]{1,0:T(8,128)(2,1)S(1)}, bf16[48,768]{1,0:T(8,128)(2,1)S(1)}, u32[]{:S(2)}, u32[]{:S(2)}) collective-permute-start(bf16[48,768]{1,0:T(8,128)(2,1)S(1)} %fusion.13), channel_id=1, source_target_pairs={{0,4},{4,0},{8,12},{12,8},{16,20},{20,16},{24,28},{28,24},{1,5},{5... | collective-permute-start | bytes 221192 | tf_op jit(solution)/shard_map/ppermute | solution.py:651
  395.2 4.9 %collective-permute-start.19 = (f32[9216]{0:T(1024)S(1)}, f32[9216]{0:T(1024)S(1)}, u32[]{:S(2)}, u32[]{:S(2)}) collective-permute-start(f32[9216]{0:T(1024)S(1)} %add.201), channel_id=1, source_target_pairs={{0,8},{4,12},{8,0},{12,4},{16,24},{20,28},{24,16},{28,20},{1,9},{5... | collective-permute-start | bytes 110600 | tf_op jit(solution)/shard_map/ppermute | solution.py:651
  400.2 12.9 %collective-permute-start.20 = (f32[9216]{0:T(1024)S(1)}, f32[9216]{0:T(1024)S(1)}, u32[]{:S(2)}, u32[]{:S(2)}) collective-permute-start(f32[9216]{0:T(1024)S(1)} %add.202), channel_id=1, source_target_pairs={{0,16},{4,20},{8,24},{12,28},{16,0},{20,4},{24,8},{28,12},{1,17},{... | collective-permute-start | bytes 110600 | tf_op jit(solution)/shard_map/ppermute | solution.py:651
  402.5 12.6 %collective-permute-start.23 = (bf16[2,48,768]{2,1,0:T(8,128)(2,1)S(1)}, bf16[2,48,768]{2,1,0:T(8,128)(2,1)S(1)}, u32[]{:S(2)}, u32[]{:S(2)}) collective-permute-start(bf16[2,48,768]{2,1,0:T(8,128)(2,1)S(1)} %pad_maximum_fusion.7), channel_id=1, source_target_pairs={{0,16},{4,20},{8,24},{12,28},{16,0},{20,4},{24,8},{28,12},{1,17},{... | collective-permute-start | bytes 442376 | tf_op jit(solution)/shard_map/ppermute | solution.py:651
  403.1 12.2 %collective-permute-start.21 = (bf16[2,48,768]{2,1,0:T(8,128)(2,1)S(1)}, bf16[2,48,768]{2,1,0:T(8,128)(2,1)S(1)}, u32[]{:S(2)}, u32[]{:S(2)}) collective-permute-start(bf16[2,48,768]{2,1,0:T(8,128)(2,1)S(1)} %pad_maximum_fusion.6), channel_id=1, source_target_pairs={{0,8},{4,12},{8,0},{12,4},{16,24},{20,28},{24,16},{28,20},{1,9},{5... | collective-permute-start | bytes 442376 | tf_op jit(solution)/shard_map/ppermute | solution.py:651
  415.1 6.8 %collective-permute-start.24 = (bf16[2,2,48,768]{3,2,1,0:T(8,128)(2,1)S(1)}, bf16[2,2,48,768]{3,2,1,0:T(8,128)(2,1)S(1)}, u32[]{:S(2)}, u32[]{:S(2)}) collective-permute-start(bf16[2,2,48,768]{3,2,1,0:T(8,128)(2,1)S(1)} %pad_maximum_fusion.5), channel_id=1, source_target_pairs={{0,8},{4,12},{8,0},{12,4},{16,24},{20,28},{24,16},{28,20},{1,9},{5... | collective-permute-start | bytes 884744 | tf_op jit(solution)/shard_map/ppermute | solution.py:651
  415.4 6.8 %collective-permute-start.22 = (bf16[2,2,48,768]{3,2,0,1:T(8,128)(2,1)S(1)}, bf16[2,2,48,768]{3,2,0,1:T(8,128)(2,1)S(1)}, u32[]{:S(2)}, u32[]{:S(2)}) collective-permute-start(bf16[2,2,48,768]{3,2,0,1:T(8,128)(2,1)S(1)} %pad_maximum_fusion.4), channel_id=1, source_target_pairs={{0,4},{4,0},{8,12},{12,8},{16,20},{20,16},{24,28},{28,24},{1,5},{5... | collective-permute-start | bytes 884744 | tf_op jit(solution)/shard_map/ppermute | solution.py:651
  (33 other events, 203.5 us)
Sparse Core Ops, SparseCore 0:
  9.6 40.2 all-gather.2
  103.9 36.4 all-gather.4
  365.4 35.9 reduce-scatter.1

commit v5 on v4

--- a/solution.py
+++ b/solution.py
@@ -14,6 +14,7 @@
 VMEM_LIMIT = 48 * 2**20
 LANES = 128
 SPARE = 16
+EXTRA = 64
 
 
 def mul(left, right, left_dim, right_dim):
@@ -117,8 +118,8 @@
 def backward_kernel(
     place_ref, lengths_ref, tokens_ref, gain_ref, qkv_ref, out_ref, bias_ref,
     proj_ref, before_ref, mixed_ref, log_ref, near_grad_ref, away_grad_ref,
-    part_ref, qkv_grad_ref, out_grad_ref, gain_grad_ref, bias_grad_ref, far_grad_ref,
-    spread_ref, near_ref, far_ref, carry_ref, pieces_ref,
+    small_ref, gain_two_ref, part_ref, packed_ref,
+    spread_ref, near_ref, far_ref, carry_ref, pieces_ref, qkv_grad_ref, out_grad_ref, gain_grad_ref,
     *, head_count, head_dim, slots, block_count, placed,
 ):
     step = pl.program_id(0)
@@ -134,7 +135,6 @@
         qkv_grad_ref[...] = jnp.zeros_like(qkv_grad_ref)
         out_grad_ref[...] = jnp.zeros_like(out_grad_ref)
         gain_grad_ref[...] = jnp.zeros_like(gain_grad_ref)
-        bias_grad_ref[...] = jnp.zeros_like(bias_grad_ref)
 
     @pl.when(step > 0)
     def _():
@@ -196,9 +196,29 @@
 
     @pl.when(step == block_count - 1)
     def _():
+        width = gain_grad_ref.shape[1]
+        packed_ref[: 3 * inner, :] = qkv_grad_ref[...].astype(jnp.bfloat16)
+        packed_ref[3 * inner : 4 * inner, :] = out_grad_ref[...].astype(jnp.bfloat16)
+        lines = []
         for head in range(head_count):
-            bias_grad_ref[head : head + 1, :] = fold_bias(near_ref[head])
-        far_grad_ref[...] = far_ref[...]
+            total = fold_bias(near_ref[head])
+            near = total[:, HALF : HALF + LANES]
+            lane = lax.broadcasted_iota(jnp.int32, near.shape, 1)
+            inside = jnp.where(lane < LANES - 1, near, 0.0)
+            rest = (
+                jnp.sum(total, axis=1, keepdims=True)
+                - jnp.sum(inside, axis=1, keepdims=True)
+                + jnp.sum(far_ref[head : head + 1], axis=1, keepdims=True)
+            )
+            lines.append(jnp.where(lane < LANES - 1, near, rest))
+        lines.append(jnp.zeros((1, width - head_count * LANES), jnp.float32))
+        bias_row = jnp.concatenate(lines, axis=1)
+        gain_row = jnp.sum(gain_grad_ref[...], axis=0, keepdims=True)
+        rows = lax.broadcasted_iota(jnp.int32, small_ref.shape, 0)
+        gain_two_row = jnp.sum(gain_two_ref[...], axis=0, keepdims=True)
+        small = jnp.where(rows == 0, gain_row, jnp.where(rows == 1, bias_row, small_ref[...]))
+        small = jnp.where(rows == 2, gain_two_row, small)
+        packed_ref[4 * inner :, :] = small.astype(jnp.bfloat16)
 
 
 def whole(shape):
@@ -282,7 +302,7 @@
 
 def attend_back(
     place, tokens, lengths, gain, qkv_flat, attn_out, rel_bias, projected, mixed, log_total, near_grad,
-    away_grad,
+    away_grad, small, gain_two,
 ):
     rows, width = tokens.shape
     inner = attn_out.shape[0]
@@ -295,7 +315,7 @@
     def placed(block, at):
         return reversed_bits(block ^ at[0], bits)
 
-    part, qkv_grad, out_grad, gain_grad, bias_grad, far_grad = pl.pallas_call(
+    return pl.pallas_call(
         functools.partial(
             backward_kernel,
             head_count=head_count,
@@ -332,14 +352,12 @@
                         jnp.maximum(placed(last - step, at) - block_count // 2, 0), 0, 0
                     ),
                 ),
+                whole(small.shape),
+                whole(gain_two.shape),
             ],
             out_specs=[
                 pl.BlockSpec((BLOCK, width), lambda step, at: (last - step, 0)),
-                whole((3 * inner, width)),
-                whole((inner, width)),
-                whole((8, width)),
-                whole((8, 2 * HALF)),
-                whole((8, HALF)),
+                whole((4 * inner + small.shape[0], width)),
             ],
             scratch_shapes=[
                 pltpu.VMEM((head_count, 2 * HALF, HALF), jnp.float32),
@@ -347,15 +365,14 @@
                 pltpu.VMEM((8, HALF), jnp.float32),
                 pltpu.VMEM((2 * inner, 2 * BLOCK), jnp.float32),
                 pltpu.VMEM((3 * inner, BLOCK), jnp.bfloat16),
+                pltpu.VMEM((3 * inner, width), jnp.float32),
+                pltpu.VMEM((inner, width), jnp.float32),
+                pltpu.VMEM((8, width), jnp.float32),
             ],
         ),
         out_shape=[
             jax.ShapeDtypeStruct((rows, width), jnp.bfloat16),
-            jax.ShapeDtypeStruct((3 * inner, width), jnp.float32),
-            jax.ShapeDtypeStruct((inner, width), jnp.float32),
-            jax.ShapeDtypeStruct((8, width), jnp.float32),
-            jax.ShapeDtypeStruct((8, 2 * HALF), jnp.float32),
-            jax.ShapeDtypeStruct((8, HALF), jnp.float32),
+            jax.ShapeDtypeStruct((4 * inner + small.shape[0], width), jnp.bfloat16),
         ],
         compiler_params=pltpu.CompilerParams(vmem_limit_bytes=VMEM_LIMIT),
         cost_estimate=pl.CostEstimate(
@@ -367,12 +384,8 @@
     )(
         place, lengths, tokens, gain[None, :], qkv_flat, attn_out, bias_line(rel_bias),
         projected, projected, mixed, log_total, near_grad, away_grad,
-    )
-    near_grad = bias_grad[:head_count, HALF : HALF + bucket_count - 1]
-    rest = jnp.sum(bias_grad[:head_count], axis=1) - jnp.sum(near_grad, axis=1)
-    rest = rest + jnp.sum(far_grad[:head_count], axis=1)
-    bias_part = jnp.concatenate([near_grad, rest[:, None]], axis=1)
-    return part, qkv_grad, out_grad, jnp.sum(gain_grad, axis=0), bias_part
+        small, gain_two,
+    )
 
 
 GELU_ONE = 0.7978845608028654
@@ -530,52 +543,73 @@
         ),
         out_shape=jax.ShapeDtypeStruct((rows, width), jnp.bfloat16),
         compiler_params=pltpu.CompilerParams(vmem_limit_bytes=VMEM_LIMIT),
-        cost_estimate=pl.CostEstimate(
-            flops=2 * rows * width * shards * hidden,
-            bytes_accessed=2 * rows * shards * hidden,
-            transcendentals=0,
-        ),
+        cost_estimate=pl.CostEstimate(flops=0, bytes_accessed=0, transcendentals=0),
         name="expert_result",
     )(place, act, weights)
 
 
-def out_weights_kernel(act_ref, landed_ref, out_ref):
+def store_half(value, send_ref, keep_ref):
+    half = pl.num_programs(0) // 2
+
+    @pl.when(pl.program_id(0) < half)
+    def _():
+        send_ref[0] = value
+
+    @pl.when(pl.program_id(0) >= half)
+    def _():
+        keep_ref[0] = value
+
+
+def half_specs(shards, rows, columns):
+    half = shards // 2
+    shape = jax.ShapeDtypeStruct((half, rows, columns), jnp.bfloat16)
+    specs = [
+        pl.BlockSpec((1, rows, columns), lambda step: (jnp.minimum(step, half - 1), 0, 0)),
+        pl.BlockSpec((1, rows, columns), lambda step: (jnp.maximum(step - half, 0), 0, 0)),
+    ]
+    return specs, [shape, shape]
+
+
+def send_first(step, shards):
+    return (step + shards // 2) % shards
+
+
+def out_weights_kernel(act_ref, landed_ref, send_ref, keep_ref):
     capacity = act_ref.shape[1] // landed_ref.shape[0]
     rows = landed_ref[:, :capacity].reshape(act_ref.shape[1], landed_ref.shape[2])
-    out_ref[0] = mul(act_ref[0], rows, 0, 0).astype(jnp.bfloat16)
+    store_half(mul(act_ref[0], rows, 0, 0).astype(jnp.bfloat16), send_ref, keep_ref)
 
 
 def out_weights_of(act, landed):
     shards, rows, hidden = act.shape
     width = landed.shape[2]
+    specs, shapes = half_specs(shards, hidden, width)
     return pl.pallas_call(
         out_weights_kernel,
         grid=(shards,),
         in_specs=[
-            pl.BlockSpec((1, rows, hidden), lambda step: (step, 0, 0)),
+            pl.BlockSpec((1, rows, hidden), lambda step: (send_first(step, shards), 0, 0)),
             whole(landed.shape),
         ],
-        out_specs=pl.BlockSpec((1, hidden, width), lambda step: (step, 0, 0)),
-        out_shape=jax.ShapeDtypeStruct((shards, hidden, width), jnp.bfloat16),
+        out_specs=specs,
+        out_shape=shapes,
         compiler_params=pltpu.CompilerParams(vmem_limit_bytes=VMEM_LIMIT),
-        cost_estimate=pl.CostEstimate(
-            flops=2 * rows * width * shards * hidden,
-            bytes_accessed=2 * rows * shards * hidden,
-            transcendentals=0,
-        ),
+        cost_estimate=pl.CostEstimate(flops=0, bytes_accessed=0, transcendentals=0),
         name="out_weights",
     )(act, landed)
 
 
-def in_weights_kernel(first_ref, last_ref, grads_ref, logits_ref, out_ref, router_ref):
+def in_weights_kernel(
+    first_ref, last_ref, grads_ref, logits_ref, send_ref, keep_ref, router_ref
+):
     sources, slots, width = first_ref.shape
     first = first_ref[...].reshape(sources * slots, width)
     last = last_ref[...].reshape(sources * slots, width)
     hidden = grads_ref.shape[4]
-    out_ref[0] = (
-        mul(first, grads_ref[0, :, 0].reshape(sources * slots, hidden), 0, 0)
-        + mul(last, grads_ref[0, :, 1].reshape(sources * slots, hidden), 0, 0)
-    ).astype(jnp.bfloat16)
+    total = mul(first, grads_ref[0, :, 0].reshape(sources * slots, hidden), 0, 0) + mul(
+        last, grads_ref[0, :, 1].reshape(sources * slots, hidden), 0, 0
+    )
+    store_half(total.astype(jnp.bfloat16), send_ref, keep_ref)
 
     @pl.when(pl.program_id(0) == 0)
     def _():
@@ -589,31 +623,140 @@
     shards, sources, _, slots, hidden = grads.shape
     width = first.shape[2]
     lanes = logit_grads.shape[3]
+    specs, shapes = half_specs(shards, width, hidden)
     return pl.pallas_call(
         in_weights_kernel,
         grid=(shards,),
         in_specs=[
             whole(first.shape),
             whole(last.shape),
-            pl.BlockSpec((1,) + grads.shape[1:], lambda step: (step, 0, 0, 0, 0)),
+            pl.BlockSpec(
+                (1,) + grads.shape[1:], lambda step: (send_first(step, shards), 0, 0, 0, 0)
+            ),
             whole(logit_grads.shape),
         ],
+        out_specs=specs + [whole((width, lanes))],
+        out_shape=shapes + [jax.ShapeDtypeStruct((width, lanes), jnp.float32)],
+        compiler_params=pltpu.CompilerParams(vmem_limit_bytes=VMEM_LIMIT),
+        cost_estimate=pl.CostEstimate(flops=0, bytes_accessed=0, transcendentals=0),
+        name="in_weights",
+    )(first, last, grads, logit_grads)
+
+
+def place_kernel(routes_ref, grad_ref, slots_ref, index_ref, *, capacity, spare):
+    expert = pl.program_id(0)
+    experts = pl.num_programs(0)
+    tokens = routes_ref.shape[1]
+    lanes = lax.broadcasted_iota(jnp.int32, (LANES, tokens), 0)
+    hot = [(routes_ref[choice : choice + 1, :] == lanes) for choice in range(2)]
+
+    @pl.when(expert == 0)
+    def _():
+        counts = (hot[0] | hot[1]).astype(jnp.bfloat16)
+        earlier = (
+            lax.broadcasted_iota(jnp.int32, (tokens, tokens), 0)
+            < lax.broadcasted_iota(jnp.int32, (tokens, tokens), 1)
+        ).astype(jnp.bfloat16)
+        before = mul(counts, earlier, 1, 0)
+        for choice in range(2):
+            rank = jnp.sum(jnp.where(hot[choice], before, 0.0), axis=0, keepdims=True)
+            index_ref[choice : choice + 1, :] = (
+                routes_ref[choice : choice + 1, :] * capacity + rank.astype(jnp.int32)
+            )
+
+    slot = lax.broadcasted_iota(jnp.int32, (capacity, tokens), 0) + expert * capacity
+    named = [(index_ref[choice : choice + 1, :] == slot) for choice in range(2)]
+    spread = (named[0] | named[1]).astype(jnp.bfloat16)
+    slots_ref[0, :capacity] = mul(spread, grad_ref[...], 1, 0).astype(jnp.bfloat16)
+    others = [
+        jnp.broadcast_to(routes_ref[1 - choice : 2 - choice, :] + 1, (spare, tokens))
+        .astype(jnp.float32)
+        .astype(jnp.bfloat16)
+        for choice in range(2)
+    ]
+    ids = mul(others[0], named[0].astype(jnp.bfloat16), 1, 1) + mul(
+        others[1], named[1].astype(jnp.bfloat16), 1, 1
+    )
+    width = slots_ref.shape[2]
+    padded = jnp.concatenate([ids, jnp.zeros((spare, width - capacity), jnp.float32)], axis=1)
+    slots_ref[0, capacity:] = padded.astype(jnp.bfloat16)
+
+
+def place_rows(routes, out_grad, experts, capacity):
+    tokens, width = out_grad.shape
+    return pl.pallas_call(
+        functools.partial(place_kernel, capacity=capacity, spare=SPARE),
+        grid=(experts,),
+        in_specs=[whole((2, tokens)), whole((tokens, width))],
         out_specs=[
-            pl.BlockSpec((1, width, hidden), lambda step: (step, 0, 0)),
-            whole((width, lanes)),
+            pl.BlockSpec((1, capacity + SPARE, width), lambda step: (step, 0, 0)),
+            whole((8, tokens)),
         ],
         out_shape=[
-            jax.ShapeDtypeStruct((shards, width, hidden), jnp.bfloat16),
-            jax.ShapeDtypeStruct((width, lanes), jnp.float32),
+            jax.ShapeDtypeStruct((experts, capacity + SPARE, width), jnp.bfloat16),
+            jax.ShapeDtypeStruct((8, tokens), jnp.int32),
         ],
         compiler_params=pltpu.CompilerParams(vmem_limit_bytes=VMEM_LIMIT),
         cost_estimate=pl.CostEstimate(
-            flops=4 * sources * slots * width * shards * hidden,
-            bytes_accessed=4 * sources * slots * shards * hidden,
+            flops=2 * experts * capacity * tokens * width,
+            bytes_accessed=2 * experts * capacity * width,
             transcendentals=0,
         ),
-        name="in_weights",
-    )(first, last, grads, logit_grads)
+        name="place_rows",
+    )(routes.T, out_grad)
+
+
+def combine_kernel(
+    first_ref, first_rows_ref, last_ref, last_rows_ref, resid_ref, gain_ref, grad_ref,
+    out_ref, sharp_ref, gain_grad_ref,
+):
+    grad_hidden = mul(first_ref[...], first_rows_ref[...], 1, 0) + mul(
+        last_ref[...], last_rows_ref[...], 1, 0
+    )
+    resid = resid_ref[...]
+    inverse = lax.rsqrt(jnp.mean(resid * resid, axis=-1, keepdims=True) + EPSILON)
+    normed = resid * inverse
+
+    @pl.when(pl.program_id(0) == 0)
+    def _():
+        gain_grad_ref[...] = jnp.zeros_like(gain_grad_ref)
+
+    rows, width = resid.shape
+    gain_grad_ref[...] += jnp.sum((grad_hidden * normed).reshape(rows // 8, 8, width), axis=0)
+    gained = grad_hidden * gain_ref[...]
+    total = grad_ref[...].astype(jnp.float32) + inverse * (
+        gained - normed * jnp.mean(gained * normed, axis=-1, keepdims=True)
+    )
+    out_ref[...] = total
+    sharp_ref[...] = total.astype(jnp.bfloat16)
+
+
+def combine(first, first_rows, last, last_rows, resid, gain, out_grad):
+    rows, width = resid.shape
+    slots = first_rows.shape[0]
+    tile = pl.BlockSpec((HALF, width), lambda step: (step, 0))
+    named = pl.BlockSpec((HALF, slots), lambda step: (step, 0))
+    total, sharp, gain_grad = pl.pallas_call(
+        combine_kernel,
+        grid=(rows // HALF,),
+        in_specs=[
+            named, whole((slots, width)), named, whole((slots, width)), tile, whole((1, width)), tile,
+        ],
+        out_specs=[tile, tile, whole((8, width))],
+        out_shape=[
+            jax.ShapeDtypeStruct((rows, width), jnp.float32),
+            jax.ShapeDtypeStruct((rows, width), jnp.bfloat16),
+            jax.ShapeDtypeStruct((8, width), jnp.float32),
+        ],
+        compiler_params=pltpu.CompilerParams(vmem_limit_bytes=VMEM_LIMIT),
+        cost_estimate=pl.CostEstimate(
+            flops=4 * rows * slots * width,
+            bytes_accessed=4 * slots * width + 12 * rows * width,
+            transcendentals=rows,
+        ),
+        name="combine",
+    )(first, first_rows, last, last_rows, resid, gain[None, :], out_grad)
+    return total, sharp, gain_grad
 
 
 def rms_norm(values, gain):
@@ -631,6 +774,10 @@
 
 def joined(keep, got):
     return keep.astype(jnp.float32) + got.astype(jnp.float32)
+
+
+def joined_low(keep, got):
+    return joined(keep, got).astype(jnp.bfloat16)
 
 
 def spread_sum(pieces, axis_name):
@@ -639,11 +786,17 @@
     return pieces[0]
 
 
+def spread_rest(pieces, axis_name):
+    for bit in range(1, bit_count(axis_name)):
+        pieces = joined(*halved(pieces, axis_name, bit))
+    return pieces[0]
+
+
 def collect(piece, axis_name):
     pieces = piece[None]
     for bit in reversed(range(1, bit_count(axis_name))):
         pieces = jnp.concatenate([pieces, swap(pieces, axis_name, bit)], axis=0)
-    return pieces, swap(pieces, axis_name, 0)
+    return pieces
 
 
 def swap(value, axis_name, bit):
@@ -655,38 +808,58 @@
     return (lax.axis_index(axis_name) >> bit) & 1
 
 
+def bit_groups(axis_name):
+    bits = list(range(bit_count(axis_name)))
+    return [tuple(bits[:1])] + [tuple(bits[low : low + 2]) for low in range(1, len(bits), 2)]
+
+
+def send_over(value, axis_name, group, offset):
+    mask = sum(((offset >> place) & 1) << bit for place, bit in enumerate(group))
+    count = lax.axis_size(axis_name)
+    return lax.ppermute(value, axis_name, [(i, i ^ mask) for i in range(count)])
+
+
+def group_sum(value, axis_name):
+    for group in bit_groups(axis_name):
+        parts = [send_over(value, axis_name, group, m) for m in range(1, 2 ** len(group))]
+        value = sum(parts, value)
+    return value
+
+
 def scatter_sum(pieces, axis_name, order):
-    count = (pieces.shape[0] - 1).bit_length()
-    bits = sorted(order, reverse=True)
-    if count > len(bits):
-        bits = list(range(count))[::-1]
-    total = pieces.reshape((2,) * count + pieces.shape[1:])
-    for bit in order:
-        dim = bits.index(bit)
-        bits.remove(bit)
-        mine = own_bit(axis_name, bit)
-        keep = lax.dynamic_index_in_dim(total, mine, dim, keepdims=False)
-        send = lax.dynamic_index_in_dim(total, 1 - mine, dim, keepdims=False)
-        got = swap(send.astype(jnp.bfloat16), axis_name, bit)
-        total = keep.astype(jnp.float32) + got.astype(jnp.float32)
+    bits = list(range(bit_count(axis_name)))[::-1]
+    total = pieces.reshape((2,) * len(bits) + pieces.shape[1:])
+    for group in order:
+        parts = []
+        for offset in range(2 ** len(group)):
+            part, left = total, list(bits)
+            for place, bit in enumerate(group):
+                dim = left.index(bit)
+                left.remove(bit)
+                index = own_bit(axis_name, bit) ^ ((offset >> place) & 1)
+                part = lax.dynamic_index_in_dim(part, index, dim, keepdims=False)
+            if offset:
+                part = send_over(part.astype(jnp.bfloat16), axis_name, group, offset)
+            parts.append(part.astype(jnp.float32))
+        total = sum(parts[1:], parts[0])
+        bits = left
     return total
 
 
 def gather(value, axis_name, order, done=()):
     bits = list(done)
-    for bit in order:
+    for group in order:
         value = value.reshape((2,) * len(bits) + value.shape[value.ndim - 2 :])
-        bits = sorted(bits + [bit], reverse=True)
-        dim = bits.index(bit)
-        got = swap(value, axis_name, bit)
-        first = own_bit(axis_name, bit) == 0
-        value = jnp.stack([jnp.where(first, value, got), jnp.where(first, got, value)], axis=dim)
-    return value
-
-
-def butterfly(value, axis_name):
-    for bit in range(bit_count(axis_name)):
-        value = value + swap(value, axis_name, bit)
+        size = 2 ** len(group)
+        parts = [value] + [send_over(value, axis_name, group, m) for m in range(1, size)]
+        for place, bit in enumerate(group):
+            flip = own_bit(axis_name, bit) == 1
+            parts = [jnp.where(flip, parts[m ^ (1 << place)], parts[m]) for m in range(size)]
+        stacked = jnp.stack(parts).reshape((2,) * len(group) + value.shape)
+        now = sorted(group, reverse=True) + bits
+        bits = sorted(now, reverse=True)
+        order_of = [now.index(bit) for bit in bits]
+        value = stacked.transpose(order_of + list(range(len(bits), stacked.ndim)))
     return value
 
 
@@ -695,21 +868,24 @@
 
 
 def scatter_rows(rows, axis_name):
-    bits = list(range(bit_count(axis_name)))
+    groups = bit_groups(axis_name)
     parts = lax.axis_size(axis_name)
-    orders = [bits[turn:] + bits[:turn] for turn in (0, 1)]
+    middle = rows.shape[0] // EXTRA // 2 * EXTRA
+    orders = [groups[turn:] + groups[:turn] for turn in (0, 1)]
     owned = [
-        scatter_sum(half.reshape((parts, -1) + rows.shape[1:]), axis_name, order).astype(jnp.bfloat16)
-        for half, order in zip(jnp.split(rows, 2, axis=0), orders)
+        scatter_sum(half.reshape((parts, -1) + rows.shape[1:]), axis_name, order).astype(
+            jnp.bfloat16
+        )
+        for half, order in zip((rows[:middle], rows[middle:]), orders)
     ]
     return owned, orders
 
 
 def gather_rows(begun, orders, axis_name):
-    halves = [
-        gather(part, axis_name, order[::-1][1:], order[::-1][:1])
-        for part, order in zip(begun, orders)
-    ]
+    halves = []
+    for part, order in zip(begun, orders):
+        done = sorted(order[-1], reverse=True)
+        halves.append(gather(part, axis_name, order[::-1][1:], done))
     return jnp.concatenate([half.reshape(-1, half.shape[-1]) for half in halves], axis=0)
 
 
@@ -736,12 +912,9 @@
     expert_count = router.shape[1]
     capacity = max(2, 4 * own_rows // expert_count)
 
-    route_hot = (routes[:, :, None] == jnp.arange(expert_count, dtype=jnp.int32)).astype(jnp.int32)
-    counts = jnp.sum(route_hot, axis=1)
-    before = jnp.cumsum(counts, axis=0) - counts
-    slot_rank = jnp.sum(route_hot * before[:, None, :], axis=-1)
     expert_index = lax.axis_index("expert")
-    slot_index = routes * capacity + slot_rank
+    grad_slots, slot_index = place_rows(routes, out_grad, expert_count, capacity)
+    slot_index = slot_index[:2].T
     half_slots = capacity // 2
 
     def named(slot_ids):
@@ -750,20 +923,6 @@
 
     slot_ids = jnp.arange(expert_count * capacity, dtype=jnp.int32)
     split_ids = slot_ids.reshape(expert_count, 2, half_slots)
-    extra = jnp.full((expert_count, SPARE), -1, jnp.int32)
-    long_ids = jnp.concatenate([slot_ids.reshape(expert_count, capacity), extra], axis=1)
-    grad_slots = mul(named(long_ids.reshape(-1)), out_grad, 0, 0).astype(jnp.bfloat16)
-    other_ids = jnp.sum(
-        jnp.where(
-            slot_index[:, :, None] == slot_ids[None, None, :], routes[:, ::-1, None] + 1, 0
-        ),
-        axis=(0, 1),
-    ).astype(jnp.bfloat16)
-    grad_slots = lax.dynamic_update_slice(
-        grad_slots.reshape(expert_count, capacity + SPARE, width),
-        other_ids.reshape(expert_count, 1, capacity),
-        (0, capacity, 0),
-    )
     landed = exchange(grad_slots)
     tokens, _ = lax.optimization_barrier((tokens, grad_slots))
     place = tensor_index.astype(jnp.int32)[None]
@@ -777,8 +936,7 @@
     branch = spread_sum(branch.reshape(n_tensor, own_rows, width), "tensor")
     own_tokens = lax.dynamic_slice_in_dim(tokens, tensor_index * own_rows, own_rows, 0)
     resid = own_tokens.astype(jnp.float32) + branch
-    normed_two, norm2_pull = jax.vjp(rms_norm, resid, norm2_gain)
-    hidden_two = normed_two.astype(jnp.bfloat16)
+    hidden_two = rms_norm(resid, norm2_gain).astype(jnp.bfloat16)
     outgoing = [mul(half, hidden_two, 0, 0).astype(jnp.bfloat16) for half in halves]
     outgoing, landed, expert_in = lax.optimization_barrier((outgoing, landed, expert_in))
     outgoing = [rows.reshape(expert_count, half_slots, width) for rows in outgoing]
@@ -806,82 +964,78 @@
         place, last_rows, act_grads, hot_gap, weights_in, router_wide, 1, kept
     )
     act = act.reshape(shards, -1, hidden)
-    grad_w_out = out_weights_of(act, landed)
-    sent_two, grad_w_out, grad_pre = lax.optimization_barrier((sent_two, grad_w_out, grad_pre))
+    out_send, out_keep = out_weights_of(act, landed)
+    sent_two, out_send, out_keep, grad_pre = lax.optimization_barrier(
+        (sent_two, out_send, out_keep, grad_pre)
+    )
     grad_sent_two = exchange(sent_two)
-    grad_w_out = spread_sum(grad_w_out, "tensor")
-    grad_w_in, router_part = in_weights_of(first_rows, last_rows, grad_pre, logit_grads)
+    out_half = joined_low(out_keep, swap(out_send, "tensor", 0))
+    out_half, grad_pre = lax.optimization_barrier((out_half, grad_pre))
+    grad_w_out = spread_rest(out_half, "tensor")
+    in_send, in_keep, router_part = in_weights_of(first_rows, last_rows, grad_pre, logit_grads)
     router_part = router_part[:, :expert_count]
-    act, grad_w_in = lax.optimization_barrier((act, grad_w_in))
+    count = 2 + expert_count
+    extra = -(-(count + 1) // EXTRA) * EXTRA - count - 1
+    blank = jnp.zeros((1, width), jnp.float32)
+    small = jnp.concatenate(
+        [blank, blank, blank, router_part.T, jnp.zeros((extra, width), jnp.float32)], axis=0
+    )
+    act, in_send, in_keep, small = lax.optimization_barrier((act, in_send, in_keep, small))
+    in_got = swap(in_send, "tensor", 0)
     result = result_of(place, act, weights_out)
     grad_sent_one, grad_sent_two, result, dispatch, grad_w_out = lax.optimization_barrier(
         (grad_sent_one, grad_sent_two, result, dispatch, grad_w_out)
     )
-    grad_in = out_grad.astype(jnp.float32)
-    grad_hidden_two = mul(halves[0], grad_sent_one.reshape(-1, width), 1, 0) + mul(
-        halves[1], grad_sent_two.reshape(-1, width), 1, 0
-    )
-    grad_resid_norm, gain_two_part = norm2_pull(grad_hidden_two)
-    grad_resid = grad_in + grad_resid_norm
-    grad_sharp = grad_resid.astype(jnp.bfloat16)
-    grad_sharp, result = lax.optimization_barrier((grad_sharp, result))
+    grad_resid, grad_sharp, gain_two_part = combine(
+        halves[0],
+        grad_sent_one.reshape(-1, width),
+        halves[1],
+        grad_sent_two.reshape(-1, width),
+        resid,
+        norm2_gain,
+        out_grad,
+    )
     came_back = exchange(result.reshape(expert_count, capacity, width)).reshape(-1, width)
-    near_grad, away_grad = collect(grad_sharp, "tensor")
     tensor_bits = bit_count("tensor")
-    for bit in range(tensor_bits - 1):
-        grad_w_in = joined(*halved(grad_w_in, "tensor", bit))
-    near_grad, away_grad, grad_w_in = lax.optimization_barrier((near_grad, away_grad, grad_w_in))
+    grad_w_in = joined_low(in_keep, in_got)
+    for bit in range(1, tensor_bits - 1):
+        grad_w_in = joined_low(*halved(grad_w_in, "tensor", bit))
+    near_grad = collect(grad_sharp, "tensor")
+    near_grad, grad_w_in = lax.optimization_barrier((near_grad, grad_w_in))
+    away_grad = swap(near_grad, "tensor", 0)
     grad_w_in, grad_w_in_got = halved(grad_w_in, "tensor", tensor_bits - 1)
 
-    tokens_part, qkv_part, out_part, gain_one_part, bias_part = attend_back(
+    tokens_part, weights_part = attend_back(
         place, tokens, lengths, norm1_gain, qkv_flat, attn_out, rel_bias,
-        projected, mixed, log_total, near_grad, away_grad,
-    )
-    tokens_part, qkv_part, out_part, gain_one_part, bias_part, came_back, grad_w_in_got = (
-        lax.optimization_barrier(
-            (tokens_part, qkv_part, out_part, gain_one_part, bias_part, came_back, grad_w_in_got)
-        )
+        projected, mixed, log_total, near_grad, away_grad, small, gain_two_part,
+    )
+    tokens_part, weights_part, came_back, grad_w_in_got = lax.optimization_barrier(
+        (tokens_part, weights_part, came_back, grad_w_in_got)
     )
     tokens_shared = lax.psum_scatter(tokens_part, "tensor", scatter_dimension=0, tiled=True)
-    weights_part = jnp.concatenate([qkv_part, out_part], axis=0).astype(jnp.bfloat16)
-    bias_slots = lax.dynamic_update_slice_in_dim(
-        jnp.zeros((n_tensor * head_count, bucket_count), jnp.float32),
-        bias_part,
-        tensor_index * head_count,
-        0,
-    )
-    small = jnp.concatenate(
-        [gain_one_part, gain_two_part, router_part.T.reshape(-1), bias_slots.reshape(-1)]
-    )
-    small = butterfly(small, "tensor")
     owned, orders = scatter_rows(weights_part, "expert")
-    owned, small = lax.optimization_barrier((owned, small))
-    small = butterfly(small, "expert")
+    owned = lax.optimization_barrier(owned)
     begun = [gather(own, "expert", order[::-1][:1]) for own, order in zip(owned, orders)]
-    begun, came_back, grad_w_in = lax.optimization_barrier((begun, came_back, grad_w_in))
+    begun, came_back, grad_w_in, tokens_shared = lax.optimization_barrier(
+        (begun, came_back, grad_w_in, tokens_shared)
+    )
     weights_total = gather_rows(begun, orders, "expert").astype(jnp.float32)
     output = resid + jnp.dot(dispatch, came_back, preferred_element_type=jnp.float32)
     grad_tokens = grad_resid + tokens_shared.astype(jnp.float32)
     grad_w_in = joined(grad_w_in, grad_w_in_got)
-    count = 2 + expert_count
+    low = 4 * inner
+    bias_total = weights_total[low + 1, : rel_bias.size].reshape(rel_bias.shape)
+    small = weights_total[low : low + count + 1]
+    small = group_sum(jnp.concatenate([small[:1], small[2:]], axis=0), "tensor")
     columns = lax.dynamic_slice_in_dim(
-        small[: count * width].reshape(count, width),
-        tensor_index * (width // n_tensor),
-        width // n_tensor,
-        1,
-    )
-    bias_total = lax.dynamic_slice_in_dim(
-        small[count * width :].reshape(n_tensor * head_count, bucket_count),
-        tensor_index * head_count,
-        head_count,
-        0,
+        small, tensor_index * (width // n_tensor), width // n_tensor, 1
     )
     return (
         output,
         grad_tokens,
         columns[0],
         weights_total[: 3 * inner].reshape(3, inner, width).transpose(2, 0, 1),
-        weights_total[3 * inner :],
+        weights_total[3 * inner : 4 * inner],
         bias_total,
         columns[1],
         columns[2:].T,

time: 440 us -> 428 us (0.973)
  Pallas kernels: 163 us -> 173 us
  waiting for transfers between devices: 123 us -> 113 us
  matrix products: 20.3 us -> 10.5 us
  other arithmetic: 34.9 us -> 25.2 us
  starting transfers between devices: 52.7 us -> 59.7 us
    ppermute x25 -> x8, waiting for transfers between devices: 72.2 us -> 41.5 us  [swap(): lax.ppermute(value, axis_name, [(i, i ^ 1 << bit) for i in range(count)])]
    ppermute x0 -> x18, starting transfers between devices: none -> 22.9 us  [send_over(): return lax.ppermute(value, axis_name, [(i, i ^ mask) for i in range(count)])]
    ppermute x0 -> x18, waiting for transfers between devices: none -> 21.6 us  [send_over(): return lax.ppermute(value, axis_name, [(i, i ^ mask) for i in range(count)])]
    ppermute x25 -> x8, starting transfers between devices: 19.9 us -> 4.34 us  [swap(): lax.ppermute(value, axis_name, [(i, i ^ 1 << bit) for i in range(count)])]
    dot_general x5 -> x2, matrix products: 15.3 us -> 5.04 us  [mul(): lax.dot_general(left, right, (((left_dim,), (right_dim,)), ((), ())), pre...]
    pallas_call x0 -> x2, Pallas kernels: none -> 9.18 us  [the longest x1 4.8 us: combine(): pl.pallas_call(combine_kernel, grid=(rows // HALF,), in_specs=[named, who...]
    slice x6 -> x3, local copies, waits for them, and re-layouts: 11.8 us -> 5.35 us  [halved(): pieces[half:].astype(jnp.bfloat16)]
    add x4 -> x2, other arithmetic: 9.16 us -> 3.38 us  [joined(): return keep.astype(jnp.float32) + got.astype(jnp.float32)]
  transfers between devices with their start and end apart: 34 -> 35, of which waited for: 18 -> 18; matrix products, arithmetic and copies ran while one was open for 15% -> 11% of each run, Pallas kernels for 37% -> 41%
where the time goes in v5:
time: 428 us; the launch traced here: 419 us
  Pallas kernels  173 us (40%)
  waiting for transfers between devices  113 us (26%)
  starting transfers between devices  59.7 us (14%)
  other arithmetic  25.2 us (6%)
  local copies, waits for them, and re-layouts  22.9 us (5%)
  between operations  14.9 us (3%)
  matrix products  10.5 us (2%)
    all_to_all x6, waiting for transfers between devices, exchange(): lax.all_to_all(pieces, 'expert', split_axis=0, concat_axis=0, tiled=True)  48.9 us
    pallas_call x2, Pallas kernels, serve(): pl.pallas_call(functools.partial(expert_kernel, sub=sub), grid_spec=pltpu...  43.9 us
    ppermute x8, waiting for transfers between devices, swap(): lax.ppermute(value, axis_name, [(i, i ^ 1 << bit) for i in range(count)])  41.5 us
    pallas_call x1, Pallas kernels, attend_back(): pl.pallas_call(functools.partial(backward_kernel, head_count=head_count,...  36.1 us
    all_to_all x6, starting transfers between devices, exchange(): lax.all_to_all(pieces, 'expert', split_axis=0, concat_axis=0, tiled=True)  32.3 us
    ppermute x18, starting transfers between devices, send_over(): return lax.ppermute(value, axis_name, [(i, i ^ mask) for i in range(count)])  22.9 us
    pallas_call x1, Pallas kernels, attend(): pl.pallas_call(functools.partial(forward_kernel, head_count=head_count, h...  22.9 us
    ppermute x18, waiting for transfers between devices, send_over(): return lax.ppermute(value, axis_name, [(i, i ^ mask) for i in range(count)])  21.6 us
  transfers between devices with their start and end apart: 35, of which 18 were waited for; matrix products, arithmetic and copies ran while one was open for 11% of the time, Pallas kernels for 41%

profile of v5, /device:TPU:0, one launch (start us, length us, event | category | flops | bytes accessed | tf_op | source)
XLA Modules:
  0.0 419.3 jit_solution(7884795184599478338)
XLA Ops:
  9.7 4.4 %place_rows.1 = (bf16[8,272,768]{2,1,0:T(8,128)(2,1)S(1)}, s32[8,512]{1,0:T(8,128)S(1)}) custom-call(s32[2,512]{1,0:T(2,128)S(1)} %bitcast.125, bf16[512,768]{1,0:T(8,128)(2,1)S(1)} %copy-done.6), custom_call_target="tpu_custom_call" | custom-call | flops 1610612736 | bytes 3145728 | tf_op jit(solution)/shard_map/place_rows/pallas_call | solution.py:687
  15.8 7.4 %all-to-all-start = ((bf16[8,272,768]{2,1,0:T(8,128)(2,1)}), bf16[8,272,768]{2,1,0:T(8,128)(2,1)S(1)}, u32[]{:S(2)}, u32[]{:S(2)}) async-start(bf16[8,272,768]{2,1,0:T(8,128)(2,1)} %copy-done.1), calls=%async_computation | async-start | bytes 6684672 | tf_op jit(solution)/shard_map/all_to_all | solution.py:767
  25.8 22.9 %attend_forward.1 = (bf16[2048,768]{1,0:T(8,128)(2,1)}, bf16[576,2048]{1,0:T(8,128)(2,1)S(1)}, bf16[192,2048]{1,0:T(8,128)(2,1)S(1)}, f32[8,2048]{1,0:T(8,128)S(1)}) custom-call(s32[1]{0:T(128)} %bitcast.1.place_ref, s32[1,8]{1,0:T(1,128)S(1)} %copy-done.13, bf16[2048,768]{1,0:T(8,128)(2,1)} %tokens_ref.1, f32[1,768]{1,0:T(1,128)S(1)} %broadcast_in_dim.13.gain_ref, ...), custom_call_target="tpu_custom_call" | custom-call | flops 3623878656 | bytes 15728640 | tf_op jit(solution)/shard_map/attend_forward/pallas_call | solution.py:260
  48.7 3.2 fusion.21
  52.0 3.4 collective-permute-done
  61.3 17.0 %collective-permute-done.1 = bf16[1,512,768]{2,1,0:T(8,128)(2,1)} collective-permute-done((bf16[1,512,768]{2,1,0:T(8,128)(2,1)}, bf16[1,512,768]{2,1,0:T(8,128)(2,1)}, u32[]{:S(2)}, u32[]{:S(2)}) %collective-permute-start.1) | collective-permute-done | bytes 786464 | tf_op jit(solution)/shard_map/ppermute | solution.py:804
  80.5 2.5 convolution_convert_fusion.1
  85.6 12.6 %all-to-all-done.rows_ref.landed_ref = bf16[8,272,768]{2,1,0:T(8,128)(2,1)S(1)} async-done(((bf16[8,272,768]{2,1,0:T(8,128)(2,1)}), bf16[8,272,768]{2,1,0:T(8,128)(2,1)S(1)}, u32[]{:S(2)}, u32[]{:S(2)}) %all-to-all-start) | async-done | bytes 3342368 | tf_op jit(solution)/shard_map/all_to_all | solution.py:767
  98.2 4.8 %all-to-all-start.1 = ((bf16[8,128,768]{2,1,0:T(8,128)(2,1)}), bf16[8,128,768]{2,1,0:T(8,128)(2,1)}, u32[]{:S(2)}, u32[]{:S(2)}) async-start(bf16[8,128,768]{2,1,0:T(8,128)(2,1)} %bitcast.148), calls=%async_computation.1 | async-start | bytes 3145728 | tf_op jit(solution)/shard_map/all_to_all | solution.py:767
  104.2 15.5 %act_grads.1 = bf16[4,2048,768]{2,1,0:T(8,128)(2,1)} custom-call(s32[1]{0:T(128)} %bitcast.1.place_ref, bf16[8,272,768]{2,1,0:T(8,128)(2,1)S(1)} %all-to-all-done.rows_ref.landed_ref, bf16[4,768,768]{2,1,0:T(8,128)(2,1)} %all-gather.3.cloned.1.call-done.weights_ref), custom_call_target="tpu_custom_call" | custom-call | flops 9663676416 | bytes 12582912 | tf_op jit(solution)/shard_map/act_grads/pallas_call | solution.py:500
  119.7 20.0 %all-to-all-done.1.rows_ref.first_ref = bf16[8,128,768]{2,1,0:T(8,128)(2,1)} async-done(((bf16[8,128,768]{2,1,0:T(8,128)(2,1)}), bf16[8,128,768]{2,1,0:T(8,128)(2,1)}, u32[]{:S(2)}, u32[]{:S(2)}) %all-to-all-start.1) | async-done | bytes 1572896 | tf_op jit(solution)/shard_map/all_to_all | solution.py:767
  139.6 3.6 all-to-all-start.3
  143.5 22.1 %expert_middle.2 = (bf16[8,128,768]{2,1,0:T(8,128)(2,1)S(1)}, bf16[4,8,2,128,768]{4,3,2,1,0:T(8,128)(2,1)}, bf16[4,8,2,128,768]{4,3,2,1,0:T(8,128)(2,1)}, bf16[8,2,128,128]{3,2,1,0:T(8,128)(2,1)S(1)}) custom-call(s32[1]{0:T(128)} %bitcast.1.place_ref, bf16[8,128,768]{2,1,0:T(8,128)(2,1)} %all-to-all-done.1.rows_ref.first_ref, ...), custom_call_target="tpu_custom_call" | custom-call | flops 9663676416 | bytes 18874368 | tf_op jit(solution)/shard_map/expert_middle/pallas_call | solution.py:456
  166.7 13.7 %all-to-all-done.3.rows_ref.last_ref = bf16[8,128,768]{2,1,0:T(8,128)(2,1)S(1)} async-done(((bf16[8,128,768]{2,1,0:T(8,128)(2,1)}), bf16[8,128,768]{2,1,0:T(8,128)(2,1)S(1)}, u32[]{:S(2)}, u32[]{:S(2)}) %all-to-all-start.3) | async-done | bytes 1572896 | tf_op jit(solution)/shard_map/all_to_all | solution.py:767
  180.4 4.3 %all-to-all-start.2 = ((bf16[8,128,768]{2,1,0:T(8,128)(2,1)}), bf16[8,128,768]{2,1,0:T(8,128)(2,1)}, u32[]{:S(2)}, u32[]{:S(2)}) async-start(bf16[8,128,768]{2,1,0:T(8,128)(2,1)} %copy-done.5), calls=%async_computation.2 | async-start | bytes 3145728 | tf_op jit(solution)/shard_map/all_to_all | solution.py:767
  184.7 21.8 %expert_middle.3 = (bf16[8,128,768]{2,1,0:T(8,128)(2,1)S(1)}, bf16[4,8,2,128,768]{4,3,2,1,0:T(8,128)(2,1)}, bf16[4,8,2,128,768]{4,3,2,1,0:T(8,128)(2,1)}, bf16[8,2,128,128]{3,2,1,0:T(8,128)(2,1)S(1)}) custom-call(s32[1]{0:T(128)} %bitcast.1.place_ref, ...), custom_call_target="tpu_custom_call", output_to_operand_aliasing={{1}: (6, {}), {2}: (7, {}), {3}: (8, {})} | custom-call | flops 9663676416 | bytes 18874368 | tf_op jit(solution)/shard_map/expert_middle/pallas_call | solution.py:456
  207.7 15.1 %out_weights.1 = (bf16[2,768,768]{2,1,0:T(8,128)(2,1)}, bf16[2,768,768]{2,1,0:T(8,128)(2,1)S(1)}) custom-call(bf16[4,2048,768]{2,1,0:T(8,128)(2,1)} %bitcast.126, bf16[8,272,768]{2,1,0:T(8,128)(2,1)} %copy-done), custom_call_target="tpu_custom_call" | custom-call | tf_op jit(solution)/shard_map/out_weights/pallas_call | solution.py:587
  224.2 6.1 %all-to-all-start.4 = ((bf16[8,128,768]{2,1,0:T(8,128)(2,1)}), bf16[8,128,768]{2,1,0:T(8,128)(2,1)}, u32[]{:S(2)}, u32[]{:S(2)}) async-start(bf16[8,128,768]{2,1,0:T(8,128)(2,1)} %copy-done.4), calls=%async_computation.4 | async-start | bytes 3145728 | tf_op jit(solution)/shard_map/all_to_all | solution.py:767
  230.3 2.9 add_convert_fusion.1
  239.4 15.8 %in_weights.1 = (bf16[2,768,768]{2,1,0:T(8,128)(2,1)}, bf16[2,768,768]{2,1,0:T(8,128)(2,1)}, f32[768,128]{1,0:T(8,128)S(1)}) custom-call(bf16[8,128,768]{2,1,0:T(8,128)(2,1)} %all-to-all-done.1.rows_ref.first_ref, bf16[8,128,768]{2,1,0:T(8,128)(2,1)S(1)} %all-to-all-done.3.rows_ref.last_ref, bf16[4,8,2,128,768]{4,3,2,1,0:T(8,128)(2,1)} %get-tuple-element.98.grads_ref, ...), custom_call_target="tpu_custom_call" | custom-call | tf_op jit(solution)/shard_map/in_weights/pallas_call | solution.py:627
  255.6 14.9 %expert_result.1 = bf16[2048,768]{1,0:T(8,128)(2,1)} custom-call(s32[1]{0:T(128)} %bitcast.1.place_ref, bf16[4,2048,768]{2,1,0:T(8,128)(2,1)} %bitcast.127, bf16[4,768,768]{2,1,0:T(8,128)(2,1)} %all-gather.3.cloned.1.call-done.weights_ref), custom_call_target="tpu_custom_call" | custom-call | tf_op jit(solution)/shard_map/expert_result/pallas_call | solution.py:533
  270.4 3.0 add_bitcast_fusion
  273.4 6.1 %all-to-all-start.5 = ((bf16[8,256,768]{2,1,0:T(8,128)(2,1)}), bf16[8,256,768]{2,1,0:T(8,128)(2,1)}, u32[]{:S(2)}, u32[]{:S(2)}) async-start(bf16[8,256,768]{2,1,0:T(8,128)(2,1)} %bitcast.24), calls=%async_computation.5 | async-start | bytes 6291456 | tf_op jit(solution)/shard_map/all_to_all | solution.py:767
  281.1 4.8 %combine.1 = (f32[512,768]{1,0:T(8,128)S(1)}, bf16[512,768]{1,0:T(8,128)(2,1)S(1)}, f32[8,768]{1,0:T(8,128)S(1)}) custom-call(bf16[512,1024]{1,0:T(8,128)(2,1)S(1)} %get-tuple-element.164.first_ref, bf16[1024,768]{1,0:T(8,128)(2,1)} %bitcast.21.first_rows_ref, bf16[512,1024]{1,0:T(8,128)(2,1)S(1)} %get-tuple-element.165.last_ref, ...), custom_call_target="tpu_custom_call" | custom-call | flops 1610612736 | bytes 7864320 | tf_op jit(solution)/shard_map/combine/pallas_call | solution.py:739
  286.5 19.4 %collective-permute-done.4 = bf16[1,512,768]{2,1,0:T(8,128)(2,1)S(1)} collective-permute-done((bf16[1,512,768]{2,1,0:T(8,128)(2,1)S(1)}, bf16[1,512,768]{2,1,0:T(8,128)(2,1)S(1)}, u32[]{:S(2)}, u32[]{:S(2)}) %collective-permute-start.4) | collective-permute-done | bytes 786464 | tf_op jit(solution)/shard_map/ppermute | solution.py:804
  311.4 36.1 %attend_backward.1 = (bf16[2048,768]{1,0:T(8,128)(2,1)}, bf16[832,768]{1,0:T(8,128)(2,1)S(1)}) custom-call(s32[1]{0:T(128)} %bitcast.1.place_ref, s32[1,8]{1,0:T(1,128)S(1)} %copy-done.13, bf16[2048,768]{1,0:T(8,128)(2,1)} %tokens_ref.1, f32[1,768]{1,0:T(1,128)S(1)} %broadcast_in_dim.13.gain_ref, bf16[576,768]{1,0:T(8,128)(2,1)S(1)} %bitcast.124, ...), custom_call_target="tpu_custom_call" | custom-call | flops 7851737088 | bytes 22020096 | tf_op jit(solution)/shard_map/attend_backward/pallas_call | solution.py:318
  347.6 2.6 all-to-all-done.5
  357.1 3.4 collective-permute-done.14
  360.6 7.1 %collective-permute-done.13 = bf16[2,56,768]{2,1,0:T(8,128)(2,1)} collective-permute-done((bf16[2,56,768]{2,1,0:T(8,128)(2,1)}, bf16[2,56,768]{2,1,0:T(8,128)(2,1)}, u32[]{:S(2)}, u32[]{:S(2)}) %collective-permute-start.13) | collective-permute-done | bytes 172064 | tf_op jit(solution)/shard_map/ppermute | solution.py:819
  378.9 2.5 collective-permute-start.16
  394.1 5.5 %convolution_add_fusion = f32[512,768]{1,0:T(8,128)} fusion(f32[512,768]{1,0:T(8,128)S(1)} %copy-done.21, bf16[512,2048]{1,0:T(8,128)(2,1)} %fusion.1, bf16[2048,768]{1,0:T(8,128)(2,1)} %bitcast.25), kind=kOutput, calls=%fused_computation.25 | convolution fusion | flops 1611005952 | bytes 8388608 | tf_op jit(solution)/shard_map/dot_general | solution.py:1023
  399.5 3.0 convert_add_fusion.1
  (196 shorter events, 76.7 us)
Async XLA Ops:
  7.2 97.0 %all-gather.3.cloned.1.call-start = ((), (), s32[]{:S(2)}) async-start(), calls=%async_computation.7 | async-start | bytes 5898240 | tf_op jit(solution)/shard_map/all_gather | solution.py:945
  15.8 82.3 %all-to-all-start = ((bf16[8,272,768]{2,1,0:T(8,128)(2,1)}), bf16[8,272,768]{2,1,0:T(8,128)(2,1)S(1)}, u32[]{:S(2)}, u32[]{:S(2)}) async-start(bf16[8,272,768]{2,1,0:T(8,128)(2,1)} %copy-done.1), calls=%async_computation | async-start | bytes 6684672 | tf_op jit(solution)/shard_map/all_to_all | solution.py:767
  23.2 116.4 %all-gather.5.cloned.1.call-start = ((), (), s32[]{:S(2)}) async-start(), calls=%async_computation.8 | async-start | bytes 5898240 | tf_op jit(solution)/shard_map/all_gather | solution.py:946
  58.4 19.9 %collective-permute-start.1 = (bf16[1,512,768]{2,1,0:T(8,128)(2,1)}, bf16[1,512,768]{2,1,0:T(8,128)(2,1)}, u32[]{:S(2)}, u32[]{:S(2)}) collective-permute-start(bf16[1,512,768]{2,1,0:T(8,128)(2,1)} %slice.185), channel_id=1, source_target_pairs={{0,2},{1,3},{2,0},{3,1},{4,6},{5,7},{6,4},{7,5},{8,10},{9,11},{10,... | collective-permute-start | bytes 2359304 | tf_op jit(solution)/shard_map/ppermute | solution.py:804
  98.2 41.4 %all-to-all-start.1 = ((bf16[8,128,768]{2,1,0:T(8,128)(2,1)}), bf16[8,128,768]{2,1,0:T(8,128)(2,1)}, u32[]{:S(2)}, u32[]{:S(2)}) async-start(bf16[8,128,768]{2,1,0:T(8,128)(2,1)} %bitcast.148), calls=%async_computation.1 | async-start | bytes 3145728 | tf_op jit(solution)/shard_map/all_to_all | solution.py:767
  139.6 40.8 %all-to-all-start.3 = ((bf16[8,128,768]{2,1,0:T(8,128)(2,1)}), bf16[8,128,768]{2,1,0:T(8,128)(2,1)S(1)}, u32[]{:S(2)}, u32[]{:S(2)}) async-start(bf16[8,128,768]{2,1,0:T(8,128)(2,1)} %bitcast.147), calls=%async_computation.3 | async-start | bytes 3145728 | tf_op jit(solution)/shard_map/all_to_all | solution.py:767
  180.4 43.7 %all-to-all-start.2 = ((bf16[8,128,768]{2,1,0:T(8,128)(2,1)}), bf16[8,128,768]{2,1,0:T(8,128)(2,1)}, u32[]{:S(2)}, u32[]{:S(2)}) async-start(bf16[8,128,768]{2,1,0:T(8,128)(2,1)} %copy-done.5), calls=%async_computation.2 | async-start | bytes 3145728 | tf_op jit(solution)/shard_map/all_to_all | solution.py:767
  224.2 6.1 %collective-permute-start.2 = (bf16[2,768,768]{2,1,0:T(8,128)(2,1)}, bf16[2,768,768]{2,1,0:T(8,128)(2,1)}, u32[]{:S(2)}, u32[]{:S(2)}) collective-permute-start(bf16[2,768,768]{2,1,0:T(8,128)(2,1)} %get-tuple-element.96), channel_id=1, source_target_pairs={{0,1},{1,0},{2,3},{3,2},{4,5},{5,4},{6,7},{7,6},{8,9},{9,8},{10,11... | collective-permute-start | bytes 7077896 | tf_op jit(solution)/shard_map/ppermute | solution.py:804
  224.2 49.3 %all-to-all-start.4 = ((bf16[8,128,768]{2,1,0:T(8,128)(2,1)}), bf16[8,128,768]{2,1,0:T(8,128)(2,1)}, u32[]{:S(2)}, u32[]{:S(2)}) async-start(bf16[8,128,768]{2,1,0:T(8,128)(2,1)} %copy-done.4), calls=%async_computation.4 | async-start | bytes 3145728 | tf_op jit(solution)/shard_map/all_to_all | solution.py:767
  234.4 36.0 %collective-permute-start.3 = (bf16[1,768,768]{2,1,0:T(8,128)(2,1)}, bf16[1,768,768]{2,1,0:T(8,128)(2,1)}, u32[]{:S(2)}, u32[]{:S(2)}) collective-permute-start(bf16[1,768,768]{2,1,0:T(8,128)(2,1)} %slice.117), channel_id=1, source_target_pairs={{0,2},{1,3},{2,0},{3,1},{4,6},{5,7},{6,4},{7,5},{8,10},{9,11},{10,... | collective-permute-start | bytes 3538952 | tf_op jit(solution)/shard_map/ppermute | solution.py:804
  273.4 76.8 %all-to-all-start.5 = ((bf16[8,256,768]{2,1,0:T(8,128)(2,1)}), bf16[8,256,768]{2,1,0:T(8,128)(2,1)}, u32[]{:S(2)}, u32[]{:S(2)}) async-start(bf16[8,256,768]{2,1,0:T(8,128)(2,1)} %bitcast.24), calls=%async_computation.5 | async-start | bytes 6291456 | tf_op jit(solution)/shard_map/all_to_all | solution.py:767
  279.6 109.0 %reduce-scatter.2.cloned.1.call-start = ((), (), s32[]{:S(2)}) async-start(), calls=%async_computation.9 | async-start | bytes 3932160 | tf_op jit(solution)/shard_map/reduce_scatter | solution.py:1015
  279.6 26.5 %collective-permute-start.5 = (bf16[2,768,768]{2,1,0:T(8,128)(2,1)}, bf16[2,768,768]{2,1,0:T(8,128)(2,1)S(1)}, u32[]{:S(2)}, u32[]{:S(2)}) collective-permute-start(bf16[2,768,768]{2,1,0:T(8,128)(2,1)} %get-tuple-element.113), channel_id=1, source_target_pairs={{0,1},{1,0},{2,3},{3,2},{4,5},{5,4},{6,7},{7,6},{8,9},{9,8},{10,11... | collective-permute-start | bytes 7077896 | tf_op jit(solution)/shard_map/ppermute | solution.py:804
  285.9 20.0 %collective-permute-start.4 = (bf16[1,512,768]{2,1,0:T(8,128)(2,1)S(1)}, bf16[1,512,768]{2,1,0:T(8,128)(2,1)S(1)}, u32[]{:S(2)}, u32[]{:S(2)}) collective-permute-start(bf16[1,512,768]{2,1,0:T(8,128)(2,1)S(1)} %bitcast.121), channel_id=1, source_target_pairs={{0,2},{1,3},{2,0},{3,1},{4,6},{5,7},{6,4},{7,5},{8,10},{9,11},{10,... | collective-permute-start | bytes 2359304 | tf_op jit(solution)/shard_map/ppermute | solution.py:804
  308.1 39.5 %collective-permute-start.7 = (bf16[1,768,768]{2,1,0:T(8,128)(2,1)S(1)}, bf16[1,768,768]{2,1,0:T(8,128)(2,1)}, u32[]{:S(2)}, u32[]{:S(2)}) collective-permute-start(bf16[1,768,768]{2,1,0:T(8,128)(2,1)S(1)} %get-tuple-element.139), channel_id=1, source_target_pairs={{0,2},{1,3},{2,0},{3,1},{4,6},{5,7},{6,4},{7,5},{8,10},{9,11},{10,... | collective-permute-start | bytes 3538952 | tf_op jit(solution)/shard_map/ppermute | solution.py:804
  351.1 9.4 %collective-permute-start.14 = (bf16[2,56,768]{2,1,0:T(8,128)(2,1)}, bf16[2,56,768]{2,1,0:T(8,128)(2,1)}, u32[]{:S(2)}, u32[]{:S(2)}) collective-permute-start(bf16[2,56,768]{2,1,0:T(8,128)(2,1)} %get-tuple-element.145), channel_id=1, source_target_pairs={{0,24},{4,28},{8,16},{12,20},{16,8},{20,12},{24,0},{28,4},{1,25},{... | collective-permute-start | bytes 516104 | tf_op jit(solution)/shard_map/ppermute | solution.py:819
  353.4 14.3 %collective-permute-start.13 = (bf16[2,56,768]{2,1,0:T(8,128)(2,1)}, bf16[2,56,768]{2,1,0:T(8,128)(2,1)}, u32[]{:S(2)}, u32[]{:S(2)}) collective-permute-start(bf16[2,56,768]{2,1,0:T(8,128)(2,1)} %get-tuple-element.146), channel_id=1, source_target_pairs={{0,16},{4,20},{8,24},{12,28},{16,0},{20,4},{24,8},{28,12},{1,17},{... | collective-permute-start | bytes 516104 | tf_op jit(solution)/shard_map/ppermute | solution.py:819
  353.4 14.3 %collective-permute-start.12 = (bf16[2,56,768]{2,1,0:T(8,128)(2,1)}, bf16[2,56,768]{2,1,0:T(8,128)(2,1)}, u32[]{:S(2)}, u32[]{:S(2)}) collective-permute-start(bf16[2,56,768]{2,1,0:T(8,128)(2,1)} %get-tuple-element.144), channel_id=1, source_target_pairs={{0,8},{4,12},{8,0},{12,4},{16,24},{20,28},{24,16},{28,20},{1,9},{5... | collective-permute-start | bytes 516104 | tf_op jit(solution)/shard_map/ppermute | solution.py:819
  355.6 14.8 %collective-permute-start.8 = (bf16[2,2,48,768]{3,2,1,0:T(8,128)(2,1)S(1)}, bf16[2,2,48,768]{3,2,1,0:T(8,128)(2,1)S(1)}, u32[]{:S(2)}, u32[]{:S(2)}) collective-permute-start(bf16[2,2,48,768]{3,2,1,0:T(8,128)(2,1)S(1)} %dynamic-slice_bitcast_fusion), channel_id=1, source_target_pairs={{0,4},{4,0},{8,12},{12,8},{16,20},{20,16},{24,28},{28,24},{1,5},{5... | collective-permute-start | bytes 884744 | tf_op jit(solution)/shard_map/ppermute | solution.py:819
  368.9 6.1 %collective-permute-start.15 = (bf16[56,768]{1,0:T(8,128)(2,1)S(1)}, bf16[56,768]{1,0:T(8,128)(2,1)S(1)}, u32[]{:S(2)}, u32[]{:S(2)}) collective-permute-start(bf16[56,768]{1,0:T(8,128)(2,1)S(1)} %fusion.12), channel_id=1, source_target_pairs={{0,4},{4,0},{8,12},{12,8},{16,20},{20,16},{24,28},{28,24},{1,5},{5... | collective-permute-start | bytes 258056 | tf_op jit(solution)/shard_map/ppermute | solution.py:819
  370.5 6.5 %collective-permute-start.11 = (bf16[48,768]{1,0:T(8,128)(2,1)S(1)}, bf16[48,768]{1,0:T(8,128)(2,1)S(1)}, u32[]{:S(2)}, u32[]{:S(2)}) collective-permute-start(bf16[48,768]{1,0:T(8,128)(2,1)S(1)} %get-tuple-element.150), channel_id=1, source_target_pairs={{0,24},{4,28},{8,16},{12,20},{16,8},{20,12},{24,0},{28,4},{1,25},{... | collective-permute-start | bytes 221192 | tf_op jit(solution)/shard_map/ppermute | solution.py:819
  373.0 5.8 %collective-permute-start.10 = (bf16[48,768]{1,0:T(8,128)(2,1)S(1)}, bf16[48,768]{1,0:T(8,128)(2,1)S(1)}, u32[]{:S(2)}, u32[]{:S(2)}) collective-permute-start(bf16[48,768]{1,0:T(8,128)(2,1)S(1)} %get-tuple-element.151), channel_id=1, source_target_pairs={{0,16},{4,20},{8,24},{12,28},{16,0},{20,4},{24,8},{28,12},{1,17},{... | collective-permute-start | bytes 221192 | tf_op jit(solution)/shard_map/ppermute | solution.py:819
  373.1 5.8 %collective-permute-start.9 = (bf16[48,768]{1,0:T(8,128)(2,1)S(1)}, bf16[48,768]{1,0:T(8,128)(2,1)S(1)}, u32[]{:S(2)}, u32[]{:S(2)}) collective-permute-start(bf16[48,768]{1,0:T(8,128)(2,1)S(1)} %get-tuple-element.149), channel_id=1, source_target_pairs={{0,8},{4,12},{8,0},{12,4},{16,24},{20,28},{24,16},{28,20},{1,9},{5... | collective-permute-start | bytes 221192 | tf_op jit(solution)/shard_map/ppermute | solution.py:819
  378.9 6.3 %collective-permute-start.16 = (bf16[48,768]{1,0:T(8,128)(2,1)S(1)}, bf16[48,768]{1,0:T(8,128)(2,1)S(1)}, u32[]{:S(2)}, u32[]{:S(2)}) collective-permute-start(bf16[48,768]{1,0:T(8,128)(2,1)S(1)} %fusion.11), channel_id=1, source_target_pairs={{0,24},{4,28},{8,16},{12,20},{16,8},{20,12},{24,0},{28,4},{1,25},{... | collective-permute-start | bytes 221192 | tf_op jit(solution)/shard_map/ppermute | solution.py:819
  381.4 5.9 %collective-permute-start.17 = (bf16[48,768]{1,0:T(8,128)(2,1)S(1)}, bf16[48,768]{1,0:T(8,128)(2,1)S(1)}, u32[]{:S(2)}, u32[]{:S(2)}) collective-permute-start(bf16[48,768]{1,0:T(8,128)(2,1)S(1)} %fusion.11), channel_id=1, source_target_pairs={{0,16},{4,20},{8,24},{12,28},{16,0},{20,4},{24,8},{28,12},{1,17},{... | collective-permute-start | bytes 221192 | tf_op jit(solution)/shard_map/ppermute | solution.py:819
  381.4 5.9 %collective-permute-start.18 = (bf16[48,768]{1,0:T(8,128)(2,1)S(1)}, bf16[48,768]{1,0:T(8,128)(2,1)S(1)}, u32[]{:S(2)}, u32[]{:S(2)}) collective-permute-start(bf16[48,768]{1,0:T(8,128)(2,1)S(1)} %fusion.11), channel_id=1, source_target_pairs={{0,8},{4,12},{8,0},{12,4},{16,24},{20,28},{24,16},{28,20},{1,9},{5... | collective-permute-start | bytes 221192 | tf_op jit(solution)/shard_map/ppermute | solution.py:819
  383.3 4.5 %collective-permute-start.19 = (bf16[56,768]{1,0:T(8,128)(2,1)S(1)}, bf16[56,768]{1,0:T(8,128)(2,1)S(1)}, u32[]{:S(2)}, u32[]{:S(2)}) collective-permute-start(bf16[56,768]{1,0:T(8,128)(2,1)S(1)} %fusion.8), channel_id=1, source_target_pairs={{0,4},{4,0},{8,12},{12,8},{16,20},{20,16},{24,28},{28,24},{1,5},{5... | collective-permute-start | bytes 258056 | tf_op jit(solution)/shard_map/ppermute | solution.py:819
  388.5 15.3 %collective-permute-start.21 = (bf16[2,56,768]{2,1,0:T(8,128)(2,1)}, bf16[2,56,768]{2,1,0:T(8,128)(2,1)S(1)}, u32[]{:S(2)}, u32[]{:S(2)}) collective-permute-start(bf16[2,56,768]{2,1,0:T(8,128)(2,1)} %pad_maximum_fusion.4), channel_id=1, source_target_pairs={{0,24},{4,28},{8,16},{12,20},{16,8},{20,12},{24,0},{28,4},{1,25},{... | collective-permute-start | bytes 516104 | tf_op jit(solution)/shard_map/ppermute | solution.py:819
  391.0 14.3 %collective-permute-start.22 = (bf16[2,56,768]{2,1,0:T(8,128)(2,1)}, bf16[2,56,768]{2,1,0:T(8,128)(2,1)S(1)}, u32[]{:S(2)}, u32[]{:S(2)}) collective-permute-start(bf16[2,56,768]{2,1,0:T(8,128)(2,1)} %pad_maximum_fusion.4), channel_id=1, source_target_pairs={{0,16},{4,20},{8,24},{12,28},{16,0},{20,4},{24,8},{28,12},{1,17},{... | collective-permute-start | bytes 516104 | tf_op jit(solution)/shard_map/ppermute | solution.py:819
  391.0 14.3 %collective-permute-start.23 = (bf16[2,56,768]{2,1,0:T(8,128)(2,1)}, bf16[2,56,768]{2,1,0:T(8,128)(2,1)S(1)}, u32[]{:S(2)}, u32[]{:S(2)}) collective-permute-start(bf16[2,56,768]{2,1,0:T(8,128)(2,1)} %pad_maximum_fusion.4), channel_id=1, source_target_pairs={{0,8},{4,12},{8,0},{12,4},{16,24},{20,28},{24,16},{28,20},{1,9},{5... | collective-permute-start | bytes 516104 | tf_op jit(solution)/shard_map/ppermute | solution.py:819
  392.9 12.5 %collective-permute-start.20 = (bf16[2,2,48,768]{3,2,1,0:T(8,128)(2,1)S(1)}, bf16[2,2,48,768]{3,2,1,0:T(8,128)(2,1)S(1)}, u32[]{:S(2)}, u32[]{:S(2)}) collective-permute-start(bf16[2,2,48,768]{3,2,1,0:T(8,128)(2,1)S(1)} %bitcast.150), channel_id=1, source_target_pairs={{0,4},{4,0},{8,12},{12,8},{16,20},{20,16},{24,28},{28,24},{1,5},{5... | collective-permute-start | bytes 884744 | tf_op jit(solution)/shard_map/ppermute | solution.py:819
  406.9 4.2 collective-permute-start.25
  (38 other events, 274.9 us)
Sparse Core Ops, SparseCore 0:
  9.6 40.1 all-gather.2
  98.3 36.4 all-gather.4
  350.4 36.0 reduce-scatter.1

commit v6 on v5

--- a/solution.py
+++ b/solution.py
@@ -954,8 +954,8 @@
     ).astype(jnp.bfloat16)
     hot_gap = hot_gap.reshape(expert_count, 2, half_slots, LANES)
     router_wide = jnp.pad(router, ((0, 0), (0, LANES - expert_count)))
-    first_rows, act_grads, hot_gap, weights_in, last = lax.optimization_barrier(
-        (first_rows, act_grads, hot_gap, weights_in, outgoing[1])
+    first_rows, act_grads, hot_gap, weights_in, last, dispatch, halves = lax.optimization_barrier(
+        (first_rows, act_grads, hot_gap, weights_in, outgoing[1], dispatch, halves)
     )
     last_rows = exchange(last)
     sent_one, *kept = serve(place, first_rows, act_grads, hot_gap, weights_in, router_wide, 0, None)
@@ -971,7 +971,9 @@
     grad_sent_two = exchange(sent_two)
     out_half = joined_low(out_keep, swap(out_send, "tensor", 0))
     out_half, grad_pre = lax.optimization_barrier((out_half, grad_pre))
-    grad_w_out = spread_rest(out_half, "tensor")
+    for bit in range(1, bit_count("tensor") - 1):
+        out_half = joined_low(*halved(out_half, "tensor", bit))
+    out_half, out_got = halved(out_half, "tensor", bit_count("tensor") - 1)
     in_send, in_keep, router_part = in_weights_of(first_rows, last_rows, grad_pre, logit_grads)
     router_part = router_part[:, :expert_count]
     count = 2 + expert_count
@@ -983,8 +985,8 @@
     act, in_send, in_keep, small = lax.optimization_barrier((act, in_send, in_keep, small))
     in_got = swap(in_send, "tensor", 0)
     result = result_of(place, act, weights_out)
-    grad_sent_one, grad_sent_two, result, dispatch, grad_w_out = lax.optimization_barrier(
-        (grad_sent_one, grad_sent_two, result, dispatch, grad_w_out)
+    grad_sent_one, grad_sent_two, result, out_half, out_got = lax.optimization_barrier(
+        (grad_sent_one, grad_sent_two, result, out_half, out_got)
     )
     grad_resid, grad_sharp, gain_two_part = combine(
         halves[0],
@@ -1016,9 +1018,10 @@
     owned, orders = scatter_rows(weights_part, "expert")
     owned = lax.optimization_barrier(owned)
     begun = [gather(own, "expert", order[::-1][:1]) for own, order in zip(owned, orders)]
-    begun, came_back, grad_w_in, tokens_shared = lax.optimization_barrier(
-        (begun, came_back, grad_w_in, tokens_shared)
-    )
+    begun, came_back, grad_w_in, tokens_shared, out_half = lax.optimization_barrier(
+        (begun, came_back, grad_w_in, tokens_shared, out_half)
+    )
+    grad_w_out = joined(out_half, out_got)
     weights_total = gather_rows(begun, orders, "expert").astype(jnp.float32)
     output = resid + jnp.dot(dispatch, came_back, preferred_element_type=jnp.float32)
     grad_tokens = grad_resid + tokens_shared.astype(jnp.float32)
@@ -1040,7 +1043,7 @@
         columns[1],
         columns[2:].T,
         grad_w_in,
-        grad_w_out[None],
+        grad_w_out,
     )
 
 

time: 428 us -> 421 us (0.984)
  waiting for transfers between devices: 113 us -> 104 us
    all_to_all x6, waiting for transfers between devices: 48.9 us -> 43.5 us  [exchange(): lax.all_to_all(pieces, 'expert', split_axis=0, concat_axis=0, tiled=True)]
    unnamed x71 -> x73, local copies, waits for them, and re-layouts: 12.4 us -> 13.5 us
  transfers between devices with their start and end apart: 35 -> 35, of which waited for: 18 -> 19; matrix products, arithmetic and copies ran while one was open for 11% -> 11% of each run, Pallas kernels for 41% -> 42%
where the time goes in v6:
time: 421 us; the launch traced here: 413 us
  Pallas kernels  172 us (41%)
  waiting for transfers between devices  104 us (25%)
  starting transfers between devices  61.8 us (15%)
  other arithmetic  26 us (6%)
  local copies, waits for them, and re-layouts  23.7 us (6%)
  between operations  14.9 us (4%)
  matrix products  10.1 us (2%)
    pallas_call x2, Pallas kernels, serve(): pl.pallas_call(functools.partial(expert_kernel, sub=sub), grid_spec=pltpu...  43.9 us
    all_to_all x6, waiting for transfers between devices, exchange(): lax.all_to_all(pieces, 'expert', split_axis=0, concat_axis=0, tiled=True)  43.5 us
    ppermute x8, waiting for transfers between devices, swap(): lax.ppermute(value, axis_name, [(i, i ^ 1 << bit) for i in range(count)])  40.7 us
    pallas_call x1, Pallas kernels, attend_back(): pl.pallas_call(functools.partial(backward_kernel, head_count=head_count,...  35.9 us
    all_to_all x6, starting transfers between devices, exchange(): lax.all_to_all(pieces, 'expert', split_axis=0, concat_axis=0, tiled=True)  31.7 us
    ppermute x18, starting transfers between devices, send_over(): return lax.ppermute(value, axis_name, [(i, i ^ mask) for i in range(count)])  24.9 us
    pallas_call x1, Pallas kernels, attend(): pl.pallas_call(functools.partial(forward_kernel, head_count=head_count, h...  22.9 us
    ppermute x18, waiting for transfers between devices, send_over(): return lax.ppermute(value, axis_name, [(i, i ^ mask) for i in range(count)])  19.3 us
  transfers between devices with their start and end apart: 35, of which 19 were waited for; matrix products, arithmetic and copies ran while one was open for 11% of the time, Pallas kernels for 42%

profile of v6, /device:TPU:0, one launch (start us, length us, event | category | flops | bytes accessed | tf_op | source)
XLA Modules:
  0.0 413.1 jit_solution(3300207101748055436)
XLA Ops:
  9.7 4.4 %place_rows.1 = (bf16[8,272,768]{2,1,0:T(8,128)(2,1)S(1)}, s32[8,512]{1,0:T(8,128)S(1)}) custom-call(s32[2,512]{1,0:T(2,128)S(1)} %bitcast.122, bf16[512,768]{1,0:T(8,128)(2,1)S(1)} %copy-done.10), custom_call_target="tpu_custom_call" | custom-call | flops 1610612736 | bytes 3145728 | tf_op jit(solution)/shard_map/place_rows/pallas_call | solution.py:687
  15.8 7.4 %all-to-all-start = ((bf16[8,272,768]{2,1,0:T(8,128)(2,1)}), bf16[8,272,768]{2,1,0:T(8,128)(2,1)S(1)}, u32[]{:S(2)}, u32[]{:S(2)}) async-start(bf16[8,272,768]{2,1,0:T(8,128)(2,1)} %copy-done.3), calls=%async_computation | async-start | bytes 6684672 | tf_op jit(solution)/shard_map/all_to_all | solution.py:767
  25.8 22.9 %attend_forward.1 = (bf16[2048,768]{1,0:T(8,128)(2,1)}, bf16[576,2048]{1,0:T(8,128)(2,1)S(1)}, bf16[192,2048]{1,0:T(8,128)(2,1)S(1)}, f32[8,2048]{1,0:T(8,128)S(1)}) custom-call(s32[1]{0:T(128)} %bitcast.1.place_ref, s32[1,8]{1,0:T(1,128)S(1)} %copy-done.17, bf16[2048,768]{1,0:T(8,128)(2,1)} %tokens_ref.1, f32[1,768]{1,0:T(1,128)S(1)} %broadcast_in_dim.11.gain_ref, ...), custom_call_target="tpu_custom_call" | custom-call | flops 3623878656 | bytes 15728640 | tf_op jit(solution)/shard_map/attend_forward/pallas_call | solution.py:260
  48.7 3.2 fusion.21
  52.0 3.4 collective-permute-done
  61.3 17.0 %collective-permute-done.1 = bf16[1,512,768]{2,1,0:T(8,128)(2,1)} collective-permute-done((bf16[1,512,768]{2,1,0:T(8,128)(2,1)}, bf16[1,512,768]{2,1,0:T(8,128)(2,1)}, u32[]{:S(2)}, u32[]{:S(2)}) %collective-permute-start.1) | collective-permute-done | bytes 786464 | tf_op jit(solution)/shard_map/ppermute | solution.py:804
  85.6 12.6 %all-to-all-done.rows_ref.landed_ref = bf16[8,272,768]{2,1,0:T(8,128)(2,1)S(1)} async-done(((bf16[8,272,768]{2,1,0:T(8,128)(2,1)}), bf16[8,272,768]{2,1,0:T(8,128)(2,1)S(1)}, u32[]{:S(2)}, u32[]{:S(2)}) %all-to-all-start) | async-done | bytes 3342368 | tf_op jit(solution)/shard_map/all_to_all | solution.py:767
  98.2 4.8 %all-to-all-start.1 = ((bf16[8,128,768]{2,1,0:T(8,128)(2,1)}), bf16[8,128,768]{2,1,0:T(8,128)(2,1)}, u32[]{:S(2)}, u32[]{:S(2)}) async-start(bf16[8,128,768]{2,1,0:T(8,128)(2,1)} %bitcast.144), calls=%async_computation.1 | async-start | bytes 3145728 | tf_op jit(solution)/shard_map/all_to_all | solution.py:767
  103.0 3.9 fusion.16
  111.5 14.9 %act_grads.1 = bf16[4,2048,768]{2,1,0:T(8,128)(2,1)} custom-call(s32[1]{0:T(128)} %bitcast.1.place_ref, bf16[8,272,768]{2,1,0:T(8,128)(2,1)S(1)} %all-to-all-done.rows_ref.landed_ref, bf16[4,768,768]{2,1,0:T(8,128)(2,1)} %all-gather.3.cloned.1.call-done.weights_ref), custom_call_target="tpu_custom_call" | custom-call | flops 9663676416 | bytes 12582912 | tf_op jit(solution)/shard_map/act_grads/pallas_call | solution.py:500
  126.4 13.2 %all-to-all-done.1.rows_ref.first_ref = bf16[8,128,768]{2,1,0:T(8,128)(2,1)} async-done(((bf16[8,128,768]{2,1,0:T(8,128)(2,1)}), bf16[8,128,768]{2,1,0:T(8,128)(2,1)}, u32[]{:S(2)}, u32[]{:S(2)}) %all-to-all-start.1) | async-done | bytes 1572896 | tf_op jit(solution)/shard_map/all_to_all | solution.py:767
  139.6 3.6 all-to-all-start.3
  143.5 22.1 %expert_middle.2 = (bf16[8,128,768]{2,1,0:T(8,128)(2,1)S(1)}, bf16[4,8,2,128,768]{4,3,2,1,0:T(8,128)(2,1)}, bf16[4,8,2,128,768]{4,3,2,1,0:T(8,128)(2,1)}, bf16[8,2,128,128]{3,2,1,0:T(8,128)(2,1)S(1)}) custom-call(s32[1]{0:T(128)} %bitcast.1.place_ref, bf16[8,128,768]{2,1,0:T(8,128)(2,1)} %all-to-all-done.1.rows_ref.first_ref, ...), custom_call_target="tpu_custom_call" | custom-call | flops 9663676416 | bytes 18874368 | tf_op jit(solution)/shard_map/expert_middle/pallas_call | solution.py:456
  166.7 13.7 %all-to-all-done.3.rows_ref.last_ref = bf16[8,128,768]{2,1,0:T(8,128)(2,1)S(1)} async-done(((bf16[8,128,768]{2,1,0:T(8,128)(2,1)}), bf16[8,128,768]{2,1,0:T(8,128)(2,1)S(1)}, u32[]{:S(2)}, u32[]{:S(2)}) %all-to-all-start.3) | async-done | bytes 1572896 | tf_op jit(solution)/shard_map/all_to_all | solution.py:767
  180.4 4.5 %all-to-all-start.2 = ((bf16[8,128,768]{2,1,0:T(8,128)(2,1)}), bf16[8,128,768]{2,1,0:T(8,128)(2,1)}, u32[]{:S(2)}, u32[]{:S(2)}) async-start(bf16[8,128,768]{2,1,0:T(8,128)(2,1)} %copy-done.7), calls=%async_computation.2 | async-start | bytes 3145728 | tf_op jit(solution)/shard_map/all_to_all | solution.py:767
  184.9 21.8 %expert_middle.3 = (bf16[8,128,768]{2,1,0:T(8,128)(2,1)S(1)}, bf16[4,8,2,128,768]{4,3,2,1,0:T(8,128)(2,1)}, bf16[4,8,2,128,768]{4,3,2,1,0:T(8,128)(2,1)}, bf16[8,2,128,128]{3,2,1,0:T(8,128)(2,1)S(1)}) custom-call(s32[1]{0:T(128)} %bitcast.1.place_ref, ...), custom_call_target="tpu_custom_call", output_to_operand_aliasing={{1}: (6, {}), {2}: (7, {}), {3}: (8, {})} | custom-call | flops 9663676416 | bytes 18874368 | tf_op jit(solution)/shard_map/expert_middle/pallas_call | solution.py:456
  207.9 15.1 %out_weights.1 = (bf16[2,768,768]{2,1,0:T(8,128)(2,1)}, bf16[2,768,768]{2,1,0:T(8,128)(2,1)S(1)}) custom-call(bf16[4,2048,768]{2,1,0:T(8,128)(2,1)} %bitcast.123, bf16[8,272,768]{2,1,0:T(8,128)(2,1)} %copy-done), custom_call_target="tpu_custom_call" | custom-call | tf_op jit(solution)/shard_map/out_weights/pallas_call | solution.py:587
  224.3 6.0 %all-to-all-start.4 = ((bf16[8,128,768]{2,1,0:T(8,128)(2,1)}), bf16[8,128,768]{2,1,0:T(8,128)(2,1)}, u32[]{:S(2)}, u32[]{:S(2)}) async-start(bf16[8,128,768]{2,1,0:T(8,128)(2,1)} %copy-done.6), calls=%async_computation.4 | async-start | bytes 3145728 | tf_op jit(solution)/shard_map/all_to_all | solution.py:767
  230.3 2.9 add_convert_fusion.1
  236.4 15.9 %in_weights.1 = (bf16[2,768,768]{2,1,0:T(8,128)(2,1)}, bf16[2,768,768]{2,1,0:T(8,128)(2,1)}, f32[768,128]{1,0:T(8,128)S(1)}) custom-call(bf16[8,128,768]{2,1,0:T(8,128)(2,1)} %all-to-all-done.1.rows_ref.first_ref, bf16[8,128,768]{2,1,0:T(8,128)(2,1)S(1)} %all-to-all-done.3.rows_ref.last_ref, bf16[4,8,2,128,768]{4,3,2,1,0:T(8,128)(2,1)} %get-tuple-element.107.grads_ref, ...), custom_call_target="tpu_custom_call" | custom-call | tf_op jit(solution)/shard_map/in_weights/pallas_call | solution.py:627
  252.6 14.7 %expert_result.1 = bf16[2048,768]{1,0:T(8,128)(2,1)} custom-call(s32[1]{0:T(128)} %bitcast.1.place_ref, bf16[4,2048,768]{2,1,0:T(8,128)(2,1)} %bitcast.124, bf16[4,768,768]{2,1,0:T(8,128)(2,1)} %all-gather.3.cloned.1.call-done.weights_ref), custom_call_target="tpu_custom_call" | custom-call | tf_op jit(solution)/shard_map/expert_result/pallas_call | solution.py:533
  268.1 5.5 %all-to-all-start.5 = ((bf16[8,256,768]{2,1,0:T(8,128)(2,1)}), bf16[8,256,768]{2,1,0:T(8,128)(2,1)}, u32[]{:S(2)}, u32[]{:S(2)}) async-start(bf16[8,256,768]{2,1,0:T(8,128)(2,1)} %bitcast.23), calls=%async_computation.5 | async-start | bytes 6291456 | tf_op jit(solution)/shard_map/all_to_all | solution.py:767
  273.8 4.8 %combine.1 = (f32[512,768]{1,0:T(8,128)S(1)}, bf16[512,768]{1,0:T(8,128)(2,1)S(1)}, f32[8,768]{1,0:T(8,128)S(1)}) custom-call(bf16[512,1024]{1,0:T(8,128)(2,1)S(1)} %copy-done.1, bf16[1024,768]{1,0:T(8,128)(2,1)} %bitcast.20.first_rows_ref, bf16[512,1024]{1,0:T(8,128)(2,1)S(1)} %copy-done.2, bf16[1024,768]{1,0:T(8,128)(2,1)} %bitcast.21.last_rows_ref, ...), custom_call_target="tpu_custom_call" | custom-call | flops 1610612736 | bytes 7864320 | tf_op jit(solution)/shard_map/combine/pallas_call | solution.py:739
  280.7 19.0 %collective-permute-done.4 = bf16[1,512,768]{2,1,0:T(8,128)(2,1)S(1)} collective-permute-done((bf16[1,512,768]{2,1,0:T(8,128)(2,1)S(1)}, bf16[1,512,768]{2,1,0:T(8,128)(2,1)S(1)}, u32[]{:S(2)}, u32[]{:S(2)}) %collective-permute-start.4) | collective-permute-done | bytes 786464 | tf_op jit(solution)/shard_map/ppermute | solution.py:804
  305.1 35.9 %attend_backward.1 = (bf16[2048,768]{1,0:T(8,128)(2,1)}, bf16[832,768]{1,0:T(8,128)(2,1)S(1)}) custom-call(s32[1]{0:T(128)} %bitcast.1.place_ref, s32[1,8]{1,0:T(1,128)S(1)} %copy-done.17, bf16[2048,768]{1,0:T(8,128)(2,1)} %tokens_ref.1, f32[1,768]{1,0:T(1,128)S(1)} %broadcast_in_dim.11.gain_ref, bf16[576,768]{1,0:T(8,128)(2,1)S(1)} %bitcast.121, ...), custom_call_target="tpu_custom_call" | custom-call | flops 7851737088 | bytes 22020096 | tf_op jit(solution)/shard_map/attend_backward/pallas_call | solution.py:318
  341.1 3.2 all-to-all-done.5
  352.7 7.4 %collective-permute-done.13 = bf16[2,56,768]{2,1,0:T(8,128)(2,1)S(1)} collective-permute-done((bf16[2,56,768]{2,1,0:T(8,128)(2,1)S(1)}, bf16[2,56,768]{2,1,0:T(8,128)(2,1)S(1)}, u32[]{:S(2)}, u32[]{:S(2)}) %collective-permute-start.13) | collective-permute-done | bytes 172064 | tf_op jit(solution)/shard_map/ppermute | solution.py:819
  361.8 3.4 collective-permute-start.10
  368.3 3.2 collective-permute-done.11
  380.9 3.2 collective-permute-start.21
  389.6 3.1 convert_add_fusion.2
  392.7 5.0 %convolution_add_fusion = f32[512,768]{1,0:T(8,128)} fusion(f32[512,768]{1,0:T(8,128)S(1)} %copy-done.23, bf16[512,2048]{1,0:T(8,128)(2,1)S(1)} %copy-done.29, bf16[2048,768]{1,0:T(8,128)(2,1)} %bitcast.24), kind=kOutput, calls=%fused_computation.25 | convolution fusion | flops 1611005952 | bytes 8388608 | tf_op jit(solution)/shard_map/dot_general | solution.py:1026
  (198 shorter events, 76.5 us)
Async XLA Ops:
  7.2 104.3 %all-gather.3.cloned.1.call-start = ((), (), s32[]{:S(2)}) async-start(), calls=%async_computation.7 | async-start | bytes 5898240 | tf_op jit(solution)/shard_map/all_gather | solution.py:945
  15.8 82.3 %all-to-all-start = ((bf16[8,272,768]{2,1,0:T(8,128)(2,1)}), bf16[8,272,768]{2,1,0:T(8,128)(2,1)S(1)}, u32[]{:S(2)}, u32[]{:S(2)}) async-start(bf16[8,272,768]{2,1,0:T(8,128)(2,1)} %copy-done.3), calls=%async_computation | async-start | bytes 6684672 | tf_op jit(solution)/shard_map/all_to_all | solution.py:767
  23.3 116.4 %all-gather.5.cloned.1.call-start = ((), (), s32[]{:S(2)}) async-start(), calls=%async_computation.8 | async-start | bytes 5898240 | tf_op jit(solution)/shard_map/all_gather | solution.py:946
  58.4 19.9 %collective-permute-start.1 = (bf16[1,512,768]{2,1,0:T(8,128)(2,1)}, bf16[1,512,768]{2,1,0:T(8,128)(2,1)}, u32[]{:S(2)}, u32[]{:S(2)}) collective-permute-start(bf16[1,512,768]{2,1,0:T(8,128)(2,1)} %slice.184), channel_id=1, source_target_pairs={{0,2},{1,3},{2,0},{3,1},{4,6},{5,7},{6,4},{7,5},{8,10},{9,11},{10,... | collective-permute-start | bytes 2359304 | tf_op jit(solution)/shard_map/ppermute | solution.py:804
  98.2 41.4 %all-to-all-start.1 = ((bf16[8,128,768]{2,1,0:T(8,128)(2,1)}), bf16[8,128,768]{2,1,0:T(8,128)(2,1)}, u32[]{:S(2)}, u32[]{:S(2)}) async-start(bf16[8,128,768]{2,1,0:T(8,128)(2,1)} %bitcast.144), calls=%async_computation.1 | async-start | bytes 3145728 | tf_op jit(solution)/shard_map/all_to_all | solution.py:767
  139.6 40.8 %all-to-all-start.3 = ((bf16[8,128,768]{2,1,0:T(8,128)(2,1)}), bf16[8,128,768]{2,1,0:T(8,128)(2,1)S(1)}, u32[]{:S(2)}, u32[]{:S(2)}) async-start(bf16[8,128,768]{2,1,0:T(8,128)(2,1)} %bitcast.143), calls=%async_computation.3 | async-start | bytes 3145728 | tf_op jit(solution)/shard_map/all_to_all | solution.py:767
  180.4 43.9 %all-to-all-start.2 = ((bf16[8,128,768]{2,1,0:T(8,128)(2,1)}), bf16[8,128,768]{2,1,0:T(8,128)(2,1)}, u32[]{:S(2)}, u32[]{:S(2)}) async-start(bf16[8,128,768]{2,1,0:T(8,128)(2,1)} %copy-done.7), calls=%async_computation.2 | async-start | bytes 3145728 | tf_op jit(solution)/shard_map/all_to_all | solution.py:767
  224.3 6.0 %collective-permute-start.2 = (bf16[2,768,768]{2,1,0:T(8,128)(2,1)}, bf16[2,768,768]{2,1,0:T(8,128)(2,1)}, u32[]{:S(2)}, u32[]{:S(2)}) collective-permute-start(bf16[2,768,768]{2,1,0:T(8,128)(2,1)} %get-tuple-element.105), channel_id=1, source_target_pairs={{0,1},{1,0},{2,3},{3,2},{4,5},{5,4},{6,7},{7,6},{8,9},{9,8},{10,11... | collective-permute-start | bytes 7077896 | tf_op jit(solution)/shard_map/ppermute | solution.py:804
  224.3 43.7 %all-to-all-start.4 = ((bf16[8,128,768]{2,1,0:T(8,128)(2,1)}), bf16[8,128,768]{2,1,0:T(8,128)(2,1)}, u32[]{:S(2)}, u32[]{:S(2)}) async-start(bf16[8,128,768]{2,1,0:T(8,128)(2,1)} %copy-done.6), calls=%async_computation.4 | async-start | bytes 3145728 | tf_op jit(solution)/shard_map/all_to_all | solution.py:767
  234.8 33.3 %collective-permute-start.3 = (bf16[1,768,768]{2,1,0:T(8,128)(2,1)}, bf16[1,768,768]{2,1,0:T(8,128)(2,1)}, u32[]{:S(2)}, u32[]{:S(2)}) collective-permute-start(bf16[1,768,768]{2,1,0:T(8,128)(2,1)} %get-tuple-element.148), channel_id=1, source_target_pairs={{0,2},{1,3},{2,0},{3,1},{4,6},{5,7},{6,4},{7,5},{8,10},{9,11},{10,... | collective-permute-start | bytes 3538952 | tf_op jit(solution)/shard_map/ppermute | solution.py:804
  268.1 76.1 %all-to-all-start.5 = ((bf16[8,256,768]{2,1,0:T(8,128)(2,1)}), bf16[8,256,768]{2,1,0:T(8,128)(2,1)}, u32[]{:S(2)}, u32[]{:S(2)}) async-start(bf16[8,256,768]{2,1,0:T(8,128)(2,1)} %bitcast.23), calls=%async_computation.5 | async-start | bytes 6291456 | tf_op jit(solution)/shard_map/all_to_all | solution.py:767
  273.6 107.2 %reduce-scatter.2.cloned.1.call-start = ((), (), s32[]{:S(2)}) async-start(), calls=%async_computation.9 | async-start | bytes 3932160 | tf_op jit(solution)/shard_map/reduce_scatter | solution.py:1017
  273.6 26.2 %collective-permute-start.5 = (bf16[2,768,768]{2,1,0:T(8,128)(2,1)}, bf16[2,768,768]{2,1,0:T(8,128)(2,1)S(1)}, u32[]{:S(2)}, u32[]{:S(2)}) collective-permute-start(bf16[2,768,768]{2,1,0:T(8,128)(2,1)} %get-tuple-element.119), channel_id=1, source_target_pairs={{0,1},{1,0},{2,3},{3,2},{4,5},{5,4},{6,7},{7,6},{8,9},{9,8},{10,11... | collective-permute-start | bytes 7077896 | tf_op jit(solution)/shard_map/ppermute | solution.py:804
  279.7 19.9 %collective-permute-start.4 = (bf16[1,512,768]{2,1,0:T(8,128)(2,1)S(1)}, bf16[1,512,768]{2,1,0:T(8,128)(2,1)S(1)}, u32[]{:S(2)}, u32[]{:S(2)}) collective-permute-start(bf16[1,512,768]{2,1,0:T(8,128)(2,1)S(1)} %bitcast.118), channel_id=1, source_target_pairs={{0,2},{1,3},{2,0},{3,1},{4,6},{5,7},{6,4},{7,5},{8,10},{9,11},{10,... | collective-permute-start | bytes 2359304 | tf_op jit(solution)/shard_map/ppermute | solution.py:804
  301.8 39.3 %collective-permute-start.7 = (bf16[1,768,768]{2,1,0:T(8,128)(2,1)S(1)}, bf16[1,768,768]{2,1,0:T(8,128)(2,1)}, u32[]{:S(2)}, u32[]{:S(2)}) collective-permute-start(bf16[1,768,768]{2,1,0:T(8,128)(2,1)S(1)} %get-tuple-element.147), channel_id=1, source_target_pairs={{0,2},{1,3},{2,0},{3,1},{4,6},{5,7},{6,4},{7,5},{8,10},{9,11},{10,... | collective-permute-start | bytes 3538952 | tf_op jit(solution)/shard_map/ppermute | solution.py:804
  344.4 8.3 %collective-permute-start.12 = (bf16[2,56,768]{2,1,0:T(8,128)(2,1)S(1)}, bf16[2,56,768]{2,1,0:T(8,128)(2,1)S(1)}, u32[]{:S(2)}, u32[]{:S(2)}) collective-permute-start(bf16[2,56,768]{2,1,0:T(8,128)(2,1)S(1)} %get-tuple-element.154), channel_id=1, source_target_pairs={{0,8},{4,12},{8,0},{12,4},{16,24},{20,28},{24,16},{28,20},{1,9},{5... | collective-permute-start | bytes 516104 | tf_op jit(solution)/shard_map/ppermute | solution.py:819
  344.5 15.6 %collective-permute-start.13 = (bf16[2,56,768]{2,1,0:T(8,128)(2,1)S(1)}, bf16[2,56,768]{2,1,0:T(8,128)(2,1)S(1)}, u32[]{:S(2)}, u32[]{:S(2)}) collective-permute-start(bf16[2,56,768]{2,1,0:T(8,128)(2,1)S(1)} %get-tuple-element.156), channel_id=1, source_target_pairs={{0,16},{4,20},{8,24},{12,28},{16,0},{20,4},{24,8},{28,12},{1,17},{... | collective-permute-start | bytes 516104 | tf_op jit(solution)/shard_map/ppermute | solution.py:819
  347.3 12.8 %collective-permute-start.14 = (bf16[2,56,768]{2,1,0:T(8,128)(2,1)S(1)}, bf16[2,56,768]{2,1,0:T(8,128)(2,1)S(1)}, u32[]{:S(2)}, u32[]{:S(2)}) collective-permute-start(bf16[2,56,768]{2,1,0:T(8,128)(2,1)S(1)} %get-tuple-element.155), channel_id=1, source_target_pairs={{0,24},{4,28},{8,16},{12,20},{16,8},{20,12},{24,0},{28,4},{1,25},{... | collective-permute-start | bytes 516104 | tf_op jit(solution)/shard_map/ppermute | solution.py:819
  348.9 12.8 %collective-permute-start.8 = (bf16[2,2,48,768]{3,2,1,0:T(8,128)(2,1)S(1)}, bf16[2,2,48,768]{3,2,1,0:T(8,128)(2,1)S(1)}, u32[]{:S(2)}, u32[]{:S(2)}) collective-permute-start(bf16[2,2,48,768]{3,2,1,0:T(8,128)(2,1)S(1)} %dynamic-slice_bitcast_fusion), channel_id=1, source_target_pairs={{0,4},{4,0},{8,12},{12,8},{16,20},{20,16},{24,28},{28,24},{1,5},{5... | collective-permute-start | bytes 884744 | tf_op jit(solution)/shard_map/ppermute | solution.py:819
  360.3 6.4 %collective-permute-start.15 = (bf16[56,768]{1,0:T(8,128)(2,1)S(1)}, bf16[56,768]{1,0:T(8,128)(2,1)S(1)}, u32[]{:S(2)}, u32[]{:S(2)}) collective-permute-start(bf16[56,768]{1,0:T(8,128)(2,1)S(1)} %fusion.12), channel_id=1, source_target_pairs={{0,4},{4,0},{8,12},{12,8},{16,20},{20,16},{24,28},{28,24},{1,5},{5... | collective-permute-start | bytes 258056 | tf_op jit(solution)/shard_map/ppermute | solution.py:819
  361.8 6.5 %collective-permute-start.10 = (bf16[48,768]{1,0:T(8,128)(2,1)S(1)}, bf16[48,768]{1,0:T(8,128)(2,1)S(1)}, u32[]{:S(2)}, u32[]{:S(2)}) collective-permute-start(bf16[48,768]{1,0:T(8,128)(2,1)S(1)} %get-tuple-element.161), channel_id=1, source_target_pairs={{0,16},{4,20},{8,24},{12,28},{16,0},{20,4},{24,8},{28,12},{1,17},{... | collective-permute-start | bytes 221192 | tf_op jit(solution)/shard_map/ppermute | solution.py:819
  365.3 6.3 %collective-permute-start.11 = (bf16[48,768]{1,0:T(8,128)(2,1)S(1)}, bf16[48,768]{1,0:T(8,128)(2,1)S(1)}, u32[]{:S(2)}, u32[]{:S(2)}) collective-permute-start(bf16[48,768]{1,0:T(8,128)(2,1)S(1)} %get-tuple-element.160), channel_id=1, source_target_pairs={{0,24},{4,28},{8,16},{12,20},{16,8},{20,12},{24,0},{28,4},{1,25},{... | collective-permute-start | bytes 221192 | tf_op jit(solution)/shard_map/ppermute | solution.py:819
  366.6 5.1 %collective-permute-start.9 = (bf16[48,768]{1,0:T(8,128)(2,1)S(1)}, bf16[48,768]{1,0:T(8,128)(2,1)S(1)}, u32[]{:S(2)}, u32[]{:S(2)}) collective-permute-start(bf16[48,768]{1,0:T(8,128)(2,1)S(1)} %get-tuple-element.159), channel_id=1, source_target_pairs={{0,8},{4,12},{8,0},{12,4},{16,24},{20,28},{24,16},{28,20},{1,9},{5... | collective-permute-start | bytes 221192 | tf_op jit(solution)/shard_map/ppermute | solution.py:819
  371.8 6.3 %collective-permute-start.16 = (bf16[48,768]{1,0:T(8,128)(2,1)S(1)}, bf16[48,768]{1,0:T(8,128)(2,1)S(1)}, u32[]{:S(2)}, u32[]{:S(2)}) collective-permute-start(bf16[48,768]{1,0:T(8,128)(2,1)S(1)} %fusion.11), channel_id=1, source_target_pairs={{0,24},{4,28},{8,16},{12,20},{16,8},{20,12},{24,0},{28,4},{1,25},{... | collective-permute-start | bytes 221192 | tf_op jit(solution)/shard_map/ppermute | solution.py:819
  373.7 6.0 %collective-permute-start.17 = (bf16[48,768]{1,0:T(8,128)(2,1)S(1)}, bf16[48,768]{1,0:T(8,128)(2,1)S(1)}, u32[]{:S(2)}, u32[]{:S(2)}) collective-permute-start(bf16[48,768]{1,0:T(8,128)(2,1)S(1)} %fusion.11), channel_id=1, source_target_pairs={{0,16},{4,20},{8,24},{12,28},{16,0},{20,4},{24,8},{28,12},{1,17},{... | collective-permute-start | bytes 221192 | tf_op jit(solution)/shard_map/ppermute | solution.py:819
  373.8 6.0 %collective-permute-start.18 = (bf16[48,768]{1,0:T(8,128)(2,1)S(1)}, bf16[48,768]{1,0:T(8,128)(2,1)S(1)}, u32[]{:S(2)}, u32[]{:S(2)}) collective-permute-start(bf16[48,768]{1,0:T(8,128)(2,1)S(1)} %fusion.11), channel_id=1, source_target_pairs={{0,8},{4,12},{8,0},{12,4},{16,24},{20,28},{24,16},{28,20},{1,9},{5... | collective-permute-start | bytes 221192 | tf_op jit(solution)/shard_map/ppermute | solution.py:819
  376.3 4.5 %collective-permute-start.19 = (bf16[56,768]{1,0:T(8,128)(2,1)S(1)}, bf16[56,768]{1,0:T(8,128)(2,1)S(1)}, u32[]{:S(2)}, u32[]{:S(2)}) collective-permute-start(bf16[56,768]{1,0:T(8,128)(2,1)S(1)} %fusion.8), channel_id=1, source_target_pairs={{0,4},{4,0},{8,12},{12,8},{16,20},{20,16},{24,28},{28,24},{1,5},{5... | collective-permute-start | bytes 258056 | tf_op jit(solution)/shard_map/ppermute | solution.py:819
  380.9 18.2 %collective-permute-start.21 = (bf16[2,56,768]{2,1,0:T(8,128)(2,1)S(1)}, bf16[2,56,768]{2,1,0:T(8,128)(2,1)S(1)}, u32[]{:S(2)}, u32[]{:S(2)}) collective-permute-start(bf16[2,56,768]{2,1,0:T(8,128)(2,1)S(1)} %pad_maximum_fusion.4), channel_id=1, source_target_pairs={{0,24},{4,28},{8,16},{12,20},{16,8},{20,12},{24,0},{28,4},{1,25},{... | collective-permute-start | bytes 516104 | tf_op jit(solution)/shard_map/ppermute | solution.py:819
  384.1 15.0 %collective-permute-start.22 = (bf16[2,56,768]{2,1,0:T(8,128)(2,1)S(1)}, bf16[2,56,768]{2,1,0:T(8,128)(2,1)S(1)}, u32[]{:S(2)}, u32[]{:S(2)}) collective-permute-start(bf16[2,56,768]{2,1,0:T(8,128)(2,1)S(1)} %pad_maximum_fusion.4), channel_id=1, source_target_pairs={{0,16},{4,20},{8,24},{12,28},{16,0},{20,4},{24,8},{28,12},{1,17},{... | collective-permute-start | bytes 516104 | tf_op jit(solution)/shard_map/ppermute | solution.py:819
  384.1 15.0 %collective-permute-start.23 = (bf16[2,56,768]{2,1,0:T(8,128)(2,1)S(1)}, bf16[2,56,768]{2,1,0:T(8,128)(2,1)S(1)}, u32[]{:S(2)}, u32[]{:S(2)}) collective-permute-start(bf16[2,56,768]{2,1,0:T(8,128)(2,1)S(1)} %pad_maximum_fusion.4), channel_id=1, source_target_pairs={{0,8},{4,12},{8,0},{12,4},{16,24},{20,28},{24,16},{28,20},{1,9},{5... | collective-permute-start | bytes 516104 | tf_op jit(solution)/shard_map/ppermute | solution.py:819
  385.3 13.9 %collective-permute-start.20 = (bf16[2,2,48,768]{3,2,1,0:T(8,128)(2,1)S(1)}, bf16[2,2,48,768]{3,2,1,0:T(8,128)(2,1)S(1)}, u32[]{:S(2)}, u32[]{:S(2)}) collective-permute-start(bf16[2,2,48,768]{3,2,1,0:T(8,128)(2,1)S(1)} %bitcast.146), channel_id=1, source_target_pairs={{0,4},{4,0},{8,12},{12,8},{16,20},{20,16},{24,28},{28,24},{1,5},{5... | collective-permute-start | bytes 884744 | tf_op jit(solution)/shard_map/ppermute | solution.py:819
  400.7 4.2 %collective-permute-start.25 = (f32[10,768]{1,0:T(8,128)S(1)}, f32[10,768]{1,0:T(8,128)S(1)}, u32[]{:S(2)}, u32[]{:S(2)}) collective-permute-start(f32[10,768]{1,0:T(8,128)S(1)} %fusion.28), channel_id=1, source_target_pairs={{0,2},{1,3},{2,0},{3,1},{4,6},{5,7},{6,4},{7,5},{8,10},{9,11},{10,... | collective-permute-start | bytes 92168 | tf_op jit(solution)/shard_map/ppermute | solution.py:819
  (39 other events, 263.7 us)
Sparse Core Ops, SparseCore 0:
  9.6 40.1 all-gather.2
  98.3 36.4 all-gather.4
  344.4 36.3 reduce-scatter.1

commit v7 on v6

--- a/solution.py
+++ b/solution.py
@@ -1016,16 +1016,16 @@
     )
     tokens_shared = lax.psum_scatter(tokens_part, "tensor", scatter_dimension=0, tiled=True)
     owned, orders = scatter_rows(weights_part, "expert")
-    owned = lax.optimization_barrier(owned)
+    owned, grad_w_in, out_half = lax.optimization_barrier((owned, grad_w_in, out_half))
+    grad_w_in = joined(grad_w_in, grad_w_in_got)
+    grad_w_out = joined(out_half, out_got)
     begun = [gather(own, "expert", order[::-1][:1]) for own, order in zip(owned, orders)]
-    begun, came_back, grad_w_in, tokens_shared, out_half = lax.optimization_barrier(
-        (begun, came_back, grad_w_in, tokens_shared, out_half)
-    )
-    grad_w_out = joined(out_half, out_got)
+    begun, came_back, grad_w_in, tokens_shared, grad_w_out = lax.optimization_barrier(
+        (begun, came_back, grad_w_in, tokens_shared, grad_w_out)
+    )
     weights_total = gather_rows(begun, orders, "expert").astype(jnp.float32)
     output = resid + jnp.dot(dispatch, came_back, preferred_element_type=jnp.float32)
     grad_tokens = grad_resid + tokens_shared.astype(jnp.float32)
-    grad_w_in = joined(grad_w_in, grad_w_in_got)
     low = 4 * inner
     bias_total = weights_total[low + 1, : rel_bias.size].reshape(rel_bias.shape)
     small = weights_total[low : low + count + 1]

time: 421 us -> 421 us (level)
    unnamed x73 -> x71, local copies, waits for them, and re-layouts: 13.5 us -> 13.5 us
  transfers between devices with their start and end apart: 35 -> 35, of which waited for: 19 -> 17; matrix products, arithmetic and copies ran while one was open for 11% -> 11% of each run, Pallas kernels for 42% -> 42%
where the time goes in v7:
time: 421 us; the launch traced here: 413 us
  Pallas kernels  172 us (41%)
  waiting for transfers between devices  105 us (25%)
  starting transfers between devices  60.8 us (14%)
  other arithmetic  26 us (6%)
  local copies, waits for them, and re-layouts  23.7 us (6%)
  between operations  14.9 us (4%)
  matrix products  10.5 us (2%)
    pallas_call x2, Pallas kernels, serve(): pl.pallas_call(functools.partial(expert_kernel, sub=sub), grid_spec=pltpu...  43.8 us
    all_to_all x6, waiting for transfers between devices, exchange(): lax.all_to_all(pieces, 'expert', split_axis=0, concat_axis=0, tiled=True)  43.5 us
    ppermute x8, waiting for transfers between devices, swap(): lax.ppermute(value, axis_name, [(i, i ^ 1 << bit) for i in range(count)])  40.7 us
    pallas_call x1, Pallas kernels, attend_back(): pl.pallas_call(functools.partial(backward_kernel, head_count=head_count,...  35.9 us
    all_to_all x6, starting transfers between devices, exchange(): lax.all_to_all(pieces, 'expert', split_axis=0, concat_axis=0, tiled=True)  31.8 us
    ppermute x18, starting transfers between devices, send_over(): return lax.ppermute(value, axis_name, [(i, i ^ mask) for i in range(count)])  23.9 us
    pallas_call x1, Pallas kernels, attend(): pl.pallas_call(functools.partial(forward_kernel, head_count=head_count, h...  22.9 us
    ppermute x18, waiting for transfers between devices, send_over(): return lax.ppermute(value, axis_name, [(i, i ^ mask) for i in range(count)])  19.6 us
  transfers between devices with their start and end apart: 35, of which 17 were waited for; matrix products, arithmetic and copies ran while one was open for 11% of the time, Pallas kernels for 42%

profile of v7, /device:TPU:0, one launch (start us, length us, event | category | flops | bytes accessed | tf_op | source)
XLA Modules:
  0.0 412.9 jit_solution(6195705226160227335)
XLA Ops:
  9.7 4.4 %place_rows.1 = (bf16[8,272,768]{2,1,0:T(8,128)(2,1)S(1)}, s32[8,512]{1,0:T(8,128)S(1)}) custom-call(s32[2,512]{1,0:T(2,128)S(1)} %bitcast.122, bf16[512,768]{1,0:T(8,128)(2,1)S(1)} %copy-done.10), custom_call_target="tpu_custom_call" | custom-call | flops 1610612736 | bytes 3145728 | tf_op jit(solution)/shard_map/place_rows/pallas_call | solution.py:687
  15.8 7.4 %all-to-all-start = ((bf16[8,272,768]{2,1,0:T(8,128)(2,1)}), bf16[8,272,768]{2,1,0:T(8,128)(2,1)S(1)}, u32[]{:S(2)}, u32[]{:S(2)}) async-start(bf16[8,272,768]{2,1,0:T(8,128)(2,1)} %copy-done.3), calls=%async_computation | async-start | bytes 6684672 | tf_op jit(solution)/shard_map/all_to_all | solution.py:767
  25.8 22.9 %attend_forward.1 = (bf16[2048,768]{1,0:T(8,128)(2,1)}, bf16[576,2048]{1,0:T(8,128)(2,1)S(1)}, bf16[192,2048]{1,0:T(8,128)(2,1)S(1)}, f32[8,2048]{1,0:T(8,128)S(1)}) custom-call(s32[1]{0:T(128)} %bitcast.1.place_ref, s32[1,8]{1,0:T(1,128)S(1)} %copy-done.17, bf16[2048,768]{1,0:T(8,128)(2,1)} %tokens_ref.1, f32[1,768]{1,0:T(1,128)S(1)} %broadcast_in_dim.11.gain_ref, ...), custom_call_target="tpu_custom_call" | custom-call | flops 3623878656 | bytes 15728640 | tf_op jit(solution)/shard_map/attend_forward/pallas_call | solution.py:260
  48.7 3.2 fusion.21
  52.0 3.4 collective-permute-done
  61.3 17.0 %collective-permute-done.1 = bf16[1,512,768]{2,1,0:T(8,128)(2,1)} collective-permute-done((bf16[1,512,768]{2,1,0:T(8,128)(2,1)}, bf16[1,512,768]{2,1,0:T(8,128)(2,1)}, u32[]{:S(2)}, u32[]{:S(2)}) %collective-permute-start.1) | collective-permute-done | bytes 786464 | tf_op jit(solution)/shard_map/ppermute | solution.py:804
  85.6 12.6 %all-to-all-done.rows_ref.landed_ref = bf16[8,272,768]{2,1,0:T(8,128)(2,1)S(1)} async-done(((bf16[8,272,768]{2,1,0:T(8,128)(2,1)}), bf16[8,272,768]{2,1,0:T(8,128)(2,1)S(1)}, u32[]{:S(2)}, u32[]{:S(2)}) %all-to-all-start) | async-done | bytes 3342368 | tf_op jit(solution)/shard_map/all_to_all | solution.py:767
  98.2 4.8 %all-to-all-start.1 = ((bf16[8,128,768]{2,1,0:T(8,128)(2,1)}), bf16[8,128,768]{2,1,0:T(8,128)(2,1)}, u32[]{:S(2)}, u32[]{:S(2)}) async-start(bf16[8,128,768]{2,1,0:T(8,128)(2,1)} %bitcast.144), calls=%async_computation.1 | async-start | bytes 3145728 | tf_op jit(solution)/shard_map/all_to_all | solution.py:767
  103.0 3.9 fusion.16
  111.5 14.9 %act_grads.1 = bf16[4,2048,768]{2,1,0:T(8,128)(2,1)} custom-call(s32[1]{0:T(128)} %bitcast.1.place_ref, bf16[8,272,768]{2,1,0:T(8,128)(2,1)S(1)} %all-to-all-done.rows_ref.landed_ref, bf16[4,768,768]{2,1,0:T(8,128)(2,1)} %all-gather.3.cloned.1.call-done.weights_ref), custom_call_target="tpu_custom_call" | custom-call | flops 9663676416 | bytes 12582912 | tf_op jit(solution)/shard_map/act_grads/pallas_call | solution.py:500
  126.5 13.2 %all-to-all-done.1.rows_ref.first_ref = bf16[8,128,768]{2,1,0:T(8,128)(2,1)} async-done(((bf16[8,128,768]{2,1,0:T(8,128)(2,1)}), bf16[8,128,768]{2,1,0:T(8,128)(2,1)}, u32[]{:S(2)}, u32[]{:S(2)}) %all-to-all-start.1) | async-done | bytes 1572896 | tf_op jit(solution)/shard_map/all_to_all | solution.py:767
  139.6 3.6 all-to-all-start.3
  143.5 22.1 %expert_middle.2 = (bf16[8,128,768]{2,1,0:T(8,128)(2,1)S(1)}, bf16[4,8,2,128,768]{4,3,2,1,0:T(8,128)(2,1)}, bf16[4,8,2,128,768]{4,3,2,1,0:T(8,128)(2,1)}, bf16[8,2,128,128]{3,2,1,0:T(8,128)(2,1)S(1)}) custom-call(s32[1]{0:T(128)} %bitcast.1.place_ref, bf16[8,128,768]{2,1,0:T(8,128)(2,1)} %all-to-all-done.1.rows_ref.first_ref, ...), custom_call_target="tpu_custom_call" | custom-call | flops 9663676416 | bytes 18874368 | tf_op jit(solution)/shard_map/expert_middle/pallas_call | solution.py:456
  166.7 13.8 %all-to-all-done.3.rows_ref.last_ref = bf16[8,128,768]{2,1,0:T(8,128)(2,1)S(1)} async-done(((bf16[8,128,768]{2,1,0:T(8,128)(2,1)}), bf16[8,128,768]{2,1,0:T(8,128)(2,1)S(1)}, u32[]{:S(2)}, u32[]{:S(2)}) %all-to-all-start.3) | async-done | bytes 1572896 | tf_op jit(solution)/shard_map/all_to_all | solution.py:767
  180.5 4.5 %all-to-all-start.2 = ((bf16[8,128,768]{2,1,0:T(8,128)(2,1)}), bf16[8,128,768]{2,1,0:T(8,128)(2,1)}, u32[]{:S(2)}, u32[]{:S(2)}) async-start(bf16[8,128,768]{2,1,0:T(8,128)(2,1)} %copy-done.7), calls=%async_computation.2 | async-start | bytes 3145728 | tf_op jit(solution)/shard_map/all_to_all | solution.py:767
  184.9 21.8 %expert_middle.3 = (bf16[8,128,768]{2,1,0:T(8,128)(2,1)S(1)}, bf16[4,8,2,128,768]{4,3,2,1,0:T(8,128)(2,1)}, bf16[4,8,2,128,768]{4,3,2,1,0:T(8,128)(2,1)}, bf16[8,2,128,128]{3,2,1,0:T(8,128)(2,1)S(1)}) custom-call(s32[1]{0:T(128)} %bitcast.1.place_ref, ...), custom_call_target="tpu_custom_call", output_to_operand_aliasing={{1}: (6, {}), {2}: (7, {}), {3}: (8, {})} | custom-call | flops 9663676416 | bytes 18874368 | tf_op jit(solution)/shard_map/expert_middle/pallas_call | solution.py:456
  207.8 15.1 %out_weights.1 = (bf16[2,768,768]{2,1,0:T(8,128)(2,1)}, bf16[2,768,768]{2,1,0:T(8,128)(2,1)S(1)}) custom-call(bf16[4,2048,768]{2,1,0:T(8,128)(2,1)} %bitcast.123, bf16[8,272,768]{2,1,0:T(8,128)(2,1)} %copy-done), custom_call_target="tpu_custom_call" | custom-call | tf_op jit(solution)/shard_map/out_weights/pallas_call | solution.py:587
  224.3 6.0 %all-to-all-start.4 = ((bf16[8,128,768]{2,1,0:T(8,128)(2,1)}), bf16[8,128,768]{2,1,0:T(8,128)(2,1)}, u32[]{:S(2)}, u32[]{:S(2)}) async-start(bf16[8,128,768]{2,1,0:T(8,128)(2,1)} %copy-done.6), calls=%async_computation.4 | async-start | bytes 3145728 | tf_op jit(solution)/shard_map/all_to_all | solution.py:767
  236.4 15.9 %in_weights.1 = (bf16[2,768,768]{2,1,0:T(8,128)(2,1)}, bf16[2,768,768]{2,1,0:T(8,128)(2,1)}, f32[768,128]{1,0:T(8,128)S(1)}) custom-call(bf16[8,128,768]{2,1,0:T(8,128)(2,1)} %all-to-all-done.1.rows_ref.first_ref, bf16[8,128,768]{2,1,0:T(8,128)(2,1)S(1)} %all-to-all-done.3.rows_ref.last_ref, bf16[4,8,2,128,768]{4,3,2,1,0:T(8,128)(2,1)} %get-tuple-element.109.grads_ref, ...), custom_call_target="tpu_custom_call" | custom-call | tf_op jit(solution)/shard_map/in_weights/pallas_call | solution.py:627
  252.6 14.7 %expert_result.1 = bf16[2048,768]{1,0:T(8,128)(2,1)} custom-call(s32[1]{0:T(128)} %bitcast.1.place_ref, bf16[4,2048,768]{2,1,0:T(8,128)(2,1)} %bitcast.124, bf16[4,768,768]{2,1,0:T(8,128)(2,1)} %all-gather.3.cloned.1.call-done.weights_ref), custom_call_target="tpu_custom_call" | custom-call | tf_op jit(solution)/shard_map/expert_result/pallas_call | solution.py:533
  268.1 5.5 %all-to-all-start.5 = ((bf16[8,256,768]{2,1,0:T(8,128)(2,1)}), bf16[8,256,768]{2,1,0:T(8,128)(2,1)}, u32[]{:S(2)}, u32[]{:S(2)}) async-start(bf16[8,256,768]{2,1,0:T(8,128)(2,1)} %bitcast.23), calls=%async_computation.5 | async-start | bytes 6291456 | tf_op jit(solution)/shard_map/all_to_all | solution.py:767
  273.8 4.8 %combine.1 = (f32[512,768]{1,0:T(8,128)S(1)}, bf16[512,768]{1,0:T(8,128)(2,1)S(1)}, f32[8,768]{1,0:T(8,128)S(1)}) custom-call(bf16[512,1024]{1,0:T(8,128)(2,1)S(1)} %copy-done.1, bf16[1024,768]{1,0:T(8,128)(2,1)} %bitcast.20.first_rows_ref, bf16[512,1024]{1,0:T(8,128)(2,1)S(1)} %copy-done.2, bf16[1024,768]{1,0:T(8,128)(2,1)} %bitcast.21.last_rows_ref, ...), custom_call_target="tpu_custom_call" | custom-call | flops 1610612736 | bytes 7864320 | tf_op jit(solution)/shard_map/combine/pallas_call | solution.py:739
  280.7 19.0 %collective-permute-done.4 = bf16[1,512,768]{2,1,0:T(8,128)(2,1)S(1)} collective-permute-done((bf16[1,512,768]{2,1,0:T(8,128)(2,1)S(1)}, bf16[1,512,768]{2,1,0:T(8,128)(2,1)S(1)}, u32[]{:S(2)}, u32[]{:S(2)}) %collective-permute-start.4) | collective-permute-done | bytes 786464 | tf_op jit(solution)/shard_map/ppermute | solution.py:804
  305.1 35.9 %attend_backward.1 = (bf16[2048,768]{1,0:T(8,128)(2,1)}, bf16[832,768]{1,0:T(8,128)(2,1)S(1)}) custom-call(s32[1]{0:T(128)} %bitcast.1.place_ref, s32[1,8]{1,0:T(1,128)S(1)} %copy-done.17, bf16[2048,768]{1,0:T(8,128)(2,1)} %tokens_ref.1, f32[1,768]{1,0:T(1,128)S(1)} %broadcast_in_dim.11.gain_ref, bf16[576,768]{1,0:T(8,128)(2,1)S(1)} %bitcast.121, ...), custom_call_target="tpu_custom_call" | custom-call | flops 7851737088 | bytes 22020096 | tf_op jit(solution)/shard_map/attend_backward/pallas_call | solution.py:318
  341.1 3.2 all-to-all-done.5
  352.7 7.4 %collective-permute-done.13 = bf16[2,56,768]{2,1,0:T(8,128)(2,1)S(1)} collective-permute-done((bf16[2,56,768]{2,1,0:T(8,128)(2,1)S(1)}, bf16[2,56,768]{2,1,0:T(8,128)(2,1)S(1)}, u32[]{:S(2)}, u32[]{:S(2)}) %collective-permute-start.13) | collective-permute-done | bytes 172064 | tf_op jit(solution)/shard_map/ppermute | solution.py:819
  361.8 3.4 collective-permute-start.10
  368.3 3.2 collective-permute-done.11
  377.7 3.0 convert_add_fusion.1
  380.6 3.1 convert_add_fusion.2
  389.1 5.5 %convolution_add_fusion = f32[512,768]{1,0:T(8,128)} fusion(f32[512,768]{1,0:T(8,128)S(1)} %copy-done.23, bf16[512,2048]{1,0:T(8,128)(2,1)} %fusion.1, bf16[2048,768]{1,0:T(8,128)(2,1)} %bitcast.24), kind=kOutput, calls=%fused_computation.25 | convolution fusion | flops 1611005952 | bytes 8388608 | tf_op jit(solution)/shard_map/dot_general | solution.py:1027
  395.9 3.0 collective-permute-done.22
  (196 shorter events, 76.0 us)
Async XLA Ops:
  7.2 104.3 %all-gather.3.cloned.1.call-start = ((), (), s32[]{:S(2)}) async-start(), calls=%async_computation.7 | async-start | bytes 5898240 | tf_op jit(solution)/shard_map/all_gather | solution.py:945
  15.8 82.3 %all-to-all-start = ((bf16[8,272,768]{2,1,0:T(8,128)(2,1)}), bf16[8,272,768]{2,1,0:T(8,128)(2,1)S(1)}, u32[]{:S(2)}, u32[]{:S(2)}) async-start(bf16[8,272,768]{2,1,0:T(8,128)(2,1)} %copy-done.3), calls=%async_computation | async-start | bytes 6684672 | tf_op jit(solution)/shard_map/all_to_all | solution.py:767
  23.3 116.4 %all-gather.5.cloned.1.call-start = ((), (), s32[]{:S(2)}) async-start(), calls=%async_computation.8 | async-start | bytes 5898240 | tf_op jit(solution)/shard_map/all_gather | solution.py:946
  58.4 19.9 %collective-permute-start.1 = (bf16[1,512,768]{2,1,0:T(8,128)(2,1)}, bf16[1,512,768]{2,1,0:T(8,128)(2,1)}, u32[]{:S(2)}, u32[]{:S(2)}) collective-permute-start(bf16[1,512,768]{2,1,0:T(8,128)(2,1)} %slice.184), channel_id=1, source_target_pairs={{0,2},{1,3},{2,0},{3,1},{4,6},{5,7},{6,4},{7,5},{8,10},{9,11},{10,... | collective-permute-start | bytes 2359304 | tf_op jit(solution)/shard_map/ppermute | solution.py:804
  98.2 41.4 %all-to-all-start.1 = ((bf16[8,128,768]{2,1,0:T(8,128)(2,1)}), bf16[8,128,768]{2,1,0:T(8,128)(2,1)}, u32[]{:S(2)}, u32[]{:S(2)}) async-start(bf16[8,128,768]{2,1,0:T(8,128)(2,1)} %bitcast.144), calls=%async_computation.1 | async-start | bytes 3145728 | tf_op jit(solution)/shard_map/all_to_all | solution.py:767
  139.6 40.8 %all-to-all-start.3 = ((bf16[8,128,768]{2,1,0:T(8,128)(2,1)}), bf16[8,128,768]{2,1,0:T(8,128)(2,1)S(1)}, u32[]{:S(2)}, u32[]{:S(2)}) async-start(bf16[8,128,768]{2,1,0:T(8,128)(2,1)} %bitcast.143), calls=%async_computation.3 | async-start | bytes 3145728 | tf_op jit(solution)/shard_map/all_to_all | solution.py:767
  180.5 43.9 %all-to-all-start.2 = ((bf16[8,128,768]{2,1,0:T(8,128)(2,1)}), bf16[8,128,768]{2,1,0:T(8,128)(2,1)}, u32[]{:S(2)}, u32[]{:S(2)}) async-start(bf16[8,128,768]{2,1,0:T(8,128)(2,1)} %copy-done.7), calls=%async_computation.2 | async-start | bytes 3145728 | tf_op jit(solution)/shard_map/all_to_all | solution.py:767
  224.3 6.0 %collective-permute-start.2 = (bf16[2,768,768]{2,1,0:T(8,128)(2,1)}, bf16[2,768,768]{2,1,0:T(8,128)(2,1)}, u32[]{:S(2)}, u32[]{:S(2)}) collective-permute-start(bf16[2,768,768]{2,1,0:T(8,128)(2,1)} %get-tuple-element.107), channel_id=1, source_target_pairs={{0,1},{1,0},{2,3},{3,2},{4,5},{5,4},{6,7},{7,6},{8,9},{9,8},{10,11... | collective-permute-start | bytes 7077896 | tf_op jit(solution)/shard_map/ppermute | solution.py:804
  224.3 43.8 %all-to-all-start.4 = ((bf16[8,128,768]{2,1,0:T(8,128)(2,1)}), bf16[8,128,768]{2,1,0:T(8,128)(2,1)}, u32[]{:S(2)}, u32[]{:S(2)}) async-start(bf16[8,128,768]{2,1,0:T(8,128)(2,1)} %copy-done.6), calls=%async_computation.4 | async-start | bytes 3145728 | tf_op jit(solution)/shard_map/all_to_all | solution.py:767
  234.8 33.3 %collective-permute-start.3 = (bf16[1,768,768]{2,1,0:T(8,128)(2,1)}, bf16[1,768,768]{2,1,0:T(8,128)(2,1)}, u32[]{:S(2)}, u32[]{:S(2)}) collective-permute-start(bf16[1,768,768]{2,1,0:T(8,128)(2,1)} %get-tuple-element.152), channel_id=1, source_target_pairs={{0,2},{1,3},{2,0},{3,1},{4,6},{5,7},{6,4},{7,5},{8,10},{9,11},{10,... | collective-permute-start | bytes 3538952 | tf_op jit(solution)/shard_map/ppermute | solution.py:804
  268.1 76.1 %all-to-all-start.5 = ((bf16[8,256,768]{2,1,0:T(8,128)(2,1)}), bf16[8,256,768]{2,1,0:T(8,128)(2,1)}, u32[]{:S(2)}, u32[]{:S(2)}) async-start(bf16[8,256,768]{2,1,0:T(8,128)(2,1)} %bitcast.23), calls=%async_computation.5 | async-start | bytes 6291456 | tf_op jit(solution)/shard_map/all_to_all | solution.py:767
  273.6 110.3 %reduce-scatter.2.cloned.1.call-start = ((), (), s32[]{:S(2)}) async-start(), calls=%async_computation.9 | async-start | bytes 3932160 | tf_op jit(solution)/shard_map/reduce_scatter | solution.py:1017
  273.6 26.2 %collective-permute-start.5 = (bf16[2,768,768]{2,1,0:T(8,128)(2,1)}, bf16[2,768,768]{2,1,0:T(8,128)(2,1)S(1)}, u32[]{:S(2)}, u32[]{:S(2)}) collective-permute-start(bf16[2,768,768]{2,1,0:T(8,128)(2,1)} %get-tuple-element.121), channel_id=1, source_target_pairs={{0,1},{1,0},{2,3},{3,2},{4,5},{5,4},{6,7},{7,6},{8,9},{9,8},{10,11... | collective-permute-start | bytes 7077896 | tf_op jit(solution)/shard_map/ppermute | solution.py:804
  279.7 19.9 %collective-permute-start.4 = (bf16[1,512,768]{2,1,0:T(8,128)(2,1)S(1)}, bf16[1,512,768]{2,1,0:T(8,128)(2,1)S(1)}, u32[]{:S(2)}, u32[]{:S(2)}) collective-permute-start(bf16[1,512,768]{2,1,0:T(8,128)(2,1)S(1)} %bitcast.118), channel_id=1, source_target_pairs={{0,2},{1,3},{2,0},{3,1},{4,6},{5,7},{6,4},{7,5},{8,10},{9,11},{10,... | collective-permute-start | bytes 2359304 | tf_op jit(solution)/shard_map/ppermute | solution.py:804
  301.8 39.3 %collective-permute-start.7 = (bf16[1,768,768]{2,1,0:T(8,128)(2,1)S(1)}, bf16[1,768,768]{2,1,0:T(8,128)(2,1)}, u32[]{:S(2)}, u32[]{:S(2)}) collective-permute-start(bf16[1,768,768]{2,1,0:T(8,128)(2,1)S(1)} %get-tuple-element.151), channel_id=1, source_target_pairs={{0,2},{1,3},{2,0},{3,1},{4,6},{5,7},{6,4},{7,5},{8,10},{9,11},{10,... | collective-permute-start | bytes 3538952 | tf_op jit(solution)/shard_map/ppermute | solution.py:804
  344.4 8.3 %collective-permute-start.12 = (bf16[2,56,768]{2,1,0:T(8,128)(2,1)S(1)}, bf16[2,56,768]{2,1,0:T(8,128)(2,1)S(1)}, u32[]{:S(2)}, u32[]{:S(2)}) collective-permute-start(bf16[2,56,768]{2,1,0:T(8,128)(2,1)S(1)} %get-tuple-element.158), channel_id=1, source_target_pairs={{0,8},{4,12},{8,0},{12,4},{16,24},{20,28},{24,16},{28,20},{1,9},{5... | collective-permute-start | bytes 516104 | tf_op jit(solution)/shard_map/ppermute | solution.py:819
  344.5 15.6 %collective-permute-start.13 = (bf16[2,56,768]{2,1,0:T(8,128)(2,1)S(1)}, bf16[2,56,768]{2,1,0:T(8,128)(2,1)S(1)}, u32[]{:S(2)}, u32[]{:S(2)}) collective-permute-start(bf16[2,56,768]{2,1,0:T(8,128)(2,1)S(1)} %get-tuple-element.160), channel_id=1, source_target_pairs={{0,16},{4,20},{8,24},{12,28},{16,0},{20,4},{24,8},{28,12},{1,17},{... | collective-permute-start | bytes 516104 | tf_op jit(solution)/shard_map/ppermute | solution.py:819
  347.3 12.8 %collective-permute-start.14 = (bf16[2,56,768]{2,1,0:T(8,128)(2,1)S(1)}, bf16[2,56,768]{2,1,0:T(8,128)(2,1)S(1)}, u32[]{:S(2)}, u32[]{:S(2)}) collective-permute-start(bf16[2,56,768]{2,1,0:T(8,128)(2,1)S(1)} %get-tuple-element.159), channel_id=1, source_target_pairs={{0,24},{4,28},{8,16},{12,20},{16,8},{20,12},{24,0},{28,4},{1,25},{... | collective-permute-start | bytes 516104 | tf_op jit(solution)/shard_map/ppermute | solution.py:819
  348.9 12.7 %collective-permute-start.8 = (bf16[2,2,48,768]{3,2,1,0:T(8,128)(2,1)S(1)}, bf16[2,2,48,768]{3,2,1,0:T(8,128)(2,1)S(1)}, u32[]{:S(2)}, u32[]{:S(2)}) collective-permute-start(bf16[2,2,48,768]{3,2,1,0:T(8,128)(2,1)S(1)} %dynamic-slice_bitcast_fusion), channel_id=1, source_target_pairs={{0,4},{4,0},{8,12},{12,8},{16,20},{20,16},{24,28},{28,24},{1,5},{5... | collective-permute-start | bytes 884744 | tf_op jit(solution)/shard_map/ppermute | solution.py:819
  360.3 6.4 %collective-permute-start.15 = (bf16[56,768]{1,0:T(8,128)(2,1)S(1)}, bf16[56,768]{1,0:T(8,128)(2,1)S(1)}, u32[]{:S(2)}, u32[]{:S(2)}) collective-permute-start(bf16[56,768]{1,0:T(8,128)(2,1)S(1)} %fusion.12), channel_id=1, source_target_pairs={{0,4},{4,0},{8,12},{12,8},{16,20},{20,16},{24,28},{28,24},{1,5},{5... | collective-permute-start | bytes 258056 | tf_op jit(solution)/shard_map/ppermute | solution.py:819
  361.8 6.5 %collective-permute-start.10 = (bf16[48,768]{1,0:T(8,128)(2,1)S(1)}, bf16[48,768]{1,0:T(8,128)(2,1)S(1)}, u32[]{:S(2)}, u32[]{:S(2)}) collective-permute-start(bf16[48,768]{1,0:T(8,128)(2,1)S(1)} %get-tuple-element.165), channel_id=1, source_target_pairs={{0,16},{4,20},{8,24},{12,28},{16,0},{20,4},{24,8},{28,12},{1,17},{... | collective-permute-start | bytes 221192 | tf_op jit(solution)/shard_map/ppermute | solution.py:819
  365.2 6.3 %collective-permute-start.11 = (bf16[48,768]{1,0:T(8,128)(2,1)S(1)}, bf16[48,768]{1,0:T(8,128)(2,1)S(1)}, u32[]{:S(2)}, u32[]{:S(2)}) collective-permute-start(bf16[48,768]{1,0:T(8,128)(2,1)S(1)} %get-tuple-element.164), channel_id=1, source_target_pairs={{0,24},{4,28},{8,16},{12,20},{16,8},{20,12},{24,0},{28,4},{1,25},{... | collective-permute-start | bytes 221192 | tf_op jit(solution)/shard_map/ppermute | solution.py:819
  366.6 5.1 %collective-permute-start.9 = (bf16[48,768]{1,0:T(8,128)(2,1)S(1)}, bf16[48,768]{1,0:T(8,128)(2,1)S(1)}, u32[]{:S(2)}, u32[]{:S(2)}) collective-permute-start(bf16[48,768]{1,0:T(8,128)(2,1)S(1)} %get-tuple-element.163), channel_id=1, source_target_pairs={{0,8},{4,12},{8,0},{12,4},{16,24},{20,28},{24,16},{28,20},{1,9},{5... | collective-permute-start | bytes 221192 | tf_op jit(solution)/shard_map/ppermute | solution.py:819
  371.8 11.9 %collective-permute-start.16 = (bf16[48,768]{1,0:T(8,128)(2,1)S(1)}, bf16[48,768]{1,0:T(8,128)(2,1)S(1)}, u32[]{:S(2)}, u32[]{:S(2)}) collective-permute-start(bf16[48,768]{1,0:T(8,128)(2,1)S(1)} %fusion.11), channel_id=1, source_target_pairs={{0,24},{4,28},{8,16},{12,20},{16,8},{20,12},{24,0},{28,4},{1,25},{... | collective-permute-start | bytes 221192 | tf_op jit(solution)/shard_map/ppermute | solution.py:819
  373.8 10.0 %collective-permute-start.17 = (bf16[48,768]{1,0:T(8,128)(2,1)S(1)}, bf16[48,768]{1,0:T(8,128)(2,1)S(1)}, u32[]{:S(2)}, u32[]{:S(2)}) collective-permute-start(bf16[48,768]{1,0:T(8,128)(2,1)S(1)} %fusion.11), channel_id=1, source_target_pairs={{0,16},{4,20},{8,24},{12,28},{16,0},{20,4},{24,8},{28,12},{1,17},{... | collective-permute-start | bytes 221192 | tf_op jit(solution)/shard_map/ppermute | solution.py:819
  373.8 10.0 %collective-permute-start.18 = (bf16[48,768]{1,0:T(8,128)(2,1)S(1)}, bf16[48,768]{1,0:T(8,128)(2,1)S(1)}, u32[]{:S(2)}, u32[]{:S(2)}) collective-permute-start(bf16[48,768]{1,0:T(8,128)(2,1)S(1)} %fusion.11), channel_id=1, source_target_pairs={{0,8},{4,12},{8,0},{12,4},{16,24},{20,28},{24,16},{28,20},{1,9},{5... | collective-permute-start | bytes 221192 | tf_op jit(solution)/shard_map/ppermute | solution.py:819
  376.3 7.5 %collective-permute-start.19 = (bf16[56,768]{1,0:T(8,128)(2,1)S(1)}, bf16[56,768]{1,0:T(8,128)(2,1)S(1)}, u32[]{:S(2)}, u32[]{:S(2)}) collective-permute-start(bf16[56,768]{1,0:T(8,128)(2,1)S(1)} %fusion.8), channel_id=1, source_target_pairs={{0,4},{4,0},{8,12},{12,8},{16,20},{20,16},{24,28},{28,24},{1,5},{5... | collective-permute-start | bytes 258056 | tf_op jit(solution)/shard_map/ppermute | solution.py:819
  384.0 11.9 %collective-permute-start.21 = (bf16[2,56,768]{2,1,0:T(8,128)(2,1)S(1)}, bf16[2,56,768]{2,1,0:T(8,128)(2,1)S(1)}, u32[]{:S(2)}, u32[]{:S(2)}) collective-permute-start(bf16[2,56,768]{2,1,0:T(8,128)(2,1)S(1)} %pad_maximum_fusion.4), channel_id=1, source_target_pairs={{0,24},{4,28},{8,16},{12,20},{16,8},{20,12},{24,0},{28,4},{1,25},{... | collective-permute-start | bytes 516104 | tf_op jit(solution)/shard_map/ppermute | solution.py:819
  385.9 13.0 %collective-permute-start.22 = (bf16[2,56,768]{2,1,0:T(8,128)(2,1)S(1)}, bf16[2,56,768]{2,1,0:T(8,128)(2,1)S(1)}, u32[]{:S(2)}, u32[]{:S(2)}) collective-permute-start(bf16[2,56,768]{2,1,0:T(8,128)(2,1)S(1)} %pad_maximum_fusion.4), channel_id=1, source_target_pairs={{0,16},{4,20},{8,24},{12,28},{16,0},{20,4},{24,8},{28,12},{1,17},{... | collective-permute-start | bytes 516104 | tf_op jit(solution)/shard_map/ppermute | solution.py:819
  385.9 13.0 %collective-permute-start.23 = (bf16[2,56,768]{2,1,0:T(8,128)(2,1)S(1)}, bf16[2,56,768]{2,1,0:T(8,128)(2,1)S(1)}, u32[]{:S(2)}, u32[]{:S(2)}) collective-permute-start(bf16[2,56,768]{2,1,0:T(8,128)(2,1)S(1)} %pad_maximum_fusion.4), channel_id=1, source_target_pairs={{0,8},{4,12},{8,0},{12,4},{16,24},{20,28},{24,16},{28,20},{1,9},{5... | collective-permute-start | bytes 516104 | tf_op jit(solution)/shard_map/ppermute | solution.py:819
  388.4 10.7 %collective-permute-start.20 = (bf16[2,2,48,768]{3,2,1,0:T(8,128)(2,1)S(1)}, bf16[2,2,48,768]{3,2,1,0:T(8,128)(2,1)S(1)}, u32[]{:S(2)}, u32[]{:S(2)}) collective-permute-start(bf16[2,2,48,768]{3,2,1,0:T(8,128)(2,1)S(1)} %bitcast.146), channel_id=1, source_target_pairs={{0,4},{4,0},{8,12},{12,8},{16,20},{20,16},{24,28},{28,24},{1,5},{5... | collective-permute-start | bytes 884744 | tf_op jit(solution)/shard_map/ppermute | solution.py:819
  400.5 4.2 %collective-permute-start.25 = (f32[10,768]{1,0:T(8,128)S(1)}, f32[10,768]{1,0:T(8,128)S(1)}, u32[]{:S(2)}, u32[]{:S(2)}) collective-permute-start(f32[10,768]{1,0:T(8,128)S(1)} %fusion.28), channel_id=1, source_target_pairs={{0,2},{1,3},{2,0},{3,1},{4,6},{5,7},{6,4},{7,5},{8,10},{9,11},{10,... | collective-permute-start | bytes 92168 | tf_op jit(solution)/shard_map/ppermute | solution.py:819
  (38 other events, 279.5 us)
Sparse Core Ops, SparseCore 0:
  9.6 40.1 all-gather.2
  98.3 36.4 all-gather.4
  344.4 36.3 reduce-scatter.1
